TPU v7x, 32 devices: a whole 2x2x4 slice. The times are simulated.
32 devices in a mesh: row: 8 (over z, y), col: 4 (over x, core).
Axes of the slice: x: 2, y: 2, z: 4, core: 2. Of those that a mesh axis runs over, the one named last changes fastest.
Arguments:
- embeddings: bfloat16 [1024, 768], P(('row', 'col')), may hold values from -8 to 8
- start_block: float32 [64, 1024], P(None, ('row', 'col')), may hold values from -6 to 6
Outputs:
- spectral_block: float32 [64, 1024], P(None, ('row', 'col'))
All inputs are finite; a program needn't handle non-finite values.
Results may differ from a plain program's by a relative error of at most 0.0059.
Values may be sent and summed in bfloat16 or wider, within the bound.
No kernel may reach another device: no remote copies, remote signals or barrier semaphores. Data moves between devices by JAX's collectives and lax.ppermute only.
A program may use at most 64 MiB of HBM per device.

v0:
```python
import math

import jax
import jax.numpy as jnp
from jax import lax
from jax.sharding import PartitionSpec as P

ITERS = 4


TEMPER = 0.5


def kernel_block(left, left_sq, right):
    right_sq = jnp.sum(jnp.square(right.astype(jnp.float32)), axis=1)
    inner = lax.dot_general(
        left, right, (((1,), (1,)), ((), ())), preferred_element_type=jnp.float32
    )
    return jnp.exp(-(left_sq[:, None] + right_sq[None, :] - 2.0 * inner) / (TEMPER * left.shape[1]))


def body(embeddings, start_block):
    per_device = embeddings.shape[0]
    total = lax.axis_size("row") * lax.axis_size("col") * per_device
    row_block = lax.all_gather(embeddings, "col", axis=0, tiled=True)
    row_sq = jnp.sum(jnp.square(row_block.astype(jnp.float32)), axis=1)
    vectors = start_block
    column_block = lax.all_gather(embeddings, "row", axis=0, tiled=True)
    degree_terms = jnp.sum(kernel_block(row_block, row_sq, column_block), axis=1)
    degree = lax.psum_scatter(degree_terms, "col", scatter_dimension=0, tiled=True)
    scale = 1.0 / jnp.sqrt(degree)
    for sweep in range(ITERS):
        scaled = (vectors * scale[None, :]).astype(jnp.bfloat16)
        column_vectors = lax.all_gather(scaled, "row", axis=1, tiled=True)
        tile = kernel_block(row_block, row_sq, column_block).astype(jnp.bfloat16)
        partial_rows = lax.dot_general(
            column_vectors, tile, (((1,), (1,)), ((), ())), preferred_element_type=jnp.float32
        )
        mixed = (
            lax.psum_scatter(partial_rows, "col", scatter_dimension=1, tiled=True) * scale[None, :]
        )
        gram = lax.psum(jnp.dot(mixed, mixed.T, precision=lax.Precision.HIGHEST), ("row", "col"))
        factor = jnp.linalg.cholesky(gram)
        vectors = jax.scipy.linalg.solve_triangular(factor, mixed, lower=True)
    return vectors * math.sqrt(total)


def solution(mesh):
    return jax.shard_map(
        body,
        mesh=mesh,
        in_specs=(P(("row", "col"), None), P(None, ("row", "col"))),
        out_specs=P(None, ("row", "col")),
        check_vma=False,
    )
```

profile of v0, /device:TPU:0, one launch (start us, length us, event | category | flops | bytes accessed | tf_op | source)
XLA Modules:
  0.0 480.1 jit_solution(10223924414328430199)
XLA Ops:
  6.5 33.1 %all_gather.19 = bf16[256,768]{1,0:T(8,128)(2,1)S(1)} all-gather(bf16[32,768]{1,0:T(8,128)(2,1)} %param.5), channel_id=1, replica_groups=mesh['row'=8,'col'=4] {'row'}, dimensions={0}, use_global_device_ids=true | all-gather | bytes 442368 | tf_op jit(solution)/shard_map/all_gather | solution.py:28
  39.6 5.6 %all_gather.18 = bf16[128,768]{1,0:T(8,128)(2,1)S(1)} all-gather(bf16[32,768]{1,0:T(8,128)(2,1)S(1)} %copy-done), channel_id=1, replica_groups=mesh['row'=8,'col'=4] {'col'}, dimensions={0}, use_global_device_ids=true | all-gather | bytes 245760 | tf_op jit(solution)/shard_map/all_gather | solution.py:25
  45.2 0.2 multiply_reduce_fusion
  45.4 0.1 multiply_reduce_fusion.1
  45.5 0.4 fusion.45
  45.9 7.1 %all-reduce = f32[128]{0:T(128)S(1)} all-reduce(f32[128]{0:T(128)S(1)} %get-tuple-element.6), channel_id=2, replica_groups=mesh['row'=8,'col'=4] {'col'}, use_global_device_ids=true, to_apply=%region_3.0.clone | all-reduce | flops 128 | bytes 1024
  53.0 0.7 copy-done.6
  53.7 0.6 dynamic-slice
  54.9 0.1 dynamic-slice_rsqrt_fusion
  55.0 0.1 multiply_convert_fusion
  55.0 30.5 %all_gather.20 = bf16[64,256]{0,1:T(8,128)(2,1)S(1)} all-gather(bf16[64,32]{0,1:T(8,128)(2,1)S(1)} %multiply_convert_fusion), channel_id=1, replica_groups=mesh['row'=8,'col'=4] {'row'}, dimensions={1}, use_global_device_ids=true | all-gather | bytes 36864 | tf_op jit(solution)/shard_map/all_gather | solution.py:34
  85.5 0.8 fusion.46
  86.3 0.0 reduce-scatter.5.cloned.1.call-update
  86.3 0.0 reduce-scatter.7.cloned.1.call-start
  86.4 19.7 %reduce-scatter.5.cloned.1.call-done = f32[64,32]{0,1:T(8,128)} async-done(((f32[64,128]{0,1:T(8,128)}), f32[64,32]{0,1:T(8,128)}) %reduce-scatter.5.cloned.1.call-update) | async-done | bytes 8208 | tf_op jit(solution)/shard_map/reduce_scatter | solution.py:40
  106.1 1.1 fusion.35
  107.2 39.5 %psum.28 = f32[64,64]{0,1:T(8,128)S(1)} all-reduce(f32[64,64]{0,1:T(8,128)S(1)} %fusion.35), channel_id=1, replica_groups=mesh['row'=8,'col'=4] {'row','col'}, use_global_device_ids=true, to_apply=%region_5.0 | all-reduce | flops 4096 | bytes 32768 | tf_op jit(solution)/shard_map/psum | solution.py:42
  146.7 0.1 copy.12
  146.8 5.8 %cholesky.74 = f32[64,64]{1,0:T(8,128)S(1)} custom-call(f32[64,64]{1,0:T(8,128)S(1)} %fusion.18), custom_call_target="Cholesky" | custom-call | tf_op jit(solution)/shard_map/jit(cholesky)/cholesky | solution.py:43
  152.7 0.6 compare_reduce_fusion.3
  153.3 0.7 fusion.7
  154.0 4.9 %custom-call.8 = f32[1,64,64]{1,2,0:T(8,128)S(1)} custom-call(f32[1,64,64]{2,1,0:T(8,128)S(1)} %fusion.7), custom_call_target="InvertDiagBlocksLowerTriangular" | custom-call | tf_op jit(solution)/shard_map/jit(_solve_triangular)/triangular_solve | solution.py:44
  158.9 0.0 copy-done.3
  158.9 0.2 fusion.4
  159.1 30.5 %all_gather.21 = bf16[64,256]{0,1:T(8,128)(2,1)S(1)} all-gather(bf16[64,32]{0,1:T(8,128)(2,1)S(1)} %fusion.4), channel_id=1, replica_groups=mesh['row'=8,'col'=4] {'row'}, dimensions={1}, use_global_device_ids=true | all-gather | bytes 36864 | tf_op jit(solution)/shard_map/all_gather | solution.py:34
  189.6 0.8 fusion.47
  190.4 0.0 reduce-scatter.7.cloned.1.call-update
  190.4 0.0 reduce-scatter.9.cloned.1.call-start
  190.5 20.2 %reduce-scatter.7.cloned.1.call-done = f32[64,32]{0,1:T(8,128)} async-done(((f32[64,128]{0,1:T(8,128)}), f32[64,32]{0,1:T(8,128)}) %reduce-scatter.7.cloned.1.call-update) | async-done | bytes 8208 | tf_op jit(solution)/shard_map/reduce_scatter | solution.py:40
  210.6 1.1 fusion.32
  211.7 39.5 %psum.29 = f32[64,64]{0,1:T(8,128)S(1)} all-reduce(f32[64,64]{0,1:T(8,128)S(1)} %fusion.32), channel_id=1, replica_groups=mesh['row'=8,'col'=4] {'row','col'}, use_global_device_ids=true, to_apply=%region_9.0 | all-reduce | flops 4096 | bytes 32768 | tf_op jit(solution)/shard_map/psum | solution.py:42
  251.3 0.1 copy.14
  251.3 5.8 %cholesky.85 = f32[64,64]{1,0:T(8,128)S(1)} custom-call(f32[64,64]{1,0:T(8,128)S(1)} %fusion.16), custom_call_target="Cholesky" | custom-call | tf_op jit(solution)/shard_map/jit(cholesky)/cholesky | solution.py:43
  257.2 0.6 compare_reduce_fusion.2
  257.9 0.7 fusion.8
  258.5 4.9 %custom-call.9 = f32[1,64,64]{1,2,0:T(8,128)S(1)} custom-call(f32[1,64,64]{2,1,0:T(8,128)S(1)} %fusion.8), custom_call_target="InvertDiagBlocksLowerTriangular" | custom-call | tf_op jit(solution)/shard_map/jit(_solve_triangular)/triangular_solve | solution.py:44
  263.4 0.0 copy-done.4
  263.5 0.2 fusion.5
  263.7 30.5 %all_gather.22 = bf16[64,256]{0,1:T(8,128)(2,1)S(1)} all-gather(bf16[64,32]{0,1:T(8,128)(2,1)S(1)} %fusion.5), channel_id=1, replica_groups=mesh['row'=8,'col'=4] {'row'}, dimensions={1}, use_global_device_ids=true | all-gather | bytes 36864 | tf_op jit(solution)/shard_map/all_gather | solution.py:34
  294.2 0.8 fusion.48
  294.9 0.0 reduce-scatter.9.cloned.1.call-update
  295.0 0.0 reduce-scatter.11.cloned.1.call-start
  295.0 20.2 %reduce-scatter.9.cloned.1.call-done = f32[64,32]{0,1:T(8,128)} async-done(((f32[64,128]{0,1:T(8,128)}), f32[64,32]{0,1:T(8,128)}) %reduce-scatter.9.cloned.1.call-update) | async-done | bytes 8208 | tf_op jit(solution)/shard_map/reduce_scatter | solution.py:40
  315.2 1.1 fusion.29
  316.3 39.5 %psum.30 = f32[64,64]{0,1:T(8,128)S(1)} all-reduce(f32[64,64]{0,1:T(8,128)S(1)} %fusion.29), channel_id=1, replica_groups=mesh['row'=8,'col'=4] {'row','col'}, use_global_device_ids=true, to_apply=%region_11.0 | all-reduce | flops 4096 | bytes 32768 | tf_op jit(solution)/shard_map/psum | solution.py:42
  355.8 0.1 copy.16
  355.9 5.8 %cholesky.96 = f32[64,64]{1,0:T(8,128)S(1)} custom-call(f32[64,64]{1,0:T(8,128)S(1)} %fusion.14), custom_call_target="Cholesky" | custom-call | tf_op jit(solution)/shard_map/jit(cholesky)/cholesky | solution.py:43
  361.8 0.6 compare_reduce_fusion.1
  362.4 0.7 fusion.9
  363.1 4.9 %custom-call.10 = f32[1,64,64]{1,2,0:T(8,128)S(1)} custom-call(f32[1,64,64]{2,1,0:T(8,128)S(1)} %fusion.9), custom_call_target="InvertDiagBlocksLowerTriangular" | custom-call | tf_op jit(solution)/shard_map/jit(_solve_triangular)/triangular_solve | solution.py:44
  368.0 0.0 copy-done.5
  368.0 0.2 fusion.6
  368.2 30.5 %all_gather.23 = bf16[64,256]{0,1:T(8,128)(2,1)S(1)} all-gather(bf16[64,32]{0,1:T(8,128)(2,1)S(1)} %fusion.6), channel_id=1, replica_groups=mesh['row'=8,'col'=4] {'row'}, dimensions={1}, use_global_device_ids=true | all-gather | bytes 36864 | tf_op jit(solution)/shard_map/all_gather | solution.py:34
  398.8 0.8 fusion.49
  399.5 0.0 reduce-scatter.11.cloned.1.call-update
  399.5 20.2 %reduce-scatter.11.cloned.1.call-done = f32[64,32]{0,1:T(8,128)} async-done(((f32[64,128]{0,1:T(8,128)}), f32[64,32]{0,1:T(8,128)}) %reduce-scatter.11.cloned.1.call-update) | async-done | bytes 8208 | tf_op jit(solution)/shard_map/reduce_scatter | solution.py:40
  419.8 1.1 fusion.26
  420.9 39.7 %psum.31 = f32[64,64]{0,1:T(8,128)S(1)} all-reduce(f32[64,64]{0,1:T(8,128)S(1)} %fusion.26), channel_id=1, replica_groups=mesh['row'=8,'col'=4] {'row','col'}, use_global_device_ids=true, to_apply=%region_13.0 | all-reduce | flops 4096 | bytes 32768 | tf_op jit(solution)/shard_map/psum | solution.py:42
  460.6 0.1 copy.18
  460.7 5.8 %cholesky.107 = f32[64,64]{1,0:T(8,128)S(1)} custom-call(f32[64,64]{1,0:T(8,128)S(1)} %fusion.12), custom_call_target="Cholesky" | custom-call | tf_op jit(solution)/shard_map/jit(cholesky)/cholesky | solution.py:43
  466.5 0.6 compare_reduce_fusion
  467.2 0.7 fusion.10
  467.9 4.9 %custom-call.11 = f32[1,64,64]{1,2,0:T(8,128)S(1)} custom-call(f32[1,64,64]{2,1,0:T(8,128)S(1)} %fusion.10), custom_call_target="InvertDiagBlocksLowerTriangular" | custom-call | tf_op jit(solution)/shard_map/jit(_solve_triangular)/triangular_solve | solution.py:44
  472.8 0.8 convolution_multiply_fusion.1
  (19 shorter events, 0.2 us)
Async XLA Ops:
  6.5 33.1 %copy-start = (bf16[32,768]{1,0:T(8,128)(2,1)S(1)}, bf16[32,768]{1,0:T(8,128)(2,1)}, u32[]{:S(2)}) copy-start(bf16[32,768]{1,0:T(8,128)(2,1)} %param.5) | copy-start | bytes 147460
  6.5 99.5 %reduce-scatter.5.cloned.1.call-start = ((), (), s32[]{:S(2)}) async-start(), calls=%async_computation.4 | async-start | bytes 81920 | tf_op jit(solution)/shard_map/reduce_scatter | solution.py:40
  45.9 9.1 %copy-start.1 = (f32[64,32]{0,1:T(8,128)S(1)}, f32[64,32]{0,1:T(8,128)}, u32[]{:S(2)}) copy-start(f32[64,32]{0,1:T(8,128)} %param.6) | copy-start | bytes 24580
  53.0 0.7 copy-start.6
  86.3 124.3 %reduce-scatter.7.cloned.1.call-start = ((), (), s32[]{:S(2)}) async-start(), calls=%async_computation.5 | async-start | bytes 81920 | tf_op jit(solution)/shard_map/reduce_scatter | solution.py:40
  153.3 5.6 %copy-start.3 = (f32[64,32]{0,1:T(8,128)S(1)}, f32[64,32]{0,1:T(8,128)}, u32[]{:S(2)}) copy-start(f32[64,32]{0,1:T(8,128)} %reduce-scatter.5.cloned.1.call-done) | copy-start | bytes 24580
  190.4 124.8 %reduce-scatter.9.cloned.1.call-start = ((), (), s32[]{:S(2)}) async-start(), calls=%async_computation.6 | async-start | bytes 81920 | tf_op jit(solution)/shard_map/reduce_scatter | solution.py:40
  257.9 5.6 %copy-start.4 = (f32[64,32]{0,1:T(8,128)S(1)}, f32[64,32]{0,1:T(8,128)}, u32[]{:S(2)}) copy-start(f32[64,32]{0,1:T(8,128)} %reduce-scatter.7.cloned.1.call-done) | copy-start | bytes 24580
  295.0 124.8 %reduce-scatter.11.cloned.1.call-start = ((), (), s32[]{:S(2)}) async-start(), calls=%async_computation.7 | async-start | bytes 81920 | tf_op jit(solution)/shard_map/reduce_scatter | solution.py:40
  362.4 5.6 %copy-start.5 = (f32[64,32]{0,1:T(8,128)S(1)}, f32[64,32]{0,1:T(8,128)}, u32[]{:S(2)}) copy-start(f32[64,32]{0,1:T(8,128)} %reduce-scatter.9.cloned.1.call-done) | copy-start | bytes 24580
  467.2 5.6 %copy-start.2 = (f32[64,32]{0,1:T(8,128)S(1)}, f32[64,32]{0,1:T(8,128)}, u32[]{:S(2)}) copy-start(f32[64,32]{0,1:T(8,128)} %reduce-scatter.11.cloned.1.call-done) | copy-start | bytes 24580
Sparse Core Ops, SparseCore 0:
  86.5 19.5 reduce-scatter.4
  190.5 20.0 reduce-scatter.6
  295.1 20.0 reduce-scatter.8
  399.7 20.0 reduce-scatter.10
where the time goes:
time: 482 us; the launch traced here: 480 us
  blocking collectives  326 us (68%)
  waiting for transfers between devices  80.3 us (17%)
  other arithmetic  48.7 us (10%)
  between operations  14 us (3%)
  matrix products  9.3 us (2%)
    psum x4, blocking collectives, body(): lax.psum(jnp.dot(mixed, mixed.T, precision=lax.Precision.HIGHEST), ('row'...  158 us
    all_gather x4, blocking collectives, body(): column_vectors = lax.all_gather(scaled, 'row', axis=1, tiled=True)  122 us
    reduce_scatter x4, waiting for transfers between devices, body(): lax.psum_scatter(partial_rows, 'col', scatter_dimension=1, tiled=True)  80.2 us
    all_gather x1, blocking collectives, body(): column_block = lax.all_gather(embeddings, 'row', axis=0, tiled=True)  33.1 us
    another operation x12, other arithmetic, body(): factor = jnp.linalg.cholesky(gram)  26.1 us
    another operation x8, other arithmetic, body(): vectors = jax.scipy.linalg.solve_triangular(factor, mixed, lower=True)  22.2 us
  transfers between devices with their start and end apart: 4, of which 4 were waited for; matrix products, arithmetic and copies ran while one was open for 0% of the time, Pallas kernels for 0%

commit v1 on v0

v1 whole, which is shorter than its diff:
```python
import functools
import math

import jax
import jax.numpy as jnp
from jax import lax
from jax.experimental import pallas as pl
from jax.experimental.pallas import tpu as pltpu
from jax.sharding import PartitionSpec as P

ITERS = 4
TEMPER = 0.5
HIGHEST = lax.Precision.HIGHEST
NT = (((1,), (1,)), ((), ()))
NN = (((1,), (0,)), ((), ()))


def lane_splat(x, c):
    return jnp.broadcast_to(x[:, c : c + 1], x.shape)


def row_splat(x, r):
    return jnp.broadcast_to(x[r : r + 1, :], x.shape)


def reciprocal(p):
    q = pltpu.reciprocal(p, approx=True)
    q = q * (2.0 - p * q)
    return q * (2.0 - p * q)


def inverse_factor(tiles):
    count = len(tiles)
    sub = lax.broadcasted_iota(jnp.int32, tiles[0].shape, 0)
    pivots = [None] * count
    for b in range(count):
        columns = [[lane_splat(tiles[t], 8 * b + j) for t in range(b, count)] for j in range(8)]
        factors, rows = [], []
        for j in range(8):
            pivot = row_splat(columns[j][0], j)
            q = reciprocal(pivot)
            m = [d * q for d in columns[j]]
            m[0] = jnp.where(sub > j, m[0], 0.0)
            row = row_splat(tiles[b], j)
            tiles[b] = tiles[b] - m[0] * row
            pivots[b] = pivot if j == 0 else jnp.where(sub >= j, pivot, pivots[b])
            for l in range(j + 1, 8):
                head = row_splat(columns[l][0], j)
                columns[l] = [d - f * head for d, f in zip(columns[l], m)]
            factors.append(m)
            rows.append(row)
        for t in range(b + 1, count):
            total = factors[0][t - b] * rows[0]
            for j in range(1, 8):
                total = total + factors[j][t - b] * rows[j]
            tiles[t] = tiles[t] - total
    return [tile * lax.rsqrt(p) for tile, p in zip(tiles, pivots)]


def embed_kernel(pieces, own, vecs, feat, *refs):
    piece_refs, out_ref = refs[:pieces], refs[pieces]
    e_ref, k_ref, v_ref, m_ref = refs[pieces + 1 :]
    per = piece_refs[0].shape[0]
    points = pieces * per
    for i, piece in enumerate(piece_refs):
        e_ref[i * per : (i + 1) * per, :] = piece[:, :feat]
        x0 = piece[:, feat : feat + vecs].astype(jnp.float32) + piece[:, feat + vecs : feat + 2 * vecs].astype(jnp.float32)
        v_ref[:, i * per : (i + 1) * per] = x0.T
    eye = lax.broadcasted_iota(jnp.int32, (per, per), 0) == lax.broadcasted_iota(jnp.int32, (per, per), 1)
    cols, rows = [], []
    for i in range(pieces):
        e = e_ref[i * per : (i + 1) * per, :]
        d = jnp.where(eye, lax.dot_general(e, e, NT, preferred_element_type=jnp.float32), 0.0)
        cols.append(jnp.sum(d, axis=1, keepdims=True))
        rows.append(jnp.sum(d, axis=0, keepdims=True))
    row_sq = jnp.concatenate(rows, axis=1)
    rate = 1.0 / (TEMPER * feat)
    degree = jnp.zeros((1, points), jnp.float32)
    step = 2 * per
    for i in range(points // step):
        g = lax.dot_general(e_ref[i * step : (i + 1) * step, :], e_ref[...], NT, preferred_element_type=jnp.float32)
        col_sq = jnp.concatenate(cols[2 * i : 2 * i + 2], axis=0)
        k = jnp.exp((2.0 * g - col_sq - row_sq) * rate)
        degree = degree + jnp.sum(k, axis=0, keepdims=True)
        k_ref[i * step : (i + 1) * step, :] = k.astype(jnp.bfloat16)
    scale = 1.0 / jnp.sqrt(degree)
    lane = lax.broadcasted_iota(jnp.int32, (vecs, 2 * vecs), 1)
    unit = (lane == lax.broadcasted_iota(jnp.int32, (vecs, 2 * vecs), 0) + vecs).astype(jnp.float32)
    for sweep in range(ITERS):
        scaled = (v_ref[...] * scale).astype(jnp.bfloat16)
        mixed = lax.dot_general(scaled, k_ref[...], NN, preferred_element_type=jnp.float32) * scale
        m_ref[:vecs, :] = mixed
        m_ref[vecs:, :] = mixed
        gram = lax.dot_general(mixed, m_ref[...], NT, preferred_element_type=jnp.float32, precision=HIGHEST)
        full = jnp.where(lane < vecs, gram, unit)
        inv = jnp.concatenate(inverse_factor([full[8 * t : 8 * t + 8, :] for t in range(vecs // 8)]), axis=0)
        inv = jnp.where(lane < vecs, 0.0, inv)
        if sweep < ITERS - 1:
            v_ref[...] = lax.dot_general(inv, m_ref[...], NN, preferred_element_type=jnp.float32, precision=HIGHEST)
        else:
            last = lax.dot_general(inv, m_ref[:, :per], NN, preferred_element_type=jnp.float32, precision=HIGHEST)
            out_ref[...] = last.T[:own, :] * math.sqrt(points)


def exchange(x, rows, cols, partner):
    pairs = []
    for r in range(rows):
        for c in range(cols):
            r2, c2 = partner(r, c)
            pairs.append((r * cols + c, r2 * cols + c2))
    return lax.ppermute(x, ("row", "col"), pairs)


def replicated(embeddings, start_block, rows, cols):
    own, feat = embeddings.shape
    vecs = start_block.shape[0]
    send = functools.partial(exchange, rows=rows, cols=cols)
    start = start_block.T
    high = start.astype(jnp.bfloat16)
    low = (start - high.astype(jnp.float32)).astype(jnp.bfloat16)
    mine = jnp.concatenate([embeddings, high, low], axis=1)
    along_z = [send(mine, partner=lambda r, c, d=d: (r ^ (2 * d), c)) for d in (1, 2, 3)]
    a = jnp.concatenate([mine] + along_z, axis=0)
    b = send(a, partner=lambda r, c: (r, c ^ 2) if c & 1 else (r ^ 1, c))
    c_ = send(a, partner=lambda r, c: (r ^ 1, c) if c & 1 else (r, c ^ 2))
    d_ = send(b, partner=lambda r, c: (r ^ 1, c) if c & 1 else (r, c ^ 2))
    pieces = []
    for piece in (a, b, c_, d_):
        pieces += [piece, send(piece, partner=lambda r, c: (r, c ^ 1))]
    count, per = len(pieces), a.shape[0]
    points = count * per
    return pl.pallas_call(
        functools.partial(embed_kernel, count, own, vecs, feat),
        out_shape=jax.ShapeDtypeStruct((own, vecs), jnp.float32),
        in_specs=[pl.BlockSpec(memory_space=pltpu.VMEM)] * count,
        out_specs=pl.BlockSpec(memory_space=pltpu.VMEM),
        scratch_shapes=[
            pltpu.VMEM((points, feat), jnp.bfloat16),
            pltpu.VMEM((points, points), jnp.bfloat16),
            pltpu.VMEM((vecs, points), jnp.float32),
            pltpu.VMEM((2 * vecs, points), jnp.float32),
        ],
        compiler_params=pltpu.CompilerParams(vmem_limit_bytes=40 * 1024 * 1024),
    )(*pieces).T


def kernel_block(left, left_sq, right):
    right_sq = jnp.sum(jnp.square(right.astype(jnp.float32)), axis=1)
    inner = lax.dot_general(left, right, NT, preferred_element_type=jnp.float32)
    return jnp.exp(-(left_sq[:, None] + right_sq[None, :] - 2.0 * inner) / (TEMPER * left.shape[1]))


def distributed(embeddings, start_block):
    per_device = embeddings.shape[0]
    total = lax.axis_size("row") * lax.axis_size("col") * per_device
    row_block = lax.all_gather(embeddings, "col", axis=0, tiled=True)
    row_sq = jnp.sum(jnp.square(row_block.astype(jnp.float32)), axis=1)
    vectors = start_block
    column_block = lax.all_gather(embeddings, "row", axis=0, tiled=True)
    degree_terms = jnp.sum(kernel_block(row_block, row_sq, column_block), axis=1)
    degree = lax.psum_scatter(degree_terms, "col", scatter_dimension=0, tiled=True)
    scale = 1.0 / jnp.sqrt(degree)
    for sweep in range(ITERS):
        scaled = (vectors * scale[None, :]).astype(jnp.bfloat16)
        column_vectors = lax.all_gather(scaled, "row", axis=1, tiled=True)
        tile = kernel_block(row_block, row_sq, column_block).astype(jnp.bfloat16)
        partial_rows = lax.dot_general(column_vectors, tile, NT, preferred_element_type=jnp.float32)
        mixed = lax.psum_scatter(partial_rows, "col", scatter_dimension=1, tiled=True) * scale[None, :]
        gram = lax.psum(jnp.dot(mixed, mixed.T, precision=HIGHEST), ("row", "col"))
        factor = jnp.linalg.cholesky(gram)
        vectors = jax.scipy.linalg.solve_triangular(factor, mixed, lower=True)
    return vectors * math.sqrt(total)


def solution(mesh):
    rows, cols = mesh.shape["row"], mesh.shape["col"]

    def body(embeddings, start_block):
        if (rows, cols) == (8, 4) and embeddings.shape[0] * 4 == 128 and start_block.shape[0] == 64:
            return replicated(embeddings, start_block, rows, cols)
        return distributed(embeddings, start_block)

    return jax.shard_map(
        body,
        mesh=mesh,
        in_specs=(P(("row", "col"), None), P(None, ("row", "col"))),
        out_specs=P(None, ("row", "col")),
        check_vma=False,
    )
```

time: 482 us -> 47 us (0.10)
  blocking collectives: 326 us -> 0 us
  waiting for transfers between devices: 80.3 us -> 16.8 us
  other arithmetic: 48.7 us -> 1.75 us
  Pallas kernels: 0 us -> 19 us
  between operations: 14 us -> 0.02 us
  matrix products: 9.3 us -> 0 us
  starting transfers between devices: 0.13 us -> 9.26 us
    all_gather x6 -> x0, blocking collectives: 161 us -> none  [the longest x4 122 us: body(): column_vectors = lax.all_gather(scaled, 'row', axis=1, tiled=True)]
    psum x4 -> x0, blocking collectives: 158 us -> none  [body(): lax.psum(jnp.dot(mixed, mixed.T, precision=lax.Precision.HIGHEST), ('row'...]
    reduce_scatter x4 -> x0, waiting for transfers between devices: 80.2 us -> none  [body(): lax.psum_scatter(partial_rows, 'col', scatter_dimension=1, tiled=True)]
    another operation x20 -> x0, other arithmetic: 48.3 us -> none  [the longest x12 26.1 us: body(): factor = jnp.linalg.cholesky(gram)]
    pallas_call x0 -> x1, Pallas kernels: none -> 19 us  [replicated(): pl.pallas_call(functools.partial(embed_kernel, count, own, vecs, feat), o...]
    ppermute x0 -> x10, waiting for transfers between devices: none -> 16.8 us  [exchange(): return lax.ppermute(x, ('row', 'col'), pairs)]
    ppermute x0 -> x10, starting transfers between devices: none -> 9.26 us  [exchange(): return lax.ppermute(x, ('row', 'col'), pairs)]
    dot_general x9 -> x0, matrix products: 7.86 us -> none  [the longest x4 4.38 us: body(): jnp.dot(mixed, mixed.T, precision=lax.Precision.HIGHEST)]
  transfers between devices with their start and end apart: 4 -> 10, of which waited for: 4 -> 5; matrix products, arithmetic and copies ran while one was open for 0% -> 0% of each run, Pallas kernels for 0% -> 0%
where the time goes in v1:
time: 47 us; the launch traced here: 46.8 us
  Pallas kernels  19 us (40%)
  waiting for transfers between devices  16.8 us (36%)
  starting transfers between devices  9.26 us (20%)
  other arithmetic  1.75 us (4%)
    pallas_call x1, Pallas kernels, replicated(): pl.pallas_call(functools.partial(embed_kernel, count, own, vecs, feat), o...  19 us
    ppermute x10, waiting for transfers between devices, exchange(): return lax.ppermute(x, ('row', 'col'), pairs)  16.8 us
    ppermute x10, starting transfers between devices, exchange(): return lax.ppermute(x, ('row', 'col'), pairs)  9.26 us
    concatenate x1, other arithmetic, replicated(): mine = jnp.concatenate([embeddings, high, low], axis=1)  0.95 us
  transfers between devices with their start and end apart: 10, of which 5 were waited for; matrix products, arithmetic and copies ran while one was open for 0% of the time, Pallas kernels for 0%

profile of v1, /device:TPU:0, one launch (start us, length us, event | category | flops | bytes accessed | tf_op | source)
XLA Modules:
  0.0 46.8 jit_solution(3696954462690572784)
XLA Ops:
  0.0 0.7 %fusion = (bf16[32,64]{1,0:T(8,128)(2,1)S(1)}, bf16[32,64]{1,0:T(8,128)(2,1)S(1)}) fusion(f32[64,32]{0,1:T(8,128)} %param.3), kind=kLoop, calls=%fused_computation.4 | loop fusion | flops 8192 | bytes 16384 | tf_op jit(solution)/shard_map/convert_element_type | solution.py:120
  0.7 0.0 copy-start
  0.7 0.9 %pad_maximum_fusion.1 = bf16[32,896]{1,0:T(8,128)(2,1)S(1)} fusion(bf16[32,64]{1,0:T(8,128)(2,1)S(1)} %get-tuple-element.5, bf16[32,64]{1,0:T(8,128)(2,1)S(1)} %get-tuple-element.6, bf16[32,768]{1,0:T(8,128)(2,1)} %param.2), kind=kLoop, calls=%fused_computation.1 | loop fusion | flops 172032 | bytes 114688 | tf_op jit(solution)/shard_map/concatenate | solution.py:121
  1.7 5.0 %collective-permute-start.2 = (bf16[32,896]{1,0:T(8,128)(2,1)S(1)}, bf16[32,896]{1,0:T(8,128)(2,1)S(1)}, u32[]{:S(2)}, u32[]{:S(2)}) collective-permute-start(bf16[32,896]{1,0:T(8,128)(2,1)S(1)} %pad_maximum_fusion.1), channel_id=1, source_target_pairs={{0,24},{1,25},{2,26},{3,27},{4,28},{5,29},{6,30},{7,31},{8,16},{9,... | collective-permute-start | bytes 172040 | tf_op jit(solution)/shard_map/ppermute | solution.py:111
  6.7 0.0 collective-permute-start.1
  6.7 0.6 %collective-permute-start = (bf16[32,896]{1,0:T(8,128)(2,1)S(1)}, bf16[32,896]{1,0:T(8,128)(2,1)S(1)}, u32[]{:S(2)}, u32[]{:S(2)}) collective-permute-start(bf16[32,896]{1,0:T(8,128)(2,1)S(1)} %pad_maximum_fusion.1), channel_id=1, source_target_pairs={{0,8},{1,9},{2,10},{3,11},{4,12},{5,13},{6,14},{7,15},{8,0},{9,1},... | collective-permute-start | bytes 172040 | tf_op jit(solution)/shard_map/ppermute | solution.py:111
  7.4 1.8 %collective-permute-done.2 = bf16[32,896]{1,0:T(8,128)(2,1)S(1)} collective-permute-done((bf16[32,896]{1,0:T(8,128)(2,1)S(1)}, bf16[32,896]{1,0:T(8,128)(2,1)S(1)}, u32[]{:S(2)}, u32[]{:S(2)}) %collective-permute-start.2) | collective-permute-done | bytes 57376 | tf_op jit(solution)/shard_map/ppermute | solution.py:111
  9.1 2.7 %collective-permute-done.1 = bf16[32,896]{1,0:T(8,128)(2,1)S(1)} collective-permute-done((bf16[32,896]{1,0:T(8,128)(2,1)S(1)}, bf16[32,896]{1,0:T(8,128)(2,1)S(1)}, u32[]{:S(2)}, u32[]{:S(2)}) %collective-permute-start.1) | collective-permute-done | bytes 57376 | tf_op jit(solution)/shard_map/ppermute | solution.py:111
  11.8 0.0 collective-permute-done
  11.8 0.0 copy-done
  11.8 0.1 pad_maximum_fusion.refs_0_
  11.9 1.6 %collective-permute-start.4 = (bf16[128,896]{1,0:T(8,128)(2,1)S(1)}, bf16[128,896]{1,0:T(8,128)(2,1)S(1)}, u32[]{:S(2)}, u32[]{:S(2)}) collective-permute-start(bf16[128,896]{1,0:T(8,128)(2,1)S(1)} %pad_maximum_fusion.refs_0_), channel_id=1, source_target_pairs={{0,4},{1,3},{2,6},{3,1},{4,0},{5,7},{6,2},{7,5},{8,12},{9,11},{10,... | collective-permute-start | bytes 688136 | tf_op jit(solution)/shard_map/ppermute | solution.py:111
  13.4 1.5 %collective-permute-start.6 = (bf16[128,896]{1,0:T(8,128)(2,1)S(1)}, bf16[128,896]{1,0:T(8,128)(2,1)S(1)}, u32[]{:S(2)}, u32[]{:S(2)}) collective-permute-start(bf16[128,896]{1,0:T(8,128)(2,1)S(1)} %pad_maximum_fusion.refs_0_), channel_id=1, source_target_pairs={{0,2},{1,5},{2,0},{3,7},{4,6},{5,1},{6,4},{7,3},{8,10},{9,13},{10,... | collective-permute-start | bytes 688136 | tf_op jit(solution)/shard_map/ppermute | solution.py:111
  14.9 5.4 %collective-permute-done.4.refs_2_ = bf16[128,896]{1,0:T(8,128)(2,1)S(1)} collective-permute-done((bf16[128,896]{1,0:T(8,128)(2,1)S(1)}, bf16[128,896]{1,0:T(8,128)(2,1)S(1)}, u32[]{:S(2)}, u32[]{:S(2)}) %collective-permute-start.4) | collective-permute-done | bytes 229408 | tf_op jit(solution)/shard_map/ppermute | solution.py:111
  20.3 0.0 collective-permute-start.8
  20.3 0.0 collective-permute-start.3
  20.3 0.5 %collective-permute-start.5 = (bf16[128,896]{1,0:T(8,128)(2,1)S(1)}, bf16[128,896]{1,0:T(8,128)(2,1)S(1)}, u32[]{:S(2)}, u32[]{:S(2)}) collective-permute-start(bf16[128,896]{1,0:T(8,128)(2,1)S(1)} %collective-permute-done.4.refs_2_), channel_id=1, source_target_pairs={{0,1},{1,0},{2,3},{3,2},{4,5},{5,4},{6,7},{7,6},{8,9},{9,8},{10,11... | collective-permute-start | bytes 688136 | tf_op jit(solution)/shard_map/ppermute | solution.py:111
  20.8 0.0 collective-permute-done.6.refs_4_
  20.8 0.0 collective-permute-start.7
  20.8 5.5 %collective-permute-done.8.refs_6_ = bf16[128,896]{1,0:T(8,128)(2,1)S(1)} collective-permute-done((bf16[128,896]{1,0:T(8,128)(2,1)S(1)}, bf16[128,896]{1,0:T(8,128)(2,1)S(1)}, u32[]{:S(2)}, u32[]{:S(2)}) %collective-permute-start.8) | collective-permute-done | bytes 229408 | tf_op jit(solution)/shard_map/ppermute | solution.py:111
  26.3 0.0 collective-permute-start.9
  26.3 0.0 collective-permute-done.3.refs_1_
  26.3 0.0 collective-permute-done.7.refs_5_
  26.3 0.0 collective-permute-done.5.refs_3_
  26.4 1.5 %collective-permute-done.9.refs_7_ = bf16[128,896]{1,0:T(8,128)(2,1)S(1)} collective-permute-done((bf16[128,896]{1,0:T(8,128)(2,1)S(1)}, bf16[128,896]{1,0:T(8,128)(2,1)S(1)}, u32[]{:S(2)}, u32[]{:S(2)}) %collective-permute-start.9) | collective-permute-done | bytes 229408 | tf_op jit(solution)/shard_map/ppermute | solution.py:111
  27.8 19.0 %shard_map.28 = f32[32,64]{1,0:T(8,128)} custom-call(bf16[128,896]{1,0:T(8,128)(2,1)S(1)} %pad_maximum_fusion.refs_0_, bf16[128,896]{1,0:T(8,128)(2,1)S(1)} %collective-permute-done.3.refs_1_, bf16[128,896]{1,0:T(8,128)(2,1)S(1)} %collective-permute-done.4.refs_2_, bf16[128,896]{1,0:T(8,128)(2,1)S(1)} %collective-permute-done.5.refs_3_, ...), custom_call_target="tpu_custom_call" | custom-call | tf_op jit(solution)/shard_map/pallas_call | solution.py:132
Async XLA Ops:
  0.7 11.1 %copy-start = (bf16[32,768]{1,0:T(8,128)(2,1)S(1)}, bf16[32,768]{1,0:T(8,128)(2,1)}, u32[]{:S(2)}) copy-start(bf16[32,768]{1,0:T(8,128)(2,1)} %param.2) | copy-start | bytes 147460
  1.7 7.5 %collective-permute-start.2 = (bf16[32,896]{1,0:T(8,128)(2,1)S(1)}, bf16[32,896]{1,0:T(8,128)(2,1)S(1)}, u32[]{:S(2)}, u32[]{:S(2)}) collective-permute-start(bf16[32,896]{1,0:T(8,128)(2,1)S(1)} %pad_maximum_fusion.1), channel_id=1, source_target_pairs={{0,24},{1,25},{2,26},{3,27},{4,28},{5,29},{6,30},{7,31},{8,16},{9,... | collective-permute-start | bytes 172040 | tf_op jit(solution)/shard_map/ppermute | solution.py:111
  6.7 5.1 %collective-permute-start.1 = (bf16[32,896]{1,0:T(8,128)(2,1)S(1)}, bf16[32,896]{1,0:T(8,128)(2,1)S(1)}, u32[]{:S(2)}, u32[]{:S(2)}) collective-permute-start(bf16[32,896]{1,0:T(8,128)(2,1)S(1)} %pad_maximum_fusion.1), channel_id=1, source_target_pairs={{0,16},{1,17},{2,18},{3,19},{4,20},{5,21},{6,22},{7,23},{8,24},{9,... | collective-permute-start | bytes 172040 | tf_op jit(solution)/shard_map/ppermute | solution.py:111
  6.7 5.1 %collective-permute-start = (bf16[32,896]{1,0:T(8,128)(2,1)S(1)}, bf16[32,896]{1,0:T(8,128)(2,1)S(1)}, u32[]{:S(2)}, u32[]{:S(2)}) collective-permute-start(bf16[32,896]{1,0:T(8,128)(2,1)S(1)} %pad_maximum_fusion.1), channel_id=1, source_target_pairs={{0,8},{1,9},{2,10},{3,11},{4,12},{5,13},{6,14},{7,15},{8,0},{9,1},... | collective-permute-start | bytes 172040 | tf_op jit(solution)/shard_map/ppermute | solution.py:111
  11.9 8.4 %collective-permute-start.4 = (bf16[128,896]{1,0:T(8,128)(2,1)S(1)}, bf16[128,896]{1,0:T(8,128)(2,1)S(1)}, u32[]{:S(2)}, u32[]{:S(2)}) collective-permute-start(bf16[128,896]{1,0:T(8,128)(2,1)S(1)} %pad_maximum_fusion.refs_0_), channel_id=1, source_target_pairs={{0,4},{1,3},{2,6},{3,1},{4,0},{5,7},{6,2},{7,5},{8,12},{9,11},{10,... | collective-permute-start | bytes 688136 | tf_op jit(solution)/shard_map/ppermute | solution.py:111
  13.4 7.4 %collective-permute-start.6 = (bf16[128,896]{1,0:T(8,128)(2,1)S(1)}, bf16[128,896]{1,0:T(8,128)(2,1)S(1)}, u32[]{:S(2)}, u32[]{:S(2)}) collective-permute-start(bf16[128,896]{1,0:T(8,128)(2,1)S(1)} %pad_maximum_fusion.refs_0_), channel_id=1, source_target_pairs={{0,2},{1,5},{2,0},{3,7},{4,6},{5,1},{6,4},{7,3},{8,10},{9,13},{10,... | collective-permute-start | bytes 688136 | tf_op jit(solution)/shard_map/ppermute | solution.py:111
  20.3 6.0 %collective-permute-start.8 = (bf16[128,896]{1,0:T(8,128)(2,1)S(1)}, bf16[128,896]{1,0:T(8,128)(2,1)S(1)}, u32[]{:S(2)}, u32[]{:S(2)}) collective-permute-start(bf16[128,896]{1,0:T(8,128)(2,1)S(1)} %collective-permute-done.4.refs_2_), channel_id=1, source_target_pairs={{0,2},{1,5},{2,0},{3,7},{4,6},{5,1},{6,4},{7,3},{8,10},{9,13},{10,... | collective-permute-start | bytes 688136 | tf_op jit(solution)/shard_map/ppermute | solution.py:111
  20.3 6.0 %collective-permute-start.3 = (bf16[128,896]{1,0:T(8,128)(2,1)S(1)}, bf16[128,896]{1,0:T(8,128)(2,1)S(1)}, u32[]{:S(2)}, u32[]{:S(2)}) collective-permute-start(bf16[128,896]{1,0:T(8,128)(2,1)S(1)} %pad_maximum_fusion.refs_0_), channel_id=1, source_target_pairs={{0,1},{1,0},{2,3},{3,2},{4,5},{5,4},{6,7},{7,6},{8,9},{9,8},{10,11... | collective-permute-start | bytes 688136 | tf_op jit(solution)/shard_map/ppermute | solution.py:111
  20.3 6.0 %collective-permute-start.5 = (bf16[128,896]{1,0:T(8,128)(2,1)S(1)}, bf16[128,896]{1,0:T(8,128)(2,1)S(1)}, u32[]{:S(2)}, u32[]{:S(2)}) collective-permute-start(bf16[128,896]{1,0:T(8,128)(2,1)S(1)} %collective-permute-done.4.refs_2_), channel_id=1, source_target_pairs={{0,1},{1,0},{2,3},{3,2},{4,5},{5,4},{6,7},{7,6},{8,9},{9,8},{10,11... | collective-permute-start | bytes 688136 | tf_op jit(solution)/shard_map/ppermute | solution.py:111
  20.8 5.5 %collective-permute-start.7 = (bf16[128,896]{1,0:T(8,128)(2,1)S(1)}, bf16[128,896]{1,0:T(8,128)(2,1)S(1)}, u32[]{:S(2)}, u32[]{:S(2)}) collective-permute-start(bf16[128,896]{1,0:T(8,128)(2,1)S(1)} %collective-permute-done.6.refs_4_), channel_id=1, source_target_pairs={{0,1},{1,0},{2,3},{3,2},{4,5},{5,4},{6,7},{7,6},{8,9},{9,8},{10,11... | collective-permute-start | bytes 688136 | tf_op jit(solution)/shard_map/ppermute | solution.py:111
  26.3 1.5 %collective-permute-start.9 = (bf16[128,896]{1,0:T(8,128)(2,1)S(1)}, bf16[128,896]{1,0:T(8,128)(2,1)S(1)}, u32[]{:S(2)}, u32[]{:S(2)}) collective-permute-start(bf16[128,896]{1,0:T(8,128)(2,1)S(1)} %collective-permute-done.8.refs_6_), channel_id=1, source_target_pairs={{0,1},{1,0},{2,3},{3,2},{4,5},{5,4},{6,7},{7,6},{8,9},{9,8},{10,11... | collective-permute-start | bytes 688136 | tf_op jit(solution)/shard_map/ppermute | solution.py:111

commit v2 on v1

--- a/solution.py
+++ b/solution.py
@@ -55,6 +55,13 @@
                 total = total + factors[j][t - b] * rows[j]
             tiles[t] = tiles[t] - total
     return [tile * lax.rsqrt(p) for tile, p in zip(tiles, pivots)]
+
+
+def pack_kernel(vecs, feat, e_ref, s_ref, o_ref):
+    o_ref[:, :feat] = e_ref[...]
+    high = s_ref[...].astype(jnp.bfloat16)
+    low = (s_ref[...] - high.astype(jnp.float32)).astype(jnp.bfloat16)
+    o_ref[:, feat:] = jnp.concatenate([high, low], axis=1)
 
 
 def embed_kernel(pieces, own, vecs, feat, *refs):
@@ -115,10 +122,12 @@
     own, feat = embeddings.shape
     vecs = start_block.shape[0]
     send = functools.partial(exchange, rows=rows, cols=cols)
-    start = start_block.T
-    high = start.astype(jnp.bfloat16)
-    low = (start - high.astype(jnp.float32)).astype(jnp.bfloat16)
-    mine = jnp.concatenate([embeddings, high, low], axis=1)
+    mine = pl.pallas_call(
+        functools.partial(pack_kernel, vecs, feat),
+        out_shape=jax.ShapeDtypeStruct((own, feat + 2 * vecs), jnp.bfloat16),
+        in_specs=[pl.BlockSpec(memory_space=pltpu.VMEM)] * 2,
+        out_specs=pl.BlockSpec(memory_space=pltpu.VMEM),
+    )(embeddings, start_block.T)
     along_z = [send(mine, partner=lambda r, c, d=d: (r ^ (2 * d), c)) for d in (1, 2, 3)]
     a = jnp.concatenate([mine] + along_z, axis=0)
     b = send(a, partner=lambda r, c: (r, c ^ 2) if c & 1 else (r ^ 1, c))

time: 47 us -> 47.8 us (1.017)
  Pallas kernels: 19 us -> 20.4 us
  other arithmetic: 1.75 us -> 0.84 us
    pallas_call x0 -> x1, Pallas kernels: none -> 1.49 us  [replicated(): pl.pallas_call(functools.partial(pack_kernel, vecs, feat), out_shape=jax....]
    concatenate x1 -> x0, other arithmetic: 0.95 us -> none  [replicated(): mine = jnp.concatenate([embeddings, high, low], axis=1)]
    concatenate x1, other arithmetic: 0.08 us -> 0.84 us  [replicated(): a = jnp.concatenate([mine] + along_z, axis=0)]
    convert_element_type x1 -> x0, other arithmetic: 0.72 us -> none  [replicated(): low = (start - high.astype(jnp.float32)).astype(jnp.bfloat16)]
where the time goes in v2:
time: 47.8 us; the launch traced here: 47.6 us
  Pallas kernels  20.4 us (43%)
  waiting for transfers between devices  17.1 us (36%)
  starting transfers between devices  9.23 us (19%)
  other arithmetic  0.84 us (2%)
    pallas_call x1, Pallas kernels, replicated(): pl.pallas_call(functools.partial(embed_kernel, count, own, vecs, feat), o...  18.9 us
    ppermute x10, waiting for transfers between devices, exchange(): return lax.ppermute(x, ('row', 'col'), pairs)  17.1 us
    ppermute x10, starting transfers between devices, exchange(): return lax.ppermute(x, ('row', 'col'), pairs)  9.23 us
    pallas_call x1, Pallas kernels, replicated(): pl.pallas_call(functools.partial(pack_kernel, vecs, feat), out_shape=jax....  1.49 us
  transfers between devices with their start and end apart: 10, of which 5 were waited for; matrix products, arithmetic and copies ran while one was open for 0% of the time, Pallas kernels for 0%

profile of v2, /device:TPU:0, one launch (start us, length us, event | category | flops | bytes accessed | tf_op | source)
XLA Modules:
  0.0 47.6 jit_solution(2937323542957398801)
XLA Ops:
  0.0 1.5 %shard_map.28 = bf16[32,896]{1,0:T(8,128)(2,1)} custom-call(bf16[32,768]{1,0:T(8,128)(2,1)} %e_ref.1, f32[32,64]{1,0:T(8,128)} %bitcast.2), custom_call_target="tpu_custom_call" | custom-call | tf_op jit(solution)/shard_map/pallas_call | solution.py:125
  1.5 5.0 %collective-permute-start.2 = (bf16[32,896]{1,0:T(8,128)(2,1)}, bf16[32,896]{1,0:T(8,128)(2,1)S(1)}, u32[]{:S(2)}, u32[]{:S(2)}) collective-permute-start(bf16[32,896]{1,0:T(8,128)(2,1)} %shard_map.28), channel_id=1, source_target_pairs={{0,24},{1,25},{2,26},{3,27},{4,28},{5,29},{6,30},{7,31},{8,16},{9,... | collective-permute-start | bytes 172040 | tf_op jit(solution)/shard_map/ppermute | solution.py:118
  6.5 0.0 collective-permute-start.1
  6.5 0.6 %collective-permute-start = (bf16[32,896]{1,0:T(8,128)(2,1)}, bf16[32,896]{1,0:T(8,128)(2,1)S(1)}, u32[]{:S(2)}, u32[]{:S(2)}) collective-permute-start(bf16[32,896]{1,0:T(8,128)(2,1)} %shard_map.28), channel_id=1, source_target_pairs={{0,8},{1,9},{2,10},{3,11},{4,12},{5,13},{6,14},{7,15},{8,0},{9,1},... | collective-permute-start | bytes 172040 | tf_op jit(solution)/shard_map/ppermute | solution.py:118
  7.1 2.1 %collective-permute-done.2 = bf16[32,896]{1,0:T(8,128)(2,1)S(1)} collective-permute-done((bf16[32,896]{1,0:T(8,128)(2,1)}, bf16[32,896]{1,0:T(8,128)(2,1)S(1)}, u32[]{:S(2)}, u32[]{:S(2)}) %collective-permute-start.2) | collective-permute-done | bytes 57376 | tf_op jit(solution)/shard_map/ppermute | solution.py:118
  9.2 2.6 %collective-permute-done.1 = bf16[32,896]{1,0:T(8,128)(2,1)S(1)} collective-permute-done((bf16[32,896]{1,0:T(8,128)(2,1)}, bf16[32,896]{1,0:T(8,128)(2,1)S(1)}, u32[]{:S(2)}, u32[]{:S(2)}) %collective-permute-start.1) | collective-permute-done | bytes 57376 | tf_op jit(solution)/shard_map/ppermute | solution.py:118
  11.8 0.0 collective-permute-done
  11.8 0.8 %pad_maximum_fusion.refs_0_ = bf16[128,896]{1,0:T(8,128)(2,1)S(1)} fusion(bf16[32,896]{1,0:T(8,128)(2,1)S(1)} %collective-permute-done.2, bf16[32,896]{1,0:T(8,128)(2,1)S(1)} %collective-permute-done.1, bf16[32,896]{1,0:T(8,128)(2,1)S(1)} %collective-permute-done, bf16[32,896]{1,0:T(8,128)(2,1)} %shard_map.28), kind=kLoop, calls=%fused_computation | loop fusion | flops 917504 | bytes 458752 | tf_op jit(solution)/shard_map/concatenate | solution.py:132
  12.7 1.6 %collective-permute-start.4 = (bf16[128,896]{1,0:T(8,128)(2,1)S(1)}, bf16[128,896]{1,0:T(8,128)(2,1)S(1)}, u32[]{:S(2)}, u32[]{:S(2)}) collective-permute-start(bf16[128,896]{1,0:T(8,128)(2,1)S(1)} %pad_maximum_fusion.refs_0_), channel_id=1, source_target_pairs={{0,4},{1,3},{2,6},{3,1},{4,0},{5,7},{6,2},{7,5},{8,12},{9,11},{10,... | collective-permute-start | bytes 688136 | tf_op jit(solution)/shard_map/ppermute | solution.py:118
  14.3 1.5 %collective-permute-start.6 = (bf16[128,896]{1,0:T(8,128)(2,1)S(1)}, bf16[128,896]{1,0:T(8,128)(2,1)S(1)}, u32[]{:S(2)}, u32[]{:S(2)}) collective-permute-start(bf16[128,896]{1,0:T(8,128)(2,1)S(1)} %pad_maximum_fusion.refs_0_), channel_id=1, source_target_pairs={{0,2},{1,5},{2,0},{3,7},{4,6},{5,1},{6,4},{7,3},{8,10},{9,13},{10,... | collective-permute-start | bytes 688136 | tf_op jit(solution)/shard_map/ppermute | solution.py:118
  15.8 5.4 %collective-permute-done.4.refs_2_ = bf16[128,896]{1,0:T(8,128)(2,1)S(1)} collective-permute-done((bf16[128,896]{1,0:T(8,128)(2,1)S(1)}, bf16[128,896]{1,0:T(8,128)(2,1)S(1)}, u32[]{:S(2)}, u32[]{:S(2)}) %collective-permute-start.4) | collective-permute-done | bytes 229408 | tf_op jit(solution)/shard_map/ppermute | solution.py:118
  21.1 0.0 collective-permute-start.8
  21.2 0.0 collective-permute-start.3
  21.2 0.5 %collective-permute-start.5 = (bf16[128,896]{1,0:T(8,128)(2,1)S(1)}, bf16[128,896]{1,0:T(8,128)(2,1)S(1)}, u32[]{:S(2)}, u32[]{:S(2)}) collective-permute-start(bf16[128,896]{1,0:T(8,128)(2,1)S(1)} %collective-permute-done.4.refs_2_), channel_id=1, source_target_pairs={{0,1},{1,0},{2,3},{3,2},{4,5},{5,4},{6,7},{7,6},{8,9},{9,8},{10,11... | collective-permute-start | bytes 688136 | tf_op jit(solution)/shard_map/ppermute | solution.py:118
  21.7 0.0 collective-permute-done.6.refs_4_
  21.7 0.0 collective-permute-start.7
  21.7 5.5 %collective-permute-done.8.refs_6_ = bf16[128,896]{1,0:T(8,128)(2,1)S(1)} collective-permute-done((bf16[128,896]{1,0:T(8,128)(2,1)S(1)}, bf16[128,896]{1,0:T(8,128)(2,1)S(1)}, u32[]{:S(2)}, u32[]{:S(2)}) %collective-permute-start.8) | collective-permute-done | bytes 229408 | tf_op jit(solution)/shard_map/ppermute | solution.py:118
  27.2 0.0 collective-permute-start.9
  27.2 0.0 collective-permute-done.3.refs_1_
  27.2 0.0 collective-permute-done.7.refs_5_
  27.2 0.0 collective-permute-done.5.refs_3_
  27.2 1.5 %collective-permute-done.9.refs_7_ = bf16[128,896]{1,0:T(8,128)(2,1)S(1)} collective-permute-done((bf16[128,896]{1,0:T(8,128)(2,1)S(1)}, bf16[128,896]{1,0:T(8,128)(2,1)S(1)}, u32[]{:S(2)}, u32[]{:S(2)}) %collective-permute-start.9) | collective-permute-done | bytes 229408 | tf_op jit(solution)/shard_map/ppermute | solution.py:118
  28.7 18.9 %shard_map.29 = f32[32,64]{1,0:T(8,128)} custom-call(bf16[128,896]{1,0:T(8,128)(2,1)S(1)} %pad_maximum_fusion.refs_0_, bf16[128,896]{1,0:T(8,128)(2,1)S(1)} %collective-permute-done.3.refs_1_, bf16[128,896]{1,0:T(8,128)(2,1)S(1)} %collective-permute-done.4.refs_2_, bf16[128,896]{1,0:T(8,128)(2,1)S(1)} %collective-permute-done.5.refs_3_, ...), custom_call_target="tpu_custom_call" | custom-call | tf_op jit(solution)/shard_map/pallas_call | solution.py:141
Async XLA Ops:
  1.5 7.7 %collective-permute-start.2 = (bf16[32,896]{1,0:T(8,128)(2,1)}, bf16[32,896]{1,0:T(8,128)(2,1)S(1)}, u32[]{:S(2)}, u32[]{:S(2)}) collective-permute-start(bf16[32,896]{1,0:T(8,128)(2,1)} %shard_map.28), channel_id=1, source_target_pairs={{0,24},{1,25},{2,26},{3,27},{4,28},{5,29},{6,30},{7,31},{8,16},{9,... | collective-permute-start | bytes 172040 | tf_op jit(solution)/shard_map/ppermute | solution.py:118
  6.5 5.3 %collective-permute-start.1 = (bf16[32,896]{1,0:T(8,128)(2,1)}, bf16[32,896]{1,0:T(8,128)(2,1)S(1)}, u32[]{:S(2)}, u32[]{:S(2)}) collective-permute-start(bf16[32,896]{1,0:T(8,128)(2,1)} %shard_map.28), channel_id=1, source_target_pairs={{0,16},{1,17},{2,18},{3,19},{4,20},{5,21},{6,22},{7,23},{8,24},{9,... | collective-permute-start | bytes 172040 | tf_op jit(solution)/shard_map/ppermute | solution.py:118
  6.5 5.3 %collective-permute-start = (bf16[32,896]{1,0:T(8,128)(2,1)}, bf16[32,896]{1,0:T(8,128)(2,1)S(1)}, u32[]{:S(2)}, u32[]{:S(2)}) collective-permute-start(bf16[32,896]{1,0:T(8,128)(2,1)} %shard_map.28), channel_id=1, source_target_pairs={{0,8},{1,9},{2,10},{3,11},{4,12},{5,13},{6,14},{7,15},{8,0},{9,1},... | collective-permute-start | bytes 172040 | tf_op jit(solution)/shard_map/ppermute | solution.py:118
  12.7 8.5 %collective-permute-start.4 = (bf16[128,896]{1,0:T(8,128)(2,1)S(1)}, bf16[128,896]{1,0:T(8,128)(2,1)S(1)}, u32[]{:S(2)}, u32[]{:S(2)}) collective-permute-start(bf16[128,896]{1,0:T(8,128)(2,1)S(1)} %pad_maximum_fusion.refs_0_), channel_id=1, source_target_pairs={{0,4},{1,3},{2,6},{3,1},{4,0},{5,7},{6,2},{7,5},{8,12},{9,11},{10,... | collective-permute-start | bytes 688136 | tf_op jit(solution)/shard_map/ppermute | solution.py:118
  14.3 7.4 %collective-permute-start.6 = (bf16[128,896]{1,0:T(8,128)(2,1)S(1)}, bf16[128,896]{1,0:T(8,128)(2,1)S(1)}, u32[]{:S(2)}, u32[]{:S(2)}) collective-permute-start(bf16[128,896]{1,0:T(8,128)(2,1)S(1)} %pad_maximum_fusion.refs_0_), channel_id=1, source_target_pairs={{0,2},{1,5},{2,0},{3,7},{4,6},{5,1},{6,4},{7,3},{8,10},{9,13},{10,... | collective-permute-start | bytes 688136 | tf_op jit(solution)/shard_map/ppermute | solution.py:118
  21.1 6.0 %collective-permute-start.8 = (bf16[128,896]{1,0:T(8,128)(2,1)S(1)}, bf16[128,896]{1,0:T(8,128)(2,1)S(1)}, u32[]{:S(2)}, u32[]{:S(2)}) collective-permute-start(bf16[128,896]{1,0:T(8,128)(2,1)S(1)} %collective-permute-done.4.refs_2_), channel_id=1, source_target_pairs={{0,2},{1,5},{2,0},{3,7},{4,6},{5,1},{6,4},{7,3},{8,10},{9,13},{10,... | collective-permute-start | bytes 688136 | tf_op jit(solution)/shard_map/ppermute | solution.py:118
  21.2 6.0 %collective-permute-start.3 = (bf16[128,896]{1,0:T(8,128)(2,1)S(1)}, bf16[128,896]{1,0:T(8,128)(2,1)S(1)}, u32[]{:S(2)}, u32[]{:S(2)}) collective-permute-start(bf16[128,896]{1,0:T(8,128)(2,1)S(1)} %pad_maximum_fusion.refs_0_), channel_id=1, source_target_pairs={{0,1},{1,0},{2,3},{3,2},{4,5},{5,4},{6,7},{7,6},{8,9},{9,8},{10,11... | collective-permute-start | bytes 688136 | tf_op jit(solution)/shard_map/ppermute | solution.py:118
  21.2 6.0 %collective-permute-start.5 = (bf16[128,896]{1,0:T(8,128)(2,1)S(1)}, bf16[128,896]{1,0:T(8,128)(2,1)S(1)}, u32[]{:S(2)}, u32[]{:S(2)}) collective-permute-start(bf16[128,896]{1,0:T(8,128)(2,1)S(1)} %collective-permute-done.4.refs_2_), channel_id=1, source_target_pairs={{0,1},{1,0},{2,3},{3,2},{4,5},{5,4},{6,7},{7,6},{8,9},{9,8},{10,11... | collective-permute-start | bytes 688136 | tf_op jit(solution)/shard_map/ppermute | solution.py:118
  21.7 5.5 %collective-permute-start.7 = (bf16[128,896]{1,0:T(8,128)(2,1)S(1)}, bf16[128,896]{1,0:T(8,128)(2,1)S(1)}, u32[]{:S(2)}, u32[]{:S(2)}) collective-permute-start(bf16[128,896]{1,0:T(8,128)(2,1)S(1)} %collective-permute-done.6.refs_4_), channel_id=1, source_target_pairs={{0,1},{1,0},{2,3},{3,2},{4,5},{5,4},{6,7},{7,6},{8,9},{9,8},{10,11... | collective-permute-start | bytes 688136 | tf_op jit(solution)/shard_map/ppermute | solution.py:118
  27.2 1.5 %collective-permute-start.9 = (bf16[128,896]{1,0:T(8,128)(2,1)S(1)}, bf16[128,896]{1,0:T(8,128)(2,1)S(1)}, u32[]{:S(2)}, u32[]{:S(2)}) collective-permute-start(bf16[128,896]{1,0:T(8,128)(2,1)S(1)} %collective-permute-done.8.refs_6_), channel_id=1, source_target_pairs={{0,1},{1,0},{2,3},{3,2},{4,5},{5,4},{6,7},{7,6},{8,9},{9,8},{10,11... | collective-permute-start | bytes 688136 | tf_op jit(solution)/shard_map/ppermute | solution.py:118

commit v3 on v2

--- a/solution.py
+++ b/solution.py
@@ -23,30 +23,28 @@
     return jnp.broadcast_to(x[r : r + 1, :], x.shape)
 
 
-def reciprocal(p):
-    q = pltpu.reciprocal(p, approx=True)
-    q = q * (2.0 - p * q)
-    return q * (2.0 - p * q)
-
-
 def inverse_factor(tiles):
     count = len(tiles)
     sub = lax.broadcasted_iota(jnp.int32, tiles[0].shape, 0)
     pivots = [None] * count
+    ahead = [lane_splat(tiles[0], j) for j in range(8)]
     for b in range(count):
-        columns = [[lane_splat(tiles[t], 8 * b + j) for t in range(b, count)] for j in range(8)]
+        columns = [[ahead[j]] + [lane_splat(tiles[t], 8 * b + j) for t in range(b + 1, count)] for j in range(8)]
+        if b + 1 < count:
+            ahead = [lane_splat(tiles[b + 1], 8 * (b + 1) + j) for j in range(8)]
         factors, rows = [], []
         for j in range(8):
             pivot = row_splat(columns[j][0], j)
-            q = reciprocal(pivot)
+            q = pltpu.reciprocal(pivot, approx=True)
             m = [d * q for d in columns[j]]
-            m[0] = jnp.where(sub > j, m[0], 0.0)
-            row = row_splat(tiles[b], j)
-            tiles[b] = tiles[b] - m[0] * row
-            pivots[b] = pivot if j == 0 else jnp.where(sub >= j, pivot, pivots[b])
             for l in range(j + 1, 8):
                 head = row_splat(columns[l][0], j)
                 columns[l] = [d - f * head for d, f in zip(columns[l], m)]
+            if b + 1 < count:
+                ahead = [d - m[1] * row_splat(columns[j][1], l) for l, d in enumerate(ahead)]
+            row = row_splat(tiles[b], j)
+            tiles[b] = tiles[b] - jnp.where(sub > j, m[0], 0.0) * row
+            pivots[b] = pivot if j == 0 else jnp.where(sub >= j, pivot, pivots[b])
             factors.append(m)
             rows.append(row)
         for t in range(b + 1, count):
@@ -62,6 +60,18 @@
     high = s_ref[...].astype(jnp.bfloat16)
     low = (s_ref[...] - high.astype(jnp.float32)).astype(jnp.bfloat16)
     o_ref[:, feat:] = jnp.concatenate([high, low], axis=1)
+
+
+def split(x, parts):
+    out = []
+    for _ in range(parts - 1):
+        out.append(x.astype(jnp.bfloat16))
+        x = x - out[-1].astype(jnp.float32)
+    return out + [x.astype(jnp.bfloat16)]
+
+
+def dot(a, b, dims=NN):
+    return lax.dot_general(a, b, dims, preferred_element_type=jnp.float32)
 
 
 def embed_kernel(pieces, own, vecs, feat, *refs):
@@ -77,7 +87,7 @@
     cols, rows = [], []
     for i in range(pieces):
         e = e_ref[i * per : (i + 1) * per, :]
-        d = jnp.where(eye, lax.dot_general(e, e, NT, preferred_element_type=jnp.float32), 0.0)
+        d = jnp.where(eye, dot(e, e, NT), 0.0)
         cols.append(jnp.sum(d, axis=1, keepdims=True))
         rows.append(jnp.sum(d, axis=0, keepdims=True))
     row_sq = jnp.concatenate(rows, axis=1)
@@ -85,7 +95,7 @@
     degree = jnp.zeros((1, points), jnp.float32)
     step = 2 * per
     for i in range(points // step):
-        g = lax.dot_general(e_ref[i * step : (i + 1) * step, :], e_ref[...], NT, preferred_element_type=jnp.float32)
+        g = dot(e_ref[i * step : (i + 1) * step, :], e_ref[...], NT)
         col_sq = jnp.concatenate(cols[2 * i : 2 * i + 2], axis=0)
         k = jnp.exp((2.0 * g - col_sq - row_sq) * rate)
         degree = degree + jnp.sum(k, axis=0, keepdims=True)
@@ -93,20 +103,32 @@
     scale = 1.0 / jnp.sqrt(degree)
     lane = lax.broadcasted_iota(jnp.int32, (vecs, 2 * vecs), 1)
     unit = (lane == lax.broadcasted_iota(jnp.int32, (vecs, 2 * vecs), 0) + vecs).astype(jnp.float32)
+    scaled = (v_ref[...] * scale).astype(jnp.bfloat16)
+    mixed = dot(scaled, k_ref[...]) * scale
     for sweep in range(ITERS):
-        scaled = (v_ref[...] * scale).astype(jnp.bfloat16)
-        mixed = lax.dot_general(scaled, k_ref[...], NN, preferred_element_type=jnp.float32) * scale
-        m_ref[:vecs, :] = mixed
-        m_ref[vecs:, :] = mixed
-        gram = lax.dot_general(mixed, m_ref[...], NT, preferred_element_type=jnp.float32, precision=HIGHEST)
-        full = jnp.where(lane < vecs, gram, unit)
+        last = sweep == ITERS - 1
+        for i, part in enumerate(split(mixed, 3)):
+            m_ref[i * vecs : (i + 1) * vecs, :] = part
+        p = dot(m_ref[...], m_ref[...], NT)
+        p = p[:vecs] + p[vecs : 2 * vecs] + p[2 * vecs :]
+        p = p[:, : 2 * vecs] + jnp.concatenate([p[:, 2 * vecs :], jnp.zeros((vecs, vecs), jnp.float32)], axis=1)
+        p = p + pltpu.roll(p, vecs, 1)
+        full = jnp.where(lane < vecs, p, unit)
+        if not last:
+            weighted = jnp.concatenate(split(mixed * scale, 2), axis=0)
+            ahead = dot(weighted, k_ref[...])
+            ahead = (ahead[:vecs] + ahead[vecs:]) * scale
         inv = jnp.concatenate(inverse_factor([full[8 * t : 8 * t + 8, :] for t in range(vecs // 8)]), axis=0)
         inv = jnp.where(lane < vecs, 0.0, inv)
-        if sweep < ITERS - 1:
-            v_ref[...] = lax.dot_general(inv, m_ref[...], NN, preferred_element_type=jnp.float32, precision=HIGHEST)
+        if not last:
+            inv = inv + pltpu.roll(inv, vecs, 1)
+            parts = jnp.concatenate(split(inv, 2), axis=0)
+            mixed = dot(parts, jnp.concatenate(split(ahead, 2), axis=0))
+            mixed = mixed[:vecs] + mixed[vecs:]
         else:
-            last = lax.dot_general(inv, m_ref[:, :per], NN, preferred_element_type=jnp.float32, precision=HIGHEST)
-            out_ref[...] = last.T[:own, :] * math.sqrt(points)
+            mine = mixed[:, :per]
+            vectors = lax.dot_general(inv, jnp.concatenate([mine, mine], axis=0), NN, preferred_element_type=jnp.float32, precision=HIGHEST)
+            out_ref[...] = vectors.T[:own, :] * math.sqrt(points)
 
 
 def exchange(x, rows, cols, partner):
@@ -124,7 +146,7 @@
     send = functools.partial(exchange, rows=rows, cols=cols)
     mine = pl.pallas_call(
         functools.partial(pack_kernel, vecs, feat),
-        out_shape=jax.ShapeDtypeStruct((own, feat + 2 * vecs), jnp.bfloat16),
+        out_shape=pltpu.VMEM((own, feat + 2 * vecs), jnp.bfloat16),
         in_specs=[pl.BlockSpec(memory_space=pltpu.VMEM)] * 2,
         out_specs=pl.BlockSpec(memory_space=pltpu.VMEM),
     )(embeddings, start_block.T)
@@ -147,7 +169,7 @@
             pltpu.VMEM((points, feat), jnp.bfloat16),
             pltpu.VMEM((points, points), jnp.bfloat16),
             pltpu.VMEM((vecs, points), jnp.float32),
-            pltpu.VMEM((2 * vecs, points), jnp.float32),
+            pltpu.VMEM((3 * vecs, points), jnp.bfloat16),
         ],
         compiler_params=pltpu.CompilerParams(vmem_limit_bytes=40 * 1024 * 1024),
     )(*pieces).T

time: 47.8 us -> 37.9 us (0.79)
  Pallas kernels: 20.4 us -> 11.6 us
  other arithmetic: 0.84 us -> 0.02 us
    pallas_call x1, Pallas kernels: 18.9 us -> 10.7 us  [replicated(): pl.pallas_call(functools.partial(embed_kernel, count, own, vecs, feat), o...]
    concatenate x1, other arithmetic: 0.84 us -> 0.02 us  [replicated(): a = jnp.concatenate([mine] + along_z, axis=0)]
    pallas_call x1, Pallas kernels: 1.49 us -> 0.88 us  [replicated(): pl.pallas_call(functools.partial(pack_kernel, vecs, feat), out_shape=pltp...]
where the time goes in v3:
time: 37.9 us; the launch traced here: 37.8 us
  waiting for transfers between devices  16.8 us (44%)
  Pallas kernels  11.6 us (31%)
  starting transfers between devices  9.32 us (25%)
    ppermute x10, waiting for transfers between devices, exchange(): return lax.ppermute(x, ('row', 'col'), pairs)  16.8 us
    pallas_call x1, Pallas kernels, replicated(): pl.pallas_call(functools.partial(embed_kernel, count, own, vecs, feat), o...  10.7 us
    ppermute x10, starting transfers between devices, exchange(): return lax.ppermute(x, ('row', 'col'), pairs)  9.32 us
    pallas_call x1, Pallas kernels, replicated(): pl.pallas_call(functools.partial(pack_kernel, vecs, feat), out_shape=pltp...  0.88 us
  transfers between devices with their start and end apart: 10, of which 5 were waited for; matrix products, arithmetic and copies ran while one was open for 0% of the time, Pallas kernels for 0%

profile of v3, /device:TPU:0, one launch (start us, length us, event | category | flops | bytes accessed | tf_op | source)
XLA Modules:
  0.0 37.8 jit_solution(14917377235296592085)
XLA Ops:
  0.0 0.9 %shard_map.28 = bf16[32,896]{1,0:T(8,128)(2,1)S(1)} custom-call(bf16[32,768]{1,0:T(8,128)(2,1)} %e_ref.1, f32[32,64]{1,0:T(8,128)} %bitcast.2), custom_call_target="tpu_custom_call" | custom-call | tf_op jit(solution)/shard_map/pallas_call | solution.py:147
  0.9 5.1 %collective-permute-start.2 = (bf16[32,896]{1,0:T(8,128)(2,1)S(1)}, bf16[32,896]{1,0:T(8,128)(2,1)S(1)}, u32[]{:S(2)}, u32[]{:S(2)}) collective-permute-start(bf16[32,896]{1,0:T(8,128)(2,1)S(1)} %shard_map.28), channel_id=1, source_target_pairs={{0,24},{1,25},{2,26},{3,27},{4,28},{5,29},{6,30},{7,31},{8,16},{9,... | collective-permute-start | bytes 172040 | tf_op jit(solution)/shard_map/ppermute | solution.py:140
  5.9 0.0 collective-permute-start.1
  5.9 0.6 %collective-permute-start = (bf16[32,896]{1,0:T(8,128)(2,1)S(1)}, bf16[32,896]{1,0:T(8,128)(2,1)S(1)}, u32[]{:S(2)}, u32[]{:S(2)}) collective-permute-start(bf16[32,896]{1,0:T(8,128)(2,1)S(1)} %shard_map.28), channel_id=1, source_target_pairs={{0,8},{1,9},{2,10},{3,11},{4,12},{5,13},{6,14},{7,15},{8,0},{9,1},... | collective-permute-start | bytes 172040 | tf_op jit(solution)/shard_map/ppermute | solution.py:140
  6.6 1.8 %collective-permute-done.2 = bf16[32,896]{1,0:T(8,128)(2,1)S(1)} collective-permute-done((bf16[32,896]{1,0:T(8,128)(2,1)S(1)}, bf16[32,896]{1,0:T(8,128)(2,1)S(1)}, u32[]{:S(2)}, u32[]{:S(2)}) %collective-permute-start.2) | collective-permute-done | bytes 57376 | tf_op jit(solution)/shard_map/ppermute | solution.py:140
  8.3 2.7 %collective-permute-done.1 = bf16[32,896]{1,0:T(8,128)(2,1)S(1)} collective-permute-done((bf16[32,896]{1,0:T(8,128)(2,1)S(1)}, bf16[32,896]{1,0:T(8,128)(2,1)S(1)}, u32[]{:S(2)}, u32[]{:S(2)}) %collective-permute-start.1) | collective-permute-done | bytes 57376 | tf_op jit(solution)/shard_map/ppermute | solution.py:140
  11.0 0.0 collective-permute-done
  11.0 1.6 %collective-permute-start.4 = (bf16[128,896]{1,0:T(8,128)(2,1)S(1)}, bf16[128,896]{1,0:T(8,128)(2,1)S(1)}, u32[]{:S(2)}, u32[]{:S(2)}) collective-permute-start(bf16[128,896]{1,0:T(8,128)(2,1)S(1)} %pad_maximum_fusion.refs_0_), channel_id=1, source_target_pairs={{0,4},{1,3},{2,6},{3,1},{4,0},{5,7},{6,2},{7,5},{8,12},{9,11},{10,... | collective-permute-start | bytes 688136 | tf_op jit(solution)/shard_map/ppermute | solution.py:140
  12.6 1.5 %collective-permute-start.6 = (bf16[128,896]{1,0:T(8,128)(2,1)S(1)}, bf16[128,896]{1,0:T(8,128)(2,1)S(1)}, u32[]{:S(2)}, u32[]{:S(2)}) collective-permute-start(bf16[128,896]{1,0:T(8,128)(2,1)S(1)} %pad_maximum_fusion.refs_0_), channel_id=1, source_target_pairs={{0,2},{1,5},{2,0},{3,7},{4,6},{5,1},{6,4},{7,3},{8,10},{9,13},{10,... | collective-permute-start | bytes 688136 | tf_op jit(solution)/shard_map/ppermute | solution.py:140
  14.1 5.4 %collective-permute-done.4.refs_2_ = bf16[128,896]{1,0:T(8,128)(2,1)S(1)} collective-permute-done((bf16[128,896]{1,0:T(8,128)(2,1)S(1)}, bf16[128,896]{1,0:T(8,128)(2,1)S(1)}, u32[]{:S(2)}, u32[]{:S(2)}) %collective-permute-start.4) | collective-permute-done | bytes 229408 | tf_op jit(solution)/shard_map/ppermute | solution.py:140
  19.5 0.0 collective-permute-start.8
  19.5 0.0 collective-permute-start.3
  19.5 0.5 %collective-permute-start.5 = (bf16[128,896]{1,0:T(8,128)(2,1)S(1)}, bf16[128,896]{1,0:T(8,128)(2,1)S(1)}, u32[]{:S(2)}, u32[]{:S(2)}) collective-permute-start(bf16[128,896]{1,0:T(8,128)(2,1)S(1)} %collective-permute-done.4.refs_2_), channel_id=1, source_target_pairs={{0,1},{1,0},{2,3},{3,2},{4,5},{5,4},{6,7},{7,6},{8,9},{9,8},{10,11... | collective-permute-start | bytes 688136 | tf_op jit(solution)/shard_map/ppermute | solution.py:140
  20.0 0.0 collective-permute-done.6.refs_4_
  20.0 0.0 collective-permute-start.7
  20.0 5.5 %collective-permute-done.8.refs_6_ = bf16[128,896]{1,0:T(8,128)(2,1)S(1)} collective-permute-done((bf16[128,896]{1,0:T(8,128)(2,1)S(1)}, bf16[128,896]{1,0:T(8,128)(2,1)S(1)}, u32[]{:S(2)}, u32[]{:S(2)}) %collective-permute-start.8) | collective-permute-done | bytes 229408 | tf_op jit(solution)/shard_map/ppermute | solution.py:140
  25.5 0.0 collective-permute-start.9
  25.5 0.0 collective-permute-done.3.refs_1_
  25.5 0.0 collective-permute-done.7.refs_5_
  25.5 0.0 collective-permute-done.5.refs_3_
  25.6 1.5 %collective-permute-done.9.refs_7_ = bf16[128,896]{1,0:T(8,128)(2,1)S(1)} collective-permute-done((bf16[128,896]{1,0:T(8,128)(2,1)S(1)}, bf16[128,896]{1,0:T(8,128)(2,1)S(1)}, u32[]{:S(2)}, u32[]{:S(2)}) %collective-permute-start.9) | collective-permute-done | bytes 229408 | tf_op jit(solution)/shard_map/ppermute | solution.py:140
  27.0 10.7 %shard_map.29 = f32[32,64]{1,0:T(8,128)} custom-call(bf16[128,896]{1,0:T(8,128)(2,1)S(1)} %pad_maximum_fusion.refs_0_, bf16[128,896]{1,0:T(8,128)(2,1)S(1)} %collective-permute-done.3.refs_1_, bf16[128,896]{1,0:T(8,128)(2,1)S(1)} %collective-permute-done.4.refs_2_, bf16[128,896]{1,0:T(8,128)(2,1)S(1)} %collective-permute-done.5.refs_3_, ...), custom_call_target="tpu_custom_call" | custom-call | tf_op jit(solution)/shard_map/pallas_call | solution.py:163
  (1 shorter events, 0.0 us)
Async XLA Ops:
  0.9 7.5 %collective-permute-start.2 = (bf16[32,896]{1,0:T(8,128)(2,1)S(1)}, bf16[32,896]{1,0:T(8,128)(2,1)S(1)}, u32[]{:S(2)}, u32[]{:S(2)}) collective-permute-start(bf16[32,896]{1,0:T(8,128)(2,1)S(1)} %shard_map.28), channel_id=1, source_target_pairs={{0,24},{1,25},{2,26},{3,27},{4,28},{5,29},{6,30},{7,31},{8,16},{9,... | collective-permute-start | bytes 172040 | tf_op jit(solution)/shard_map/ppermute | solution.py:140
  5.9 5.1 %collective-permute-start.1 = (bf16[32,896]{1,0:T(8,128)(2,1)S(1)}, bf16[32,896]{1,0:T(8,128)(2,1)S(1)}, u32[]{:S(2)}, u32[]{:S(2)}) collective-permute-start(bf16[32,896]{1,0:T(8,128)(2,1)S(1)} %shard_map.28), channel_id=1, source_target_pairs={{0,16},{1,17},{2,18},{3,19},{4,20},{5,21},{6,22},{7,23},{8,24},{9,... | collective-permute-start | bytes 172040 | tf_op jit(solution)/shard_map/ppermute | solution.py:140
  5.9 5.1 %collective-permute-start = (bf16[32,896]{1,0:T(8,128)(2,1)S(1)}, bf16[32,896]{1,0:T(8,128)(2,1)S(1)}, u32[]{:S(2)}, u32[]{:S(2)}) collective-permute-start(bf16[32,896]{1,0:T(8,128)(2,1)S(1)} %shard_map.28), channel_id=1, source_target_pairs={{0,8},{1,9},{2,10},{3,11},{4,12},{5,13},{6,14},{7,15},{8,0},{9,1},... | collective-permute-start | bytes 172040 | tf_op jit(solution)/shard_map/ppermute | solution.py:140
  11.0 8.5 %collective-permute-start.4 = (bf16[128,896]{1,0:T(8,128)(2,1)S(1)}, bf16[128,896]{1,0:T(8,128)(2,1)S(1)}, u32[]{:S(2)}, u32[]{:S(2)}) collective-permute-start(bf16[128,896]{1,0:T(8,128)(2,1)S(1)} %pad_maximum_fusion.refs_0_), channel_id=1, source_target_pairs={{0,4},{1,3},{2,6},{3,1},{4,0},{5,7},{6,2},{7,5},{8,12},{9,11},{10,... | collective-permute-start | bytes 688136 | tf_op jit(solution)/shard_map/ppermute | solution.py:140
  12.6 7.4 %collective-permute-start.6 = (bf16[128,896]{1,0:T(8,128)(2,1)S(1)}, bf16[128,896]{1,0:T(8,128)(2,1)S(1)}, u32[]{:S(2)}, u32[]{:S(2)}) collective-permute-start(bf16[128,896]{1,0:T(8,128)(2,1)S(1)} %pad_maximum_fusion.refs_0_), channel_id=1, source_target_pairs={{0,2},{1,5},{2,0},{3,7},{4,6},{5,1},{6,4},{7,3},{8,10},{9,13},{10,... | collective-permute-start | bytes 688136 | tf_op jit(solution)/shard_map/ppermute | solution.py:140
  19.5 6.0 %collective-permute-start.8 = (bf16[128,896]{1,0:T(8,128)(2,1)S(1)}, bf16[128,896]{1,0:T(8,128)(2,1)S(1)}, u32[]{:S(2)}, u32[]{:S(2)}) collective-permute-start(bf16[128,896]{1,0:T(8,128)(2,1)S(1)} %collective-permute-done.4.refs_2_), channel_id=1, source_target_pairs={{0,2},{1,5},{2,0},{3,7},{4,6},{5,1},{6,4},{7,3},{8,10},{9,13},{10,... | collective-permute-start | bytes 688136 | tf_op jit(solution)/shard_map/ppermute | solution.py:140
  19.5 6.0 %collective-permute-start.3 = (bf16[128,896]{1,0:T(8,128)(2,1)S(1)}, bf16[128,896]{1,0:T(8,128)(2,1)S(1)}, u32[]{:S(2)}, u32[]{:S(2)}) collective-permute-start(bf16[128,896]{1,0:T(8,128)(2,1)S(1)} %pad_maximum_fusion.refs_0_), channel_id=1, source_target_pairs={{0,1},{1,0},{2,3},{3,2},{4,5},{5,4},{6,7},{7,6},{8,9},{9,8},{10,11... | collective-permute-start | bytes 688136 | tf_op jit(solution)/shard_map/ppermute | solution.py:140
  19.5 6.0 %collective-permute-start.5 = (bf16[128,896]{1,0:T(8,128)(2,1)S(1)}, bf16[128,896]{1,0:T(8,128)(2,1)S(1)}, u32[]{:S(2)}, u32[]{:S(2)}) collective-permute-start(bf16[128,896]{1,0:T(8,128)(2,1)S(1)} %collective-permute-done.4.refs_2_), channel_id=1, source_target_pairs={{0,1},{1,0},{2,3},{3,2},{4,5},{5,4},{6,7},{7,6},{8,9},{9,8},{10,11... | collective-permute-start | bytes 688136 | tf_op jit(solution)/shard_map/ppermute | solution.py:140
  20.0 5.5 %collective-permute-start.7 = (bf16[128,896]{1,0:T(8,128)(2,1)S(1)}, bf16[128,896]{1,0:T(8,128)(2,1)S(1)}, u32[]{:S(2)}, u32[]{:S(2)}) collective-permute-start(bf16[128,896]{1,0:T(8,128)(2,1)S(1)} %collective-permute-done.6.refs_4_), channel_id=1, source_target_pairs={{0,1},{1,0},{2,3},{3,2},{4,5},{5,4},{6,7},{7,6},{8,9},{9,8},{10,11... | collective-permute-start | bytes 688136 | tf_op jit(solution)/shard_map/ppermute | solution.py:140
  25.5 1.5 %collective-permute-start.9 = (bf16[128,896]{1,0:T(8,128)(2,1)S(1)}, bf16[128,896]{1,0:T(8,128)(2,1)S(1)}, u32[]{:S(2)}, u32[]{:S(2)}) collective-permute-start(bf16[128,896]{1,0:T(8,128)(2,1)S(1)} %collective-permute-done.8.refs_6_), channel_id=1, source_target_pairs={{0,1},{1,0},{2,3},{3,2},{4,5},{5,4},{6,7},{7,6},{8,9},{9,8},{10,11... | collective-permute-start | bytes 688136 | tf_op jit(solution)/shard_map/ppermute | solution.py:140

commit v4 on v3

--- a/solution.py
+++ b/solution.py
@@ -76,16 +76,17 @@
 
 def embed_kernel(pieces, own, vecs, feat, *refs):
     piece_refs, out_ref = refs[:pieces], refs[pieces]
-    e_ref, k_ref, v_ref, m_ref = refs[pieces + 1 :]
-    per = piece_refs[0].shape[0]
-    points = pieces * per
-    for i, piece in enumerate(piece_refs):
-        e_ref[i * per : (i + 1) * per, :] = piece[:, :feat]
-        x0 = piece[:, feat : feat + vecs].astype(jnp.float32) + piece[:, feat + vecs : feat + 2 * vecs].astype(jnp.float32)
-        v_ref[:, i * per : (i + 1) * per] = x0.T
+    e_ref, k_ref, x_ref, m_ref = refs[pieces + 1 :]
+    points, per = e_ref.shape[0], 2 * vecs
+    at = 0
+    for piece in piece_refs:
+        to = at + piece.shape[0]
+        e_ref[at:to, :] = piece[:, :feat]
+        x_ref[at:to, :] = piece[:, feat:].astype(jnp.float32)
+        at = to
     eye = lax.broadcasted_iota(jnp.int32, (per, per), 0) == lax.broadcasted_iota(jnp.int32, (per, per), 1)
     cols, rows = [], []
-    for i in range(pieces):
+    for i in range(points // per):
         e = e_ref[i * per : (i + 1) * per, :]
         d = jnp.where(eye, dot(e, e, NT), 0.0)
         cols.append(jnp.sum(d, axis=1, keepdims=True))
@@ -103,7 +104,8 @@
     scale = 1.0 / jnp.sqrt(degree)
     lane = lax.broadcasted_iota(jnp.int32, (vecs, 2 * vecs), 1)
     unit = (lane == lax.broadcasted_iota(jnp.int32, (vecs, 2 * vecs), 0) + vecs).astype(jnp.float32)
-    scaled = (v_ref[...] * scale).astype(jnp.bfloat16)
+    start = jnp.concatenate([x_ref[i * per : (i + 1) * per, :].T for i in range(points // per)], axis=1)
+    scaled = ((start[:vecs] + start[vecs:]) * scale).astype(jnp.bfloat16)
     mixed = dot(scaled, k_ref[...]) * scale
     for sweep in range(ITERS):
         last = sweep == ITERS - 1
@@ -150,16 +152,20 @@
         in_specs=[pl.BlockSpec(memory_space=pltpu.VMEM)] * 2,
         out_specs=pl.BlockSpec(memory_space=pltpu.VMEM),
     )(embeddings, start_block.T)
+    first = lambda r, c: (r, c ^ 2) if c & 1 else (r ^ 1, c)
+    second = lambda r, c: (r ^ 1, c) if c & 1 else (r, c ^ 2)
+    swap = lambda r, c: (r, c ^ 1)
     along_z = [send(mine, partner=lambda r, c, d=d: (r ^ (2 * d), c)) for d in (1, 2, 3)]
-    a = jnp.concatenate([mine] + along_z, axis=0)
-    b = send(a, partner=lambda r, c: (r, c ^ 2) if c & 1 else (r ^ 1, c))
-    c_ = send(a, partner=lambda r, c: (r ^ 1, c) if c & 1 else (r, c ^ 2))
-    d_ = send(b, partner=lambda r, c: (r ^ 1, c) if c & 1 else (r, c ^ 2))
-    pieces = []
-    for piece in (a, b, c_, d_):
-        pieces += [piece, send(piece, partner=lambda r, c: (r, c ^ 1))]
-    count, per = len(pieces), a.shape[0]
-    points = count * per
+    px, py, pxy = (lambda r, c: (r, c ^ 2)), (lambda r, c: (r ^ 1, c)), (lambda r, c: (r ^ 1, c ^ 2))
+    near = jnp.concatenate([mine, along_z[0]], axis=0)
+    far = jnp.concatenate(along_z[1:], axis=0)
+    pieces = [near, send(near, partner=swap), far, send(far, partner=swap)]
+    for piece in (near, far):
+        for p in (pxy, px, py):
+            got = send(piece, partner=p)
+            pieces += [got, send(got, partner=swap)]
+    count = len(pieces)
+    points = sum(piece.shape[0] for piece in pieces)
     return pl.pallas_call(
         functools.partial(embed_kernel, count, own, vecs, feat),
         out_shape=jax.ShapeDtypeStruct((own, vecs), jnp.float32),
@@ -168,7 +174,7 @@
         scratch_shapes=[
             pltpu.VMEM((points, feat), jnp.bfloat16),
             pltpu.VMEM((points, points), jnp.bfloat16),
-            pltpu.VMEM((vecs, points), jnp.float32),
+            pltpu.VMEM((points, 2 * vecs), jnp.float32),
             pltpu.VMEM((3 * vecs, points), jnp.bfloat16),
         ],
         compiler_params=pltpu.CompilerParams(vmem_limit_bytes=40 * 1024 * 1024),

time: 37.9 us -> 34.4 us (0.908)
  waiting for transfers between devices: 16.8 us -> 8.6 us
  starting transfers between devices: 9.32 us -> 13.8 us
    ppermute x10 -> x17, waiting for transfers between devices: 16.8 us -> 8.6 us  [exchange(): return lax.ppermute(x, ('row', 'col'), pairs)]
    ppermute x10 -> x17, starting transfers between devices: 9.32 us -> 13.8 us  [exchange(): return lax.ppermute(x, ('row', 'col'), pairs)]
  transfers between devices with their start and end apart: 10 -> 17, of which waited for: 5 -> 7; matrix products, arithmetic and copies ran while one was open for 0% -> 0% of each run, Pallas kernels for 0% -> 0%
where the time goes in v4:
time: 34.4 us; the launch traced here: 34.2 us
  starting transfers between devices  13.8 us (40%)
  Pallas kernels  11.7 us (34%)
  waiting for transfers between devices  8.6 us (25%)
    ppermute x17, starting transfers between devices, exchange(): return lax.ppermute(x, ('row', 'col'), pairs)  13.8 us
    pallas_call x1, Pallas kernels, replicated(): pl.pallas_call(functools.partial(embed_kernel, count, own, vecs, feat), o...  10.8 us
    ppermute x17, waiting for transfers between devices, exchange(): return lax.ppermute(x, ('row', 'col'), pairs)  8.6 us
    pallas_call x1, Pallas kernels, replicated(): pl.pallas_call(functools.partial(pack_kernel, vecs, feat), out_shape=pltp...  0.88 us
  transfers between devices with their start and end apart: 17, of which 7 were waited for; matrix products, arithmetic and copies ran while one was open for 0% of the time, Pallas kernels for 0%

profile of v4, /device:TPU:0, one launch (start us, length us, event | category | flops | bytes accessed | tf_op | source)
XLA Modules:
  0.0 34.2 jit_solution(12409683292221009656)
XLA Ops:
  0.0 0.9 %shard_map.28 = bf16[32,896]{1,0:T(8,128)(2,1)S(1)} custom-call(bf16[32,768]{1,0:T(8,128)(2,1)} %e_ref.1, f32[32,64]{1,0:T(8,128)} %bitcast.2), custom_call_target="tpu_custom_call" | custom-call | tf_op jit(solution)/shard_map/pallas_call | solution.py:149
  0.9 3.0 %collective-permute-start = (bf16[32,896]{1,0:T(8,128)(2,1)S(1)}, bf16[32,896]{1,0:T(8,128)(2,1)S(1)}, u32[]{:S(2)}, u32[]{:S(2)}) collective-permute-start(bf16[32,896]{1,0:T(8,128)(2,1)S(1)} %shard_map.28), channel_id=1, source_target_pairs={{0,8},{1,9},{2,10},{3,11},{4,12},{5,13},{6,14},{7,15},{8,0},{9,1},... | collective-permute-start | bytes 172040 | tf_op jit(solution)/shard_map/ppermute | solution.py:142
  3.9 2.5 %collective-permute-start.3 = (bf16[32,896]{1,0:T(8,128)(2,1)S(1)}, bf16[32,896]{1,0:T(8,128)(2,1)S(1)}, u32[]{:S(2)}, u32[]{:S(2)}) collective-permute-start(bf16[32,896]{1,0:T(8,128)(2,1)S(1)} %shard_map.28), channel_id=1, source_target_pairs={{0,24},{1,25},{2,26},{3,27},{4,28},{5,29},{6,30},{7,31},{8,16},{9,... | collective-permute-start | bytes 172040 | tf_op jit(solution)/shard_map/ppermute | solution.py:142
  6.4 0.1 collective-permute-start.2
  6.5 0.0 collective-permute-done
  6.5 1.6 %collective-permute-start.9 = (bf16[64,896]{1,0:T(8,128)(2,1)S(1)}, bf16[64,896]{1,0:T(8,128)(2,1)S(1)}, u32[]{:S(2)}, u32[]{:S(2)}) collective-permute-start(bf16[64,896]{1,0:T(8,128)(2,1)S(1)} %pad_maximum_fusion.refs_0_), channel_id=1, source_target_pairs={{0,4},{1,5},{2,6},{3,7},{4,0},{5,1},{6,2},{7,3},{8,12},{9,13},{10,... | collective-permute-start | bytes 344072 | tf_op jit(solution)/shard_map/ppermute | solution.py:142
  8.1 1.5 %collective-permute-start.7 = (bf16[64,896]{1,0:T(8,128)(2,1)S(1)}, bf16[64,896]{1,0:T(8,128)(2,1)S(1)}, u32[]{:S(2)}, u32[]{:S(2)}) collective-permute-start(bf16[64,896]{1,0:T(8,128)(2,1)S(1)} %pad_maximum_fusion.refs_0_), channel_id=1, source_target_pairs={{0,2},{1,3},{2,0},{3,1},{4,6},{5,7},{6,4},{7,5},{8,10},{9,11},{10,... | collective-permute-start | bytes 344072 | tf_op jit(solution)/shard_map/ppermute | solution.py:142
  9.6 0.5 %collective-permute-start.5 = (bf16[64,896]{1,0:T(8,128)(2,1)S(1)}, bf16[64,896]{1,0:T(8,128)(2,1)S(1)}, u32[]{:S(2)}, u32[]{:S(2)}) collective-permute-start(bf16[64,896]{1,0:T(8,128)(2,1)S(1)} %pad_maximum_fusion.refs_0_), channel_id=1, source_target_pairs={{0,6},{1,7},{2,4},{3,5},{4,2},{5,3},{6,0},{7,1},{8,14},{9,15},{10,... | collective-permute-start | bytes 344072 | tf_op jit(solution)/shard_map/ppermute | solution.py:142
  10.1 2.1 %collective-permute-done.2 = bf16[32,896]{1,0:T(8,128)(2,1)S(1)} collective-permute-done((bf16[32,896]{1,0:T(8,128)(2,1)S(1)}, bf16[32,896]{1,0:T(8,128)(2,1)S(1)}, u32[]{:S(2)}, u32[]{:S(2)}) %collective-permute-start.2) | collective-permute-done | bytes 57376 | tf_op jit(solution)/shard_map/ppermute | solution.py:142
  12.2 0.0 collective-permute-start.1
  12.2 0.0 collective-permute-done.3
  12.3 1.6 %collective-permute-start.15 = (bf16[64,896]{1,0:T(8,128)(2,1)S(1)}, bf16[64,896]{1,0:T(8,128)(2,1)S(1)}, u32[]{:S(2)}, u32[]{:S(2)}) collective-permute-start(bf16[64,896]{1,0:T(8,128)(2,1)S(1)} %constant_dynamic-update-slice_fusion.refs_2_), channel_id=1, source_target_pairs={{0,4},{1,5},{2,6},{3,7},{4,0},{5,1},{6,2},{7,3},{8,12},{9,13},{10,... | collective-permute-start | bytes 344072 | tf_op jit(solution)/shard_map/ppermute | solution.py:142
  13.8 0.0 collective-permute-done.9.refs_8_
  13.8 1.5 %collective-permute-start.13 = (bf16[64,896]{1,0:T(8,128)(2,1)S(1)}, bf16[64,896]{1,0:T(8,128)(2,1)S(1)}, u32[]{:S(2)}, u32[]{:S(2)}) collective-permute-start(bf16[64,896]{1,0:T(8,128)(2,1)S(1)} %constant_dynamic-update-slice_fusion.refs_2_), channel_id=1, source_target_pairs={{0,2},{1,3},{2,0},{3,1},{4,6},{5,7},{6,4},{7,5},{8,10},{9,11},{10,... | collective-permute-start | bytes 344072 | tf_op jit(solution)/shard_map/ppermute | solution.py:142
  15.3 0.0 collective-permute-done.7.refs_6_
  15.3 0.5 %collective-permute-start.11 = (bf16[64,896]{1,0:T(8,128)(2,1)S(1)}, bf16[64,896]{1,0:T(8,128)(2,1)S(1)}, u32[]{:S(2)}, u32[]{:S(2)}) collective-permute-start(bf16[64,896]{1,0:T(8,128)(2,1)S(1)} %constant_dynamic-update-slice_fusion.refs_2_), channel_id=1, source_target_pairs={{0,6},{1,7},{2,4},{3,5},{4,2},{5,3},{6,0},{7,1},{8,14},{9,15},{10,... | collective-permute-start | bytes 344072 | tf_op jit(solution)/shard_map/ppermute | solution.py:142
  15.8 0.0 collective-permute-done.5.refs_4_
  15.8 0.0 collective-permute-start.4
  15.8 0.0 collective-permute-done.1.refs_1_
  15.8 0.5 %collective-permute-start.10 = (bf16[64,896]{1,0:T(8,128)(2,1)S(1)}, bf16[64,896]{1,0:T(8,128)(2,1)S(1)}, u32[]{:S(2)}, u32[]{:S(2)}) collective-permute-start(bf16[64,896]{1,0:T(8,128)(2,1)S(1)} %collective-permute-done.9.refs_8_), channel_id=1, source_target_pairs={{0,1},{1,0},{2,3},{3,2},{4,5},{5,4},{6,7},{7,6},{8,9},{9,8},{10,11... | collective-permute-start | bytes 344072 | tf_op jit(solution)/shard_map/ppermute | solution.py:142
  16.3 1.5 %collective-permute-done.15.refs_14_ = bf16[64,896]{1,0:T(8,128)(2,1)S(1)} collective-permute-done((bf16[64,896]{1,0:T(8,128)(2,1)S(1)}, bf16[64,896]{1,0:T(8,128)(2,1)S(1)}, u32[]{:S(2)}, u32[]{:S(2)}) %collective-permute-start.15) | collective-permute-done | bytes 114720 | tf_op jit(solution)/shard_map/ppermute | solution.py:142
  17.9 0.0 collective-permute-start.8
  17.9 1.9 %collective-permute-done.13.refs_12_ = bf16[64,896]{1,0:T(8,128)(2,1)S(1)} collective-permute-done((bf16[64,896]{1,0:T(8,128)(2,1)S(1)}, bf16[64,896]{1,0:T(8,128)(2,1)S(1)}, u32[]{:S(2)}, u32[]{:S(2)}) %collective-permute-start.13) | collective-permute-done | bytes 114720 | tf_op jit(solution)/shard_map/ppermute | solution.py:142
  19.8 0.0 collective-permute-start.6
  19.8 1.7 %collective-permute-done.11.refs_10_ = bf16[64,896]{1,0:T(8,128)(2,1)S(1)} collective-permute-done((bf16[64,896]{1,0:T(8,128)(2,1)S(1)}, bf16[64,896]{1,0:T(8,128)(2,1)S(1)}, u32[]{:S(2)}, u32[]{:S(2)}) %collective-permute-start.11) | collective-permute-done | bytes 114720 | tf_op jit(solution)/shard_map/ppermute | solution.py:142
  21.5 0.0 collective-permute-start.16
  21.5 0.0 collective-permute-done.4.refs_3_
  21.5 0.5 %collective-permute-start.14 = (bf16[64,896]{1,0:T(8,128)(2,1)S(1)}, bf16[64,896]{1,0:T(8,128)(2,1)S(1)}, u32[]{:S(2)}, u32[]{:S(2)}) collective-permute-start(bf16[64,896]{1,0:T(8,128)(2,1)S(1)} %collective-permute-done.13.refs_12_), channel_id=1, source_target_pairs={{0,1},{1,0},{2,3},{3,2},{4,5},{5,4},{6,7},{7,6},{8,9},{9,8},{10,11... | collective-permute-start | bytes 344072 | tf_op jit(solution)/shard_map/ppermute | solution.py:142
  22.0 0.0 collective-permute-done.10.refs_9_
  22.0 0.1 collective-permute-start.12
  22.1 0.0 collective-permute-done.8.refs_7_
  22.1 0.0 collective-permute-done.6.refs_5_
  22.1 0.7 %collective-permute-done.16.refs_15_ = bf16[64,896]{1,0:T(8,128)(2,1)S(1)} collective-permute-done((bf16[64,896]{1,0:T(8,128)(2,1)S(1)}, bf16[64,896]{1,0:T(8,128)(2,1)S(1)}, u32[]{:S(2)}, u32[]{:S(2)}) %collective-permute-start.16) | collective-permute-done | bytes 114720 | tf_op jit(solution)/shard_map/ppermute | solution.py:142
  22.8 0.2 collective-permute-done.14.refs_13_
  23.0 0.4 %collective-permute-done.12.refs_11_ = bf16[64,896]{1,0:T(8,128)(2,1)S(1)} collective-permute-done((bf16[64,896]{1,0:T(8,128)(2,1)S(1)}, bf16[64,896]{1,0:T(8,128)(2,1)S(1)}, u32[]{:S(2)}, u32[]{:S(2)}) %collective-permute-start.12) | collective-permute-done | bytes 114720 | tf_op jit(solution)/shard_map/ppermute | solution.py:142
  23.4 10.8 %shard_map.29 = f32[32,64]{1,0:T(8,128)} custom-call(bf16[64,896]{1,0:T(8,128)(2,1)S(1)} %pad_maximum_fusion.refs_0_, bf16[64,896]{1,0:T(8,128)(2,1)S(1)} %collective-permute-done.1.refs_1_, bf16[64,896]{1,0:T(8,128)(2,1)S(1)} %constant_dynamic-update-slice_fusion.refs_2_, bf16[64,896]{1,0:T(8,128)(2,1)S(1)} %collective-permute-done.4.refs_3_, ...), custom_call_target="tpu_custom_call" | custom-call | tf_op jit(solution)/shard_map/pallas_call | solution.py:169
  (3 shorter events, 0.0 us)
Async XLA Ops:
  0.9 5.6 %collective-permute-start = (bf16[32,896]{1,0:T(8,128)(2,1)S(1)}, bf16[32,896]{1,0:T(8,128)(2,1)S(1)}, u32[]{:S(2)}, u32[]{:S(2)}) collective-permute-start(bf16[32,896]{1,0:T(8,128)(2,1)S(1)} %shard_map.28), channel_id=1, source_target_pairs={{0,8},{1,9},{2,10},{3,11},{4,12},{5,13},{6,14},{7,15},{8,0},{9,1},... | collective-permute-start | bytes 172040 | tf_op jit(solution)/shard_map/ppermute | solution.py:142
  3.9 8.3 %collective-permute-start.3 = (bf16[32,896]{1,0:T(8,128)(2,1)S(1)}, bf16[32,896]{1,0:T(8,128)(2,1)S(1)}, u32[]{:S(2)}, u32[]{:S(2)}) collective-permute-start(bf16[32,896]{1,0:T(8,128)(2,1)S(1)} %shard_map.28), channel_id=1, source_target_pairs={{0,24},{1,25},{2,26},{3,27},{4,28},{5,29},{6,30},{7,31},{8,16},{9,... | collective-permute-start | bytes 172040 | tf_op jit(solution)/shard_map/ppermute | solution.py:142
  6.4 5.8 %collective-permute-start.2 = (bf16[32,896]{1,0:T(8,128)(2,1)S(1)}, bf16[32,896]{1,0:T(8,128)(2,1)S(1)}, u32[]{:S(2)}, u32[]{:S(2)}) collective-permute-start(bf16[32,896]{1,0:T(8,128)(2,1)S(1)} %shard_map.28), channel_id=1, source_target_pairs={{0,16},{1,17},{2,18},{3,19},{4,20},{5,21},{6,22},{7,23},{8,24},{9,... | collective-permute-start | bytes 172040 | tf_op jit(solution)/shard_map/ppermute | solution.py:142
  6.5 7.3 %collective-permute-start.9 = (bf16[64,896]{1,0:T(8,128)(2,1)S(1)}, bf16[64,896]{1,0:T(8,128)(2,1)S(1)}, u32[]{:S(2)}, u32[]{:S(2)}) collective-permute-start(bf16[64,896]{1,0:T(8,128)(2,1)S(1)} %pad_maximum_fusion.refs_0_), channel_id=1, source_target_pairs={{0,4},{1,5},{2,6},{3,7},{4,0},{5,1},{6,2},{7,3},{8,12},{9,13},{10,... | collective-permute-start | bytes 344072 | tf_op jit(solution)/shard_map/ppermute | solution.py:142
  8.1 7.2 %collective-permute-start.7 = (bf16[64,896]{1,0:T(8,128)(2,1)S(1)}, bf16[64,896]{1,0:T(8,128)(2,1)S(1)}, u32[]{:S(2)}, u32[]{:S(2)}) collective-permute-start(bf16[64,896]{1,0:T(8,128)(2,1)S(1)} %pad_maximum_fusion.refs_0_), channel_id=1, source_target_pairs={{0,2},{1,3},{2,0},{3,1},{4,6},{5,7},{6,4},{7,5},{8,10},{9,11},{10,... | collective-permute-start | bytes 344072 | tf_op jit(solution)/shard_map/ppermute | solution.py:142
  9.6 6.2 %collective-permute-start.5 = (bf16[64,896]{1,0:T(8,128)(2,1)S(1)}, bf16[64,896]{1,0:T(8,128)(2,1)S(1)}, u32[]{:S(2)}, u32[]{:S(2)}) collective-permute-start(bf16[64,896]{1,0:T(8,128)(2,1)S(1)} %pad_maximum_fusion.refs_0_), channel_id=1, source_target_pairs={{0,6},{1,7},{2,4},{3,5},{4,2},{5,3},{6,0},{7,1},{8,14},{9,15},{10,... | collective-permute-start | bytes 344072 | tf_op jit(solution)/shard_map/ppermute | solution.py:142
  12.2 3.6 %collective-permute-start.1 = (bf16[64,896]{1,0:T(8,128)(2,1)S(1)}, bf16[64,896]{1,0:T(8,128)(2,1)S(1)}, u32[]{:S(2)}, u32[]{:S(2)}) collective-permute-start(bf16[64,896]{1,0:T(8,128)(2,1)S(1)} %pad_maximum_fusion.refs_0_), channel_id=1, source_target_pairs={{0,1},{1,0},{2,3},{3,2},{4,5},{5,4},{6,7},{7,6},{8,9},{9,8},{10,11... | collective-permute-start | bytes 344072 | tf_op jit(solution)/shard_map/ppermute | solution.py:142
  12.3 5.6 %collective-permute-start.15 = (bf16[64,896]{1,0:T(8,128)(2,1)S(1)}, bf16[64,896]{1,0:T(8,128)(2,1)S(1)}, u32[]{:S(2)}, u32[]{:S(2)}) collective-permute-start(bf16[64,896]{1,0:T(8,128)(2,1)S(1)} %constant_dynamic-update-slice_fusion.refs_2_), channel_id=1, source_target_pairs={{0,4},{1,5},{2,6},{3,7},{4,0},{5,1},{6,2},{7,3},{8,12},{9,13},{10,... | collective-permute-start | bytes 344072 | tf_op jit(solution)/shard_map/ppermute | solution.py:142
  13.8 6.0 %collective-permute-start.13 = (bf16[64,896]{1,0:T(8,128)(2,1)S(1)}, bf16[64,896]{1,0:T(8,128)(2,1)S(1)}, u32[]{:S(2)}, u32[]{:S(2)}) collective-permute-start(bf16[64,896]{1,0:T(8,128)(2,1)S(1)} %constant_dynamic-update-slice_fusion.refs_2_), channel_id=1, source_target_pairs={{0,2},{1,3},{2,0},{3,1},{4,6},{5,7},{6,4},{7,5},{8,10},{9,11},{10,... | collective-permute-start | bytes 344072 | tf_op jit(solution)/shard_map/ppermute | solution.py:142
  15.3 6.2 %collective-permute-start.11 = (bf16[64,896]{1,0:T(8,128)(2,1)S(1)}, bf16[64,896]{1,0:T(8,128)(2,1)S(1)}, u32[]{:S(2)}, u32[]{:S(2)}) collective-permute-start(bf16[64,896]{1,0:T(8,128)(2,1)S(1)} %constant_dynamic-update-slice_fusion.refs_2_), channel_id=1, source_target_pairs={{0,6},{1,7},{2,4},{3,5},{4,2},{5,3},{6,0},{7,1},{8,14},{9,15},{10,... | collective-permute-start | bytes 344072 | tf_op jit(solution)/shard_map/ppermute | solution.py:142
  15.8 5.7 %collective-permute-start.4 = (bf16[64,896]{1,0:T(8,128)(2,1)S(1)}, bf16[64,896]{1,0:T(8,128)(2,1)S(1)}, u32[]{:S(2)}, u32[]{:S(2)}) collective-permute-start(bf16[64,896]{1,0:T(8,128)(2,1)S(1)} %constant_dynamic-update-slice_fusion.refs_2_), channel_id=1, source_target_pairs={{0,1},{1,0},{2,3},{3,2},{4,5},{5,4},{6,7},{7,6},{8,9},{9,8},{10,11... | collective-permute-start | bytes 344072 | tf_op jit(solution)/shard_map/ppermute | solution.py:142
  15.8 6.2 %collective-permute-start.10 = (bf16[64,896]{1,0:T(8,128)(2,1)S(1)}, bf16[64,896]{1,0:T(8,128)(2,1)S(1)}, u32[]{:S(2)}, u32[]{:S(2)}) collective-permute-start(bf16[64,896]{1,0:T(8,128)(2,1)S(1)} %collective-permute-done.9.refs_8_), channel_id=1, source_target_pairs={{0,1},{1,0},{2,3},{3,2},{4,5},{5,4},{6,7},{7,6},{8,9},{9,8},{10,11... | collective-permute-start | bytes 344072 | tf_op jit(solution)/shard_map/ppermute | solution.py:142
  17.9 4.2 %collective-permute-start.8 = (bf16[64,896]{1,0:T(8,128)(2,1)S(1)}, bf16[64,896]{1,0:T(8,128)(2,1)S(1)}, u32[]{:S(2)}, u32[]{:S(2)}) collective-permute-start(bf16[64,896]{1,0:T(8,128)(2,1)S(1)} %collective-permute-done.7.refs_6_), channel_id=1, source_target_pairs={{0,1},{1,0},{2,3},{3,2},{4,5},{5,4},{6,7},{7,6},{8,9},{9,8},{10,11... | collective-permute-start | bytes 344072 | tf_op jit(solution)/shard_map/ppermute | solution.py:142
  19.8 2.3 %collective-permute-start.6 = (bf16[64,896]{1,0:T(8,128)(2,1)S(1)}, bf16[64,896]{1,0:T(8,128)(2,1)S(1)}, u32[]{:S(2)}, u32[]{:S(2)}) collective-permute-start(bf16[64,896]{1,0:T(8,128)(2,1)S(1)} %collective-permute-done.5.refs_4_), channel_id=1, source_target_pairs={{0,1},{1,0},{2,3},{3,2},{4,5},{5,4},{6,7},{7,6},{8,9},{9,8},{10,11... | collective-permute-start | bytes 344072 | tf_op jit(solution)/shard_map/ppermute | solution.py:142
  21.5 1.3 %collective-permute-start.16 = (bf16[64,896]{1,0:T(8,128)(2,1)S(1)}, bf16[64,896]{1,0:T(8,128)(2,1)S(1)}, u32[]{:S(2)}, u32[]{:S(2)}) collective-permute-start(bf16[64,896]{1,0:T(8,128)(2,1)S(1)} %collective-permute-done.15.refs_14_), channel_id=1, source_target_pairs={{0,1},{1,0},{2,3},{3,2},{4,5},{5,4},{6,7},{7,6},{8,9},{9,8},{10,11... | collective-permute-start | bytes 344072 | tf_op jit(solution)/shard_map/ppermute | solution.py:142
  21.5 1.5 %collective-permute-start.14 = (bf16[64,896]{1,0:T(8,128)(2,1)S(1)}, bf16[64,896]{1,0:T(8,128)(2,1)S(1)}, u32[]{:S(2)}, u32[]{:S(2)}) collective-permute-start(bf16[64,896]{1,0:T(8,128)(2,1)S(1)} %collective-permute-done.13.refs_12_), channel_id=1, source_target_pairs={{0,1},{1,0},{2,3},{3,2},{4,5},{5,4},{6,7},{7,6},{8,9},{9,8},{10,11... | collective-permute-start | bytes 344072 | tf_op jit(solution)/shard_map/ppermute | solution.py:142
  22.0 1.3 %collective-permute-start.12 = (bf16[64,896]{1,0:T(8,128)(2,1)S(1)}, bf16[64,896]{1,0:T(8,128)(2,1)S(1)}, u32[]{:S(2)}, u32[]{:S(2)}) collective-permute-start(bf16[64,896]{1,0:T(8,128)(2,1)S(1)} %collective-permute-done.11.refs_10_), channel_id=1, source_target_pairs={{0,1},{1,0},{2,3},{3,2},{4,5},{5,4},{6,7},{7,6},{8,9},{9,8},{10,11... | collective-permute-start | bytes 344072 | tf_op jit(solution)/shard_map/ppermute | solution.py:142

commit v5 on v4

--- a/solution.py
+++ b/solution.py
@@ -152,18 +152,25 @@
         in_specs=[pl.BlockSpec(memory_space=pltpu.VMEM)] * 2,
         out_specs=pl.BlockSpec(memory_space=pltpu.VMEM),
     )(embeddings, start_block.T)
-    first = lambda r, c: (r, c ^ 2) if c & 1 else (r ^ 1, c)
-    second = lambda r, c: (r ^ 1, c) if c & 1 else (r, c ^ 2)
-    swap = lambda r, c: (r, c ^ 1)
-    along_z = [send(mine, partner=lambda r, c, d=d: (r ^ (2 * d), c)) for d in (1, 2, 3)]
-    px, py, pxy = (lambda r, c: (r, c ^ 2)), (lambda r, c: (r ^ 1, c)), (lambda r, c: (r ^ 1, c ^ 2))
-    near = jnp.concatenate([mine, along_z[0]], axis=0)
-    far = jnp.concatenate(along_z[1:], axis=0)
-    pieces = [near, send(near, partner=swap), far, send(far, partner=swap)]
-    for piece in (near, far):
-        for p in (pxy, px, py):
-            got = send(piece, partner=p)
-            pieces += [got, send(got, partner=swap)]
+    along_x, along_y = (lambda r, c: (r, c ^ 2)), (lambda r, c: (r ^ 1, c))
+    diagonal, swap = (lambda r, c: (r ^ 1, c ^ 2)), (lambda r, c: (r, c ^ 1))
+    along_z = lambda d: lambda r, c: (r ^ (2 * d), c)
+    farther = [send(mine, partner=along_z(d)) for d in (2, 3)]
+    beside = send(mine, partner=along_z(1))
+    own_x = send(mine, partner=along_x)
+    own_y = send(mine, partner=along_y)
+    own_d = send(mine, partner=diagonal)
+    own_y, *farther = lax.optimization_barrier((own_y, *farther))
+    far = jnp.concatenate(farther, axis=0)
+    far_y = send(far, partner=along_y)
+    far_d = send(far, partner=diagonal)
+    far_x = send(far, partner=along_x)
+    plane = jnp.concatenate([own_x, own_y, own_d], axis=0)
+    beside_plane = send(plane, partner=along_z(1))
+    near = jnp.concatenate([mine, plane], axis=0)
+    pieces = []
+    for piece in (near, beside, beside_plane, far, far_y, far_d, far_x):
+        pieces += [piece, send(piece, partner=swap)]
     count = len(pieces)
     points = sum(piece.shape[0] for piece in pieces)
     return pl.pallas_call(

time: 34.4 us -> 33.1 us (0.962)
  waiting for transfers between devices: 8.6 us -> 5.51 us
  starting transfers between devices: 13.8 us -> 15.6 us
    ppermute x17, waiting for transfers between devices: 8.6 us -> 5.51 us  [exchange(): return lax.ppermute(x, ('row', 'col'), pairs)]
    ppermute x17, starting transfers between devices: 13.8 us -> 15.6 us  [exchange(): return lax.ppermute(x, ('row', 'col'), pairs)]
  transfers between devices with their start and end apart: 17 -> 17, of which waited for: 7 -> 6; matrix products, arithmetic and copies ran while one was open for 0% -> 0% of each run, Pallas kernels for 0% -> 0%
where the time goes in v5:
time: 33.1 us; the launch traced here: 33 us
  starting transfers between devices  15.6 us (47%)
  Pallas kernels  11.8 us (36%)
  waiting for transfers between devices  5.51 us (17%)
    ppermute x17, starting transfers between devices, exchange(): return lax.ppermute(x, ('row', 'col'), pairs)  15.6 us
    pallas_call x1, Pallas kernels, replicated(): pl.pallas_call(functools.partial(embed_kernel, count, own, vecs, feat), o...  10.9 us
    ppermute x17, waiting for transfers between devices, exchange(): return lax.ppermute(x, ('row', 'col'), pairs)  5.51 us
    pallas_call x1, Pallas kernels, replicated(): pl.pallas_call(functools.partial(pack_kernel, vecs, feat), out_shape=pltp...  0.88 us
  transfers between devices with their start and end apart: 17, of which 6 were waited for; matrix products, arithmetic and copies ran while one was open for 0% of the time, Pallas kernels for 0%

profile of v5, /device:TPU:0, one launch (start us, length us, event | category | flops | bytes accessed | tf_op | source)
XLA Modules:
  0.0 33.0 jit_solution(10068003923027323490)
XLA Ops:
  0.0 0.9 %shard_map.28 = bf16[32,896]{1,0:T(8,128)(2,1)S(1)} custom-call(bf16[32,768]{1,0:T(8,128)(2,1)} %e_ref.1, f32[32,64]{1,0:T(8,128)} %bitcast.2), custom_call_target="tpu_custom_call" | custom-call | tf_op jit(solution)/shard_map/pallas_call | solution.py:149
  0.9 5.1 %collective-permute-start.3 = (bf16[32,896]{1,0:T(8,128)(2,1)S(1)}, bf16[32,896]{1,0:T(8,128)(2,1)S(1)}, u32[]{:S(2)}, u32[]{:S(2)}) collective-permute-start(bf16[32,896]{1,0:T(8,128)(2,1)S(1)} %shard_map.28), channel_id=1, source_target_pairs={{0,24},{1,25},{2,26},{3,27},{4,28},{5,29},{6,30},{7,31},{8,16},{9,... | collective-permute-start | bytes 172040 | tf_op jit(solution)/shard_map/ppermute | solution.py:142
  5.9 0.0 collective-permute-start.2
  5.9 1.5 %collective-permute-start.1 = (bf16[32,896]{1,0:T(8,128)(2,1)S(1)}, bf16[32,896]{1,0:T(8,128)(2,1)S(1)}, u32[]{:S(2)}, u32[]{:S(2)}) collective-permute-start(bf16[32,896]{1,0:T(8,128)(2,1)S(1)} %shard_map.28), channel_id=1, source_target_pairs={{0,4},{1,5},{2,6},{3,7},{4,0},{5,1},{6,2},{7,3},{8,12},{9,13},{10,... | collective-permute-start | bytes 172040 | tf_op jit(solution)/shard_map/ppermute | solution.py:142
  7.5 0.8 %collective-permute-start.6 = (bf16[32,896]{1,0:T(8,128)(2,1)S(1)}, bf16[32,896]{1,0:T(8,128)(2,1)S(1)}, u32[]{:S(2)}, u32[]{:S(2)}) collective-permute-start(bf16[32,896]{1,0:T(8,128)(2,1)S(1)} %shard_map.28), channel_id=1, source_target_pairs={{0,8},{1,9},{2,10},{3,11},{4,12},{5,13},{6,14},{7,15},{8,0},{9,1},... | collective-permute-start | bytes 172040 | tf_op jit(solution)/shard_map/ppermute | solution.py:142
  8.2 1.4 %collective-permute-start.4 = (bf16[32,896]{1,0:T(8,128)(2,1)S(1)}, bf16[32,896]{1,0:T(8,128)(2,1)S(1)}, u32[]{:S(2)}, u32[]{:S(2)}) collective-permute-start(bf16[32,896]{1,0:T(8,128)(2,1)S(1)} %shard_map.28), channel_id=1, source_target_pairs={{0,6},{1,7},{2,4},{3,5},{4,2},{5,3},{6,0},{7,1},{8,14},{9,15},{10,... | collective-permute-start | bytes 172040 | tf_op jit(solution)/shard_map/ppermute | solution.py:142
  9.7 0.0 collective-permute-done.3
  9.7 0.5 %collective-permute-start = (bf16[32,896]{1,0:T(8,128)(2,1)S(1)}, bf16[32,896]{1,0:T(8,128)(2,1)S(1)}, u32[]{:S(2)}, u32[]{:S(2)}) collective-permute-start(bf16[32,896]{1,0:T(8,128)(2,1)S(1)} %shard_map.28), channel_id=1, source_target_pairs={{0,2},{1,3},{2,0},{3,1},{4,6},{5,7},{6,4},{7,5},{8,10},{9,11},{10,... | collective-permute-start | bytes 172040 | tf_op jit(solution)/shard_map/ppermute | solution.py:142
  10.2 0.8 %collective-permute-done.2 = bf16[32,896]{1,0:T(8,128)(2,1)S(1)} collective-permute-done((bf16[32,896]{1,0:T(8,128)(2,1)S(1)}, bf16[32,896]{1,0:T(8,128)(2,1)S(1)}, u32[]{:S(2)}, u32[]{:S(2)}) %collective-permute-start.2) | collective-permute-done | bytes 57376 | tf_op jit(solution)/shard_map/ppermute | solution.py:142
  11.0 0.0 collective-permute-done.1
  11.0 1.6 %collective-permute-start.15 = (bf16[64,896]{1,0:T(8,128)(2,1)S(1)}, bf16[64,896]{1,0:T(8,128)(2,1)S(1)}, u32[]{:S(2)}, u32[]{:S(2)}) collective-permute-start(bf16[64,896]{1,0:T(8,128)(2,1)S(1)} %constant_dynamic-update-slice_fusion.refs_6_), channel_id=1, source_target_pairs={{0,2},{1,3},{2,0},{3,1},{4,6},{5,7},{6,4},{7,5},{8,10},{9,11},{10,... | collective-permute-start | bytes 344072 | tf_op jit(solution)/shard_map/ppermute | solution.py:142
  12.6 1.6 %collective-permute-start.13 = (bf16[64,896]{1,0:T(8,128)(2,1)S(1)}, bf16[64,896]{1,0:T(8,128)(2,1)S(1)}, u32[]{:S(2)}, u32[]{:S(2)}) collective-permute-start(bf16[64,896]{1,0:T(8,128)(2,1)S(1)} %constant_dynamic-update-slice_fusion.refs_6_), channel_id=1, source_target_pairs={{0,6},{1,7},{2,4},{3,5},{4,2},{5,3},{6,0},{7,1},{8,14},{9,15},{10,... | collective-permute-start | bytes 344072 | tf_op jit(solution)/shard_map/ppermute | solution.py:142
  14.1 0.0 collective-permute-done.4
  14.1 0.4 %collective-permute-start.11 = (bf16[64,896]{1,0:T(8,128)(2,1)S(1)}, bf16[64,896]{1,0:T(8,128)(2,1)S(1)}, u32[]{:S(2)}, u32[]{:S(2)}) collective-permute-start(bf16[64,896]{1,0:T(8,128)(2,1)S(1)} %constant_dynamic-update-slice_fusion.refs_6_), channel_id=1, source_target_pairs={{0,4},{1,5},{2,6},{3,7},{4,0},{5,1},{6,2},{7,3},{8,12},{9,13},{10,... | collective-permute-start | bytes 344072 | tf_op jit(solution)/shard_map/ppermute | solution.py:142
  14.6 0.0 collective-permute-done
  14.6 1.2 %collective-permute-start.8 = (bf16[96,896]{1,0:T(8,128)(2,1)S(1)}, bf16[96,896]{1,0:T(8,128)(2,1)S(1)}, u32[]{:S(2)}, u32[]{:S(2)}) collective-permute-start(bf16[96,896]{1,0:T(8,128)(2,1)S(1)} %pad_maximum_fusion.1), channel_id=1, source_target_pairs={{0,8},{1,9},{2,10},{3,11},{4,12},{5,13},{6,14},{7,15},{8,0},{9,1},... | collective-permute-start | bytes 516104 | tf_op jit(solution)/shard_map/ppermute | solution.py:142
  15.9 0.0 collective-permute-done.6.refs_2_
  15.9 0.0 collective-permute-start.7
  15.9 1.2 %collective-permute-done.7.refs_3_ = bf16[32,896]{1,0:T(8,128)(2,1)S(1)} collective-permute-done((bf16[32,896]{1,0:T(8,128)(2,1)S(1)}, bf16[32,896]{1,0:T(8,128)(2,1)S(1)}, u32[]{:S(2)}, u32[]{:S(2)}) %collective-permute-start.7) | collective-permute-done | bytes 57376 | tf_op jit(solution)/shard_map/ppermute | solution.py:142
  17.1 0.2 collective-permute-start.10
  17.3 0.0 collective-permute-done.15.refs_12_
  17.3 0.4 %collective-permute-start.5 = (bf16[128,896]{1,0:T(8,128)(2,1)S(1)}, bf16[128,896]{1,0:T(8,128)(2,1)S(1)}, u32[]{:S(2)}, u32[]{:S(2)}) collective-permute-start(bf16[128,896]{1,0:T(8,128)(2,1)S(1)} %pad_maximum_fusion.refs_0_), channel_id=1, source_target_pairs={{0,1},{1,0},{2,3},{3,2},{4,5},{5,4},{6,7},{7,6},{8,9},{9,8},{10,11... | collective-permute-start | bytes 688136 | tf_op jit(solution)/shard_map/ppermute | solution.py:142
  17.6 2.5 %collective-permute-done.8.refs_4_ = bf16[96,896]{1,0:T(8,128)(2,1)S(1)} collective-permute-done((bf16[96,896]{1,0:T(8,128)(2,1)S(1)}, bf16[96,896]{1,0:T(8,128)(2,1)S(1)}, u32[]{:S(2)}, u32[]{:S(2)}) %collective-permute-start.8) | collective-permute-done | bytes 172064 | tf_op jit(solution)/shard_map/ppermute | solution.py:142
  20.1 0.0 collective-permute-start.9
  20.1 0.0 collective-permute-done.13.refs_10_
  20.1 0.5 %collective-permute-start.16 = (bf16[64,896]{1,0:T(8,128)(2,1)S(1)}, bf16[64,896]{1,0:T(8,128)(2,1)S(1)}, u32[]{:S(2)}, u32[]{:S(2)}) collective-permute-start(bf16[64,896]{1,0:T(8,128)(2,1)S(1)} %collective-permute-done.15.refs_12_), channel_id=1, source_target_pairs={{0,1},{1,0},{2,3},{3,2},{4,5},{5,4},{6,7},{7,6},{8,9},{9,8},{10,11... | collective-permute-start | bytes 344072 | tf_op jit(solution)/shard_map/ppermute | solution.py:142
  20.6 0.0 collective-permute-done.11.refs_8_
  20.6 0.1 collective-permute-start.14
  20.7 0.0 collective-permute-done.10.refs_7_
  20.7 0.4 %collective-permute-start.12 = (bf16[64,896]{1,0:T(8,128)(2,1)S(1)}, bf16[64,896]{1,0:T(8,128)(2,1)S(1)}, u32[]{:S(2)}, u32[]{:S(2)}) collective-permute-start(bf16[64,896]{1,0:T(8,128)(2,1)S(1)} %collective-permute-done.11.refs_8_), channel_id=1, source_target_pairs={{0,1},{1,0},{2,3},{3,2},{4,5},{5,4},{6,7},{7,6},{8,9},{9,8},{10,11... | collective-permute-start | bytes 344072 | tf_op jit(solution)/shard_map/ppermute | solution.py:142
  21.1 0.5 %collective-permute-done.16.refs_13_ = bf16[64,896]{1,0:T(8,128)(2,1)S(1)} collective-permute-done((bf16[64,896]{1,0:T(8,128)(2,1)S(1)}, bf16[64,896]{1,0:T(8,128)(2,1)S(1)}, u32[]{:S(2)}, u32[]{:S(2)}) %collective-permute-start.16) | collective-permute-done | bytes 114720 | tf_op jit(solution)/shard_map/ppermute | solution.py:142
  21.7 0.3 collective-permute-done.14.refs_11_
  21.9 0.2 collective-permute-done.12.refs_9_
  22.1 0.0 collective-permute-done.5.refs_1_
  22.1 0.0 collective-permute-done.9.refs_5_
  22.1 10.9 %shard_map.29 = f32[32,64]{1,0:T(8,128)} custom-call(bf16[128,896]{1,0:T(8,128)(2,1)S(1)} %pad_maximum_fusion.refs_0_, bf16[128,896]{1,0:T(8,128)(2,1)S(1)} %collective-permute-done.5.refs_1_, bf16[32,896]{1,0:T(8,128)(2,1)S(1)} %collective-permute-done.6.refs_2_, bf16[32,896]{1,0:T(8,128)(2,1)S(1)} %collective-permute-done.7.refs_3_, ...), custom_call_target="tpu_custom_call" | custom-call | tf_op jit(solution)/shard_map/pallas_call | solution.py:176
  (4 shorter events, 0.1 us)
Async XLA Ops:
  0.9 8.8 %collective-permute-start.3 = (bf16[32,896]{1,0:T(8,128)(2,1)S(1)}, bf16[32,896]{1,0:T(8,128)(2,1)S(1)}, u32[]{:S(2)}, u32[]{:S(2)}) collective-permute-start(bf16[32,896]{1,0:T(8,128)(2,1)S(1)} %shard_map.28), channel_id=1, source_target_pairs={{0,24},{1,25},{2,26},{3,27},{4,28},{5,29},{6,30},{7,31},{8,16},{9,... | collective-permute-start | bytes 172040 | tf_op jit(solution)/shard_map/ppermute | solution.py:142
  5.9 5.1 %collective-permute-start.2 = (bf16[32,896]{1,0:T(8,128)(2,1)S(1)}, bf16[32,896]{1,0:T(8,128)(2,1)S(1)}, u32[]{:S(2)}, u32[]{:S(2)}) collective-permute-start(bf16[32,896]{1,0:T(8,128)(2,1)S(1)} %shard_map.28), channel_id=1, source_target_pairs={{0,16},{1,17},{2,18},{3,19},{4,20},{5,21},{6,22},{7,23},{8,24},{9,... | collective-permute-start | bytes 172040 | tf_op jit(solution)/shard_map/ppermute | solution.py:142
  5.9 5.1 %collective-permute-start.1 = (bf16[32,896]{1,0:T(8,128)(2,1)S(1)}, bf16[32,896]{1,0:T(8,128)(2,1)S(1)}, u32[]{:S(2)}, u32[]{:S(2)}) collective-permute-start(bf16[32,896]{1,0:T(8,128)(2,1)S(1)} %shard_map.28), channel_id=1, source_target_pairs={{0,4},{1,5},{2,6},{3,7},{4,0},{5,1},{6,2},{7,3},{8,12},{9,13},{10,... | collective-permute-start | bytes 172040 | tf_op jit(solution)/shard_map/ppermute | solution.py:142
  7.5 8.4 %collective-permute-start.6 = (bf16[32,896]{1,0:T(8,128)(2,1)S(1)}, bf16[32,896]{1,0:T(8,128)(2,1)S(1)}, u32[]{:S(2)}, u32[]{:S(2)}) collective-permute-start(bf16[32,896]{1,0:T(8,128)(2,1)S(1)} %shard_map.28), channel_id=1, source_target_pairs={{0,8},{1,9},{2,10},{3,11},{4,12},{5,13},{6,14},{7,15},{8,0},{9,1},... | collective-permute-start | bytes 172040 | tf_op jit(solution)/shard_map/ppermute | solution.py:142
  8.2 5.9 %collective-permute-start.4 = (bf16[32,896]{1,0:T(8,128)(2,1)S(1)}, bf16[32,896]{1,0:T(8,128)(2,1)S(1)}, u32[]{:S(2)}, u32[]{:S(2)}) collective-permute-start(bf16[32,896]{1,0:T(8,128)(2,1)S(1)} %shard_map.28), channel_id=1, source_target_pairs={{0,6},{1,7},{2,4},{3,5},{4,2},{5,3},{6,0},{7,1},{8,14},{9,15},{10,... | collective-permute-start | bytes 172040 | tf_op jit(solution)/shard_map/ppermute | solution.py:142
  9.7 4.9 %collective-permute-start = (bf16[32,896]{1,0:T(8,128)(2,1)S(1)}, bf16[32,896]{1,0:T(8,128)(2,1)S(1)}, u32[]{:S(2)}, u32[]{:S(2)}) collective-permute-start(bf16[32,896]{1,0:T(8,128)(2,1)S(1)} %shard_map.28), channel_id=1, source_target_pairs={{0,2},{1,3},{2,0},{3,1},{4,6},{5,7},{6,4},{7,5},{8,10},{9,11},{10,... | collective-permute-start | bytes 172040 | tf_op jit(solution)/shard_map/ppermute | solution.py:142
  11.0 6.2 %collective-permute-start.15 = (bf16[64,896]{1,0:T(8,128)(2,1)S(1)}, bf16[64,896]{1,0:T(8,128)(2,1)S(1)}, u32[]{:S(2)}, u32[]{:S(2)}) collective-permute-start(bf16[64,896]{1,0:T(8,128)(2,1)S(1)} %constant_dynamic-update-slice_fusion.refs_6_), channel_id=1, source_target_pairs={{0,2},{1,3},{2,0},{3,1},{4,6},{5,7},{6,4},{7,5},{8,10},{9,11},{10,... | collective-permute-start | bytes 344072 | tf_op jit(solution)/shard_map/ppermute | solution.py:142
  12.6 7.5 %collective-permute-start.13 = (bf16[64,896]{1,0:T(8,128)(2,1)S(1)}, bf16[64,896]{1,0:T(8,128)(2,1)S(1)}, u32[]{:S(2)}, u32[]{:S(2)}) collective-permute-start(bf16[64,896]{1,0:T(8,128)(2,1)S(1)} %constant_dynamic-update-slice_fusion.refs_6_), channel_id=1, source_target_pairs={{0,6},{1,7},{2,4},{3,5},{4,2},{5,3},{6,0},{7,1},{8,14},{9,15},{10,... | collective-permute-start | bytes 344072 | tf_op jit(solution)/shard_map/ppermute | solution.py:142
  14.1 6.5 %collective-permute-start.11 = (bf16[64,896]{1,0:T(8,128)(2,1)S(1)}, bf16[64,896]{1,0:T(8,128)(2,1)S(1)}, u32[]{:S(2)}, u32[]{:S(2)}) collective-permute-start(bf16[64,896]{1,0:T(8,128)(2,1)S(1)} %constant_dynamic-update-slice_fusion.refs_6_), channel_id=1, source_target_pairs={{0,4},{1,5},{2,6},{3,7},{4,0},{5,1},{6,2},{7,3},{8,12},{9,13},{10,... | collective-permute-start | bytes 344072 | tf_op jit(solution)/shard_map/ppermute | solution.py:142
  14.6 5.5 %collective-permute-start.8 = (bf16[96,896]{1,0:T(8,128)(2,1)S(1)}, bf16[96,896]{1,0:T(8,128)(2,1)S(1)}, u32[]{:S(2)}, u32[]{:S(2)}) collective-permute-start(bf16[96,896]{1,0:T(8,128)(2,1)S(1)} %pad_maximum_fusion.1), channel_id=1, source_target_pairs={{0,8},{1,9},{2,10},{3,11},{4,12},{5,13},{6,14},{7,15},{8,0},{9,1},... | collective-permute-start | bytes 516104 | tf_op jit(solution)/shard_map/ppermute | solution.py:142
  15.9 1.2 %collective-permute-start.7 = (bf16[32,896]{1,0:T(8,128)(2,1)S(1)}, bf16[32,896]{1,0:T(8,128)(2,1)S(1)}, u32[]{:S(2)}, u32[]{:S(2)}) collective-permute-start(bf16[32,896]{1,0:T(8,128)(2,1)S(1)} %collective-permute-done.6.refs_2_), channel_id=1, source_target_pairs={{0,1},{1,0},{2,3},{3,2},{4,5},{5,4},{6,7},{7,6},{8,9},{9,8},{10,11... | collective-permute-start | bytes 172040 | tf_op jit(solution)/shard_map/ppermute | solution.py:142
  17.1 3.6 %collective-permute-start.10 = (bf16[64,896]{1,0:T(8,128)(2,1)S(1)}, bf16[64,896]{1,0:T(8,128)(2,1)S(1)}, u32[]{:S(2)}, u32[]{:S(2)}) collective-permute-start(bf16[64,896]{1,0:T(8,128)(2,1)S(1)} %constant_dynamic-update-slice_fusion.refs_6_), channel_id=1, source_target_pairs={{0,1},{1,0},{2,3},{3,2},{4,5},{5,4},{6,7},{7,6},{8,9},{9,8},{10,11... | collective-permute-start | bytes 344072 | tf_op jit(solution)/shard_map/ppermute | solution.py:142
  17.3 4.8 %collective-permute-start.5 = (bf16[128,896]{1,0:T(8,128)(2,1)S(1)}, bf16[128,896]{1,0:T(8,128)(2,1)S(1)}, u32[]{:S(2)}, u32[]{:S(2)}) collective-permute-start(bf16[128,896]{1,0:T(8,128)(2,1)S(1)} %pad_maximum_fusion.refs_0_), channel_id=1, source_target_pairs={{0,1},{1,0},{2,3},{3,2},{4,5},{5,4},{6,7},{7,6},{8,9},{9,8},{10,11... | collective-permute-start | bytes 688136 | tf_op jit(solution)/shard_map/ppermute | solution.py:142
  20.1 2.0 %collective-permute-start.9 = (bf16[96,896]{1,0:T(8,128)(2,1)S(1)}, bf16[96,896]{1,0:T(8,128)(2,1)S(1)}, u32[]{:S(2)}, u32[]{:S(2)}) collective-permute-start(bf16[96,896]{1,0:T(8,128)(2,1)S(1)} %collective-permute-done.8.refs_4_), channel_id=1, source_target_pairs={{0,1},{1,0},{2,3},{3,2},{4,5},{5,4},{6,7},{7,6},{8,9},{9,8},{10,11... | collective-permute-start | bytes 516104 | tf_op jit(solution)/shard_map/ppermute | solution.py:142
  20.1 1.6 %collective-permute-start.16 = (bf16[64,896]{1,0:T(8,128)(2,1)S(1)}, bf16[64,896]{1,0:T(8,128)(2,1)S(1)}, u32[]{:S(2)}, u32[]{:S(2)}) collective-permute-start(bf16[64,896]{1,0:T(8,128)(2,1)S(1)} %collective-permute-done.15.refs_12_), channel_id=1, source_target_pairs={{0,1},{1,0},{2,3},{3,2},{4,5},{5,4},{6,7},{7,6},{8,9},{9,8},{10,11... | collective-permute-start | bytes 344072 | tf_op jit(solution)/shard_map/ppermute | solution.py:142
  20.6 1.3 %collective-permute-start.14 = (bf16[64,896]{1,0:T(8,128)(2,1)S(1)}, bf16[64,896]{1,0:T(8,128)(2,1)S(1)}, u32[]{:S(2)}, u32[]{:S(2)}) collective-permute-start(bf16[64,896]{1,0:T(8,128)(2,1)S(1)} %collective-permute-done.13.refs_10_), channel_id=1, source_target_pairs={{0,1},{1,0},{2,3},{3,2},{4,5},{5,4},{6,7},{7,6},{8,9},{9,8},{10,11... | collective-permute-start | bytes 344072 | tf_op jit(solution)/shard_map/ppermute | solution.py:142
  20.7 1.4 %collective-permute-start.12 = (bf16[64,896]{1,0:T(8,128)(2,1)S(1)}, bf16[64,896]{1,0:T(8,128)(2,1)S(1)}, u32[]{:S(2)}, u32[]{:S(2)}) collective-permute-start(bf16[64,896]{1,0:T(8,128)(2,1)S(1)} %collective-permute-done.11.refs_8_), channel_id=1, source_target_pairs={{0,1},{1,0},{2,3},{3,2},{4,5},{5,4},{6,7},{7,6},{8,9},{9,8},{10,11... | collective-permute-start | bytes 344072 | tf_op jit(solution)/shard_map/ppermute | solution.py:142

commit v6 on v5

--- a/solution.py
+++ b/solution.py
@@ -27,24 +27,30 @@
     count = len(tiles)
     sub = lax.broadcasted_iota(jnp.int32, tiles[0].shape, 0)
     pivots = [None] * count
-    ahead = [lane_splat(tiles[0], j) for j in range(8)]
+    ahead = [[lane_splat(tiles[k], j) for j in range(8)] for k in range(2)]
     for b in range(count):
-        columns = [[ahead[j]] + [lane_splat(tiles[t], 8 * b + j) for t in range(b + 1, count)] for j in range(8)]
-        if b + 1 < count:
-            ahead = [lane_splat(tiles[b + 1], 8 * (b + 1) + j) for j in range(8)]
+        held = len(ahead)
+        columns = [[a[j] for a in ahead] + [lane_splat(tiles[t], 8 * b + j) for t in range(b + held, count)] for j in range(8)]
+        ahead = [[lane_splat(tiles[t], 8 * (b + 1) + j) for j in range(8)] for t in range(b + 1, min(b + 3, count))]
         factors, rows = [], []
+        pivot = row_splat(columns[0][0], 0)
         for j in range(8):
-            pivot = row_splat(columns[j][0], j)
             q = pltpu.reciprocal(pivot, approx=True)
+            if j < 7:
+                below = row_splat(columns[j][0], j + 1)
+                coming = row_splat(columns[j + 1][0], j + 1) - below * below * q
             m = [d * q for d in columns[j]]
             for l in range(j + 1, 8):
                 head = row_splat(columns[l][0], j)
                 columns[l] = [d - f * head for d, f in zip(columns[l], m)]
-            if b + 1 < count:
-                ahead = [d - m[1] * row_splat(columns[j][1], l) for l, d in enumerate(ahead)]
+            if ahead:
+                heads = [row_splat(columns[j][1], l) for l in range(8)]
+                ahead = [[d - m[1 + k] * h for d, h in zip(a, heads)] for k, a in enumerate(ahead)]
             row = row_splat(tiles[b], j)
             tiles[b] = tiles[b] - jnp.where(sub > j, m[0], 0.0) * row
             pivots[b] = pivot if j == 0 else jnp.where(sub >= j, pivot, pivots[b])
+            if j < 7:
+                pivot = coming
             factors.append(m)
             rows.append(row)
         for t in range(b + 1, count):

time: 33.1 us -> 32.5 us (0.982)
  Pallas kernels: 11.8 us -> 11.1 us
    pallas_call x1, Pallas kernels: 10.9 us -> 10.2 us  [replicated(): pl.pallas_call(functools.partial(embed_kernel, count, own, vecs, feat), o...]
where the time goes in v6:
time: 32.5 us; the launch traced here: 32.3 us
  starting transfers between devices  15.6 us (48%)
  Pallas kernels  11.1 us (34%)
  waiting for transfers between devices  5.51 us (17%)
    ppermute x17, starting transfers between devices, exchange(): return lax.ppermute(x, ('row', 'col'), pairs)  15.6 us
    pallas_call x1, Pallas kernels, replicated(): pl.pallas_call(functools.partial(embed_kernel, count, own, vecs, feat), o...  10.2 us
    ppermute x17, waiting for transfers between devices, exchange(): return lax.ppermute(x, ('row', 'col'), pairs)  5.51 us
    pallas_call x1, Pallas kernels, replicated(): pl.pallas_call(functools.partial(pack_kernel, vecs, feat), out_shape=pltp...  0.88 us
  transfers between devices with their start and end apart: 17, of which 6 were waited for; matrix products, arithmetic and copies ran while one was open for 0% of the time, Pallas kernels for 0%

profile of v6, /device:TPU:0, one launch (start us, length us, event | category | flops | bytes accessed | tf_op | source)
XLA Modules:
  0.0 32.3 jit_solution(14690515041118480751)
XLA Ops:
  0.0 0.9 %shard_map.28 = bf16[32,896]{1,0:T(8,128)(2,1)S(1)} custom-call(bf16[32,768]{1,0:T(8,128)(2,1)} %e_ref.1, f32[32,64]{1,0:T(8,128)} %bitcast.2), custom_call_target="tpu_custom_call" | custom-call | tf_op jit(solution)/shard_map/pallas_call | solution.py:155
  0.9 5.1 %collective-permute-start.3 = (bf16[32,896]{1,0:T(8,128)(2,1)S(1)}, bf16[32,896]{1,0:T(8,128)(2,1)S(1)}, u32[]{:S(2)}, u32[]{:S(2)}) collective-permute-start(bf16[32,896]{1,0:T(8,128)(2,1)S(1)} %shard_map.28), channel_id=1, source_target_pairs={{0,24},{1,25},{2,26},{3,27},{4,28},{5,29},{6,30},{7,31},{8,16},{9,... | collective-permute-start | bytes 172040 | tf_op jit(solution)/shard_map/ppermute | solution.py:148
  5.9 0.0 collective-permute-start.2
  5.9 1.5 %collective-permute-start.1 = (bf16[32,896]{1,0:T(8,128)(2,1)S(1)}, bf16[32,896]{1,0:T(8,128)(2,1)S(1)}, u32[]{:S(2)}, u32[]{:S(2)}) collective-permute-start(bf16[32,896]{1,0:T(8,128)(2,1)S(1)} %shard_map.28), channel_id=1, source_target_pairs={{0,4},{1,5},{2,6},{3,7},{4,0},{5,1},{6,2},{7,3},{8,12},{9,13},{10,... | collective-permute-start | bytes 172040 | tf_op jit(solution)/shard_map/ppermute | solution.py:148
  7.5 0.8 %collective-permute-start.6 = (bf16[32,896]{1,0:T(8,128)(2,1)S(1)}, bf16[32,896]{1,0:T(8,128)(2,1)S(1)}, u32[]{:S(2)}, u32[]{:S(2)}) collective-permute-start(bf16[32,896]{1,0:T(8,128)(2,1)S(1)} %shard_map.28), channel_id=1, source_target_pairs={{0,8},{1,9},{2,10},{3,11},{4,12},{5,13},{6,14},{7,15},{8,0},{9,1},... | collective-permute-start | bytes 172040 | tf_op jit(solution)/shard_map/ppermute | solution.py:148
  8.2 1.4 %collective-permute-start.4 = (bf16[32,896]{1,0:T(8,128)(2,1)S(1)}, bf16[32,896]{1,0:T(8,128)(2,1)S(1)}, u32[]{:S(2)}, u32[]{:S(2)}) collective-permute-start(bf16[32,896]{1,0:T(8,128)(2,1)S(1)} %shard_map.28), channel_id=1, source_target_pairs={{0,6},{1,7},{2,4},{3,5},{4,2},{5,3},{6,0},{7,1},{8,14},{9,15},{10,... | collective-permute-start | bytes 172040 | tf_op jit(solution)/shard_map/ppermute | solution.py:148
  9.7 0.0 collective-permute-done.3
  9.7 0.5 %collective-permute-start = (bf16[32,896]{1,0:T(8,128)(2,1)S(1)}, bf16[32,896]{1,0:T(8,128)(2,1)S(1)}, u32[]{:S(2)}, u32[]{:S(2)}) collective-permute-start(bf16[32,896]{1,0:T(8,128)(2,1)S(1)} %shard_map.28), channel_id=1, source_target_pairs={{0,2},{1,3},{2,0},{3,1},{4,6},{5,7},{6,4},{7,5},{8,10},{9,11},{10,... | collective-permute-start | bytes 172040 | tf_op jit(solution)/shard_map/ppermute | solution.py:148
  10.2 0.8 %collective-permute-done.2 = bf16[32,896]{1,0:T(8,128)(2,1)S(1)} collective-permute-done((bf16[32,896]{1,0:T(8,128)(2,1)S(1)}, bf16[32,896]{1,0:T(8,128)(2,1)S(1)}, u32[]{:S(2)}, u32[]{:S(2)}) %collective-permute-start.2) | collective-permute-done | bytes 57376 | tf_op jit(solution)/shard_map/ppermute | solution.py:148
  11.0 0.0 collective-permute-done.1
  11.0 1.6 %collective-permute-start.15 = (bf16[64,896]{1,0:T(8,128)(2,1)S(1)}, bf16[64,896]{1,0:T(8,128)(2,1)S(1)}, u32[]{:S(2)}, u32[]{:S(2)}) collective-permute-start(bf16[64,896]{1,0:T(8,128)(2,1)S(1)} %constant_dynamic-update-slice_fusion.refs_6_), channel_id=1, source_target_pairs={{0,2},{1,3},{2,0},{3,1},{4,6},{5,7},{6,4},{7,5},{8,10},{9,11},{10,... | collective-permute-start | bytes 344072 | tf_op jit(solution)/shard_map/ppermute | solution.py:148
  12.6 1.6 %collective-permute-start.13 = (bf16[64,896]{1,0:T(8,128)(2,1)S(1)}, bf16[64,896]{1,0:T(8,128)(2,1)S(1)}, u32[]{:S(2)}, u32[]{:S(2)}) collective-permute-start(bf16[64,896]{1,0:T(8,128)(2,1)S(1)} %constant_dynamic-update-slice_fusion.refs_6_), channel_id=1, source_target_pairs={{0,6},{1,7},{2,4},{3,5},{4,2},{5,3},{6,0},{7,1},{8,14},{9,15},{10,... | collective-permute-start | bytes 344072 | tf_op jit(solution)/shard_map/ppermute | solution.py:148
  14.1 0.0 collective-permute-done.4
  14.1 0.4 %collective-permute-start.11 = (bf16[64,896]{1,0:T(8,128)(2,1)S(1)}, bf16[64,896]{1,0:T(8,128)(2,1)S(1)}, u32[]{:S(2)}, u32[]{:S(2)}) collective-permute-start(bf16[64,896]{1,0:T(8,128)(2,1)S(1)} %constant_dynamic-update-slice_fusion.refs_6_), channel_id=1, source_target_pairs={{0,4},{1,5},{2,6},{3,7},{4,0},{5,1},{6,2},{7,3},{8,12},{9,13},{10,... | collective-permute-start | bytes 344072 | tf_op jit(solution)/shard_map/ppermute | solution.py:148
  14.6 0.0 collective-permute-done
  14.6 1.2 %collective-permute-start.8 = (bf16[96,896]{1,0:T(8,128)(2,1)S(1)}, bf16[96,896]{1,0:T(8,128)(2,1)S(1)}, u32[]{:S(2)}, u32[]{:S(2)}) collective-permute-start(bf16[96,896]{1,0:T(8,128)(2,1)S(1)} %pad_maximum_fusion.1), channel_id=1, source_target_pairs={{0,8},{1,9},{2,10},{3,11},{4,12},{5,13},{6,14},{7,15},{8,0},{9,1},... | collective-permute-start | bytes 516104 | tf_op jit(solution)/shard_map/ppermute | solution.py:148
  15.9 0.0 collective-permute-done.6.refs_2_
  15.9 0.0 collective-permute-start.7
  15.9 1.2 %collective-permute-done.7.refs_3_ = bf16[32,896]{1,0:T(8,128)(2,1)S(1)} collective-permute-done((bf16[32,896]{1,0:T(8,128)(2,1)S(1)}, bf16[32,896]{1,0:T(8,128)(2,1)S(1)}, u32[]{:S(2)}, u32[]{:S(2)}) %collective-permute-start.7) | collective-permute-done | bytes 57376 | tf_op jit(solution)/shard_map/ppermute | solution.py:148
  17.1 0.2 collective-permute-start.10
  17.3 0.0 collective-permute-done.15.refs_12_
  17.3 0.4 %collective-permute-start.5 = (bf16[128,896]{1,0:T(8,128)(2,1)S(1)}, bf16[128,896]{1,0:T(8,128)(2,1)S(1)}, u32[]{:S(2)}, u32[]{:S(2)}) collective-permute-start(bf16[128,896]{1,0:T(8,128)(2,1)S(1)} %pad_maximum_fusion.refs_0_), channel_id=1, source_target_pairs={{0,1},{1,0},{2,3},{3,2},{4,5},{5,4},{6,7},{7,6},{8,9},{9,8},{10,11... | collective-permute-start | bytes 688136 | tf_op jit(solution)/shard_map/ppermute | solution.py:148
  17.6 2.5 %collective-permute-done.8.refs_4_ = bf16[96,896]{1,0:T(8,128)(2,1)S(1)} collective-permute-done((bf16[96,896]{1,0:T(8,128)(2,1)S(1)}, bf16[96,896]{1,0:T(8,128)(2,1)S(1)}, u32[]{:S(2)}, u32[]{:S(2)}) %collective-permute-start.8) | collective-permute-done | bytes 172064 | tf_op jit(solution)/shard_map/ppermute | solution.py:148
  20.1 0.0 collective-permute-start.9
  20.1 0.0 collective-permute-done.13.refs_10_
  20.1 0.5 %collective-permute-start.16 = (bf16[64,896]{1,0:T(8,128)(2,1)S(1)}, bf16[64,896]{1,0:T(8,128)(2,1)S(1)}, u32[]{:S(2)}, u32[]{:S(2)}) collective-permute-start(bf16[64,896]{1,0:T(8,128)(2,1)S(1)} %collective-permute-done.15.refs_12_), channel_id=1, source_target_pairs={{0,1},{1,0},{2,3},{3,2},{4,5},{5,4},{6,7},{7,6},{8,9},{9,8},{10,11... | collective-permute-start | bytes 344072 | tf_op jit(solution)/shard_map/ppermute | solution.py:148
  20.6 0.0 collective-permute-done.11.refs_8_
  20.6 0.1 collective-permute-start.14
  20.7 0.0 collective-permute-done.10.refs_7_
  20.7 0.4 %collective-permute-start.12 = (bf16[64,896]{1,0:T(8,128)(2,1)S(1)}, bf16[64,896]{1,0:T(8,128)(2,1)S(1)}, u32[]{:S(2)}, u32[]{:S(2)}) collective-permute-start(bf16[64,896]{1,0:T(8,128)(2,1)S(1)} %collective-permute-done.11.refs_8_), channel_id=1, source_target_pairs={{0,1},{1,0},{2,3},{3,2},{4,5},{5,4},{6,7},{7,6},{8,9},{9,8},{10,11... | collective-permute-start | bytes 344072 | tf_op jit(solution)/shard_map/ppermute | solution.py:148
  21.1 0.5 %collective-permute-done.16.refs_13_ = bf16[64,896]{1,0:T(8,128)(2,1)S(1)} collective-permute-done((bf16[64,896]{1,0:T(8,128)(2,1)S(1)}, bf16[64,896]{1,0:T(8,128)(2,1)S(1)}, u32[]{:S(2)}, u32[]{:S(2)}) %collective-permute-start.16) | collective-permute-done | bytes 114720 | tf_op jit(solution)/shard_map/ppermute | solution.py:148
  21.7 0.3 collective-permute-done.14.refs_11_
  21.9 0.2 collective-permute-done.12.refs_9_
  22.1 0.0 collective-permute-done.5.refs_1_
  22.1 0.0 collective-permute-done.9.refs_5_
  22.1 10.2 %shard_map.29 = f32[32,64]{1,0:T(8,128)} custom-call(bf16[128,896]{1,0:T(8,128)(2,1)S(1)} %pad_maximum_fusion.refs_0_, bf16[128,896]{1,0:T(8,128)(2,1)S(1)} %collective-permute-done.5.refs_1_, bf16[32,896]{1,0:T(8,128)(2,1)S(1)} %collective-permute-done.6.refs_2_, bf16[32,896]{1,0:T(8,128)(2,1)S(1)} %collective-permute-done.7.refs_3_, ...), custom_call_target="tpu_custom_call" | custom-call | tf_op jit(solution)/shard_map/pallas_call | solution.py:182
  (4 shorter events, 0.1 us)
Async XLA Ops:
  0.9 8.8 %collective-permute-start.3 = (bf16[32,896]{1,0:T(8,128)(2,1)S(1)}, bf16[32,896]{1,0:T(8,128)(2,1)S(1)}, u32[]{:S(2)}, u32[]{:S(2)}) collective-permute-start(bf16[32,896]{1,0:T(8,128)(2,1)S(1)} %shard_map.28), channel_id=1, source_target_pairs={{0,24},{1,25},{2,26},{3,27},{4,28},{5,29},{6,30},{7,31},{8,16},{9,... | collective-permute-start | bytes 172040 | tf_op jit(solution)/shard_map/ppermute | solution.py:148
  5.9 5.1 %collective-permute-start.2 = (bf16[32,896]{1,0:T(8,128)(2,1)S(1)}, bf16[32,896]{1,0:T(8,128)(2,1)S(1)}, u32[]{:S(2)}, u32[]{:S(2)}) collective-permute-start(bf16[32,896]{1,0:T(8,128)(2,1)S(1)} %shard_map.28), channel_id=1, source_target_pairs={{0,16},{1,17},{2,18},{3,19},{4,20},{5,21},{6,22},{7,23},{8,24},{9,... | collective-permute-start | bytes 172040 | tf_op jit(solution)/shard_map/ppermute | solution.py:148
  5.9 5.1 %collective-permute-start.1 = (bf16[32,896]{1,0:T(8,128)(2,1)S(1)}, bf16[32,896]{1,0:T(8,128)(2,1)S(1)}, u32[]{:S(2)}, u32[]{:S(2)}) collective-permute-start(bf16[32,896]{1,0:T(8,128)(2,1)S(1)} %shard_map.28), channel_id=1, source_target_pairs={{0,4},{1,5},{2,6},{3,7},{4,0},{5,1},{6,2},{7,3},{8,12},{9,13},{10,... | collective-permute-start | bytes 172040 | tf_op jit(solution)/shard_map/ppermute | solution.py:148
  7.5 8.4 %collective-permute-start.6 = (bf16[32,896]{1,0:T(8,128)(2,1)S(1)}, bf16[32,896]{1,0:T(8,128)(2,1)S(1)}, u32[]{:S(2)}, u32[]{:S(2)}) collective-permute-start(bf16[32,896]{1,0:T(8,128)(2,1)S(1)} %shard_map.28), channel_id=1, source_target_pairs={{0,8},{1,9},{2,10},{3,11},{4,12},{5,13},{6,14},{7,15},{8,0},{9,1},... | collective-permute-start | bytes 172040 | tf_op jit(solution)/shard_map/ppermute | solution.py:148
  8.2 5.9 %collective-permute-start.4 = (bf16[32,896]{1,0:T(8,128)(2,1)S(1)}, bf16[32,896]{1,0:T(8,128)(2,1)S(1)}, u32[]{:S(2)}, u32[]{:S(2)}) collective-permute-start(bf16[32,896]{1,0:T(8,128)(2,1)S(1)} %shard_map.28), channel_id=1, source_target_pairs={{0,6},{1,7},{2,4},{3,5},{4,2},{5,3},{6,0},{7,1},{8,14},{9,15},{10,... | collective-permute-start | bytes 172040 | tf_op jit(solution)/shard_map/ppermute | solution.py:148
  9.7 4.9 %collective-permute-start = (bf16[32,896]{1,0:T(8,128)(2,1)S(1)}, bf16[32,896]{1,0:T(8,128)(2,1)S(1)}, u32[]{:S(2)}, u32[]{:S(2)}) collective-permute-start(bf16[32,896]{1,0:T(8,128)(2,1)S(1)} %shard_map.28), channel_id=1, source_target_pairs={{0,2},{1,3},{2,0},{3,1},{4,6},{5,7},{6,4},{7,5},{8,10},{9,11},{10,... | collective-permute-start | bytes 172040 | tf_op jit(solution)/shard_map/ppermute | solution.py:148
  11.0 6.2 %collective-permute-start.15 = (bf16[64,896]{1,0:T(8,128)(2,1)S(1)}, bf16[64,896]{1,0:T(8,128)(2,1)S(1)}, u32[]{:S(2)}, u32[]{:S(2)}) collective-permute-start(bf16[64,896]{1,0:T(8,128)(2,1)S(1)} %constant_dynamic-update-slice_fusion.refs_6_), channel_id=1, source_target_pairs={{0,2},{1,3},{2,0},{3,1},{4,6},{5,7},{6,4},{7,5},{8,10},{9,11},{10,... | collective-permute-start | bytes 344072 | tf_op jit(solution)/shard_map/ppermute | solution.py:148
  12.6 7.5 %collective-permute-start.13 = (bf16[64,896]{1,0:T(8,128)(2,1)S(1)}, bf16[64,896]{1,0:T(8,128)(2,1)S(1)}, u32[]{:S(2)}, u32[]{:S(2)}) collective-permute-start(bf16[64,896]{1,0:T(8,128)(2,1)S(1)} %constant_dynamic-update-slice_fusion.refs_6_), channel_id=1, source_target_pairs={{0,6},{1,7},{2,4},{3,5},{4,2},{5,3},{6,0},{7,1},{8,14},{9,15},{10,... | collective-permute-start | bytes 344072 | tf_op jit(solution)/shard_map/ppermute | solution.py:148
  14.1 6.5 %collective-permute-start.11 = (bf16[64,896]{1,0:T(8,128)(2,1)S(1)}, bf16[64,896]{1,0:T(8,128)(2,1)S(1)}, u32[]{:S(2)}, u32[]{:S(2)}) collective-permute-start(bf16[64,896]{1,0:T(8,128)(2,1)S(1)} %constant_dynamic-update-slice_fusion.refs_6_), channel_id=1, source_target_pairs={{0,4},{1,5},{2,6},{3,7},{4,0},{5,1},{6,2},{7,3},{8,12},{9,13},{10,... | collective-permute-start | bytes 344072 | tf_op jit(solution)/shard_map/ppermute | solution.py:148
  14.6 5.5 %collective-permute-start.8 = (bf16[96,896]{1,0:T(8,128)(2,1)S(1)}, bf16[96,896]{1,0:T(8,128)(2,1)S(1)}, u32[]{:S(2)}, u32[]{:S(2)}) collective-permute-start(bf16[96,896]{1,0:T(8,128)(2,1)S(1)} %pad_maximum_fusion.1), channel_id=1, source_target_pairs={{0,8},{1,9},{2,10},{3,11},{4,12},{5,13},{6,14},{7,15},{8,0},{9,1},... | collective-permute-start | bytes 516104 | tf_op jit(solution)/shard_map/ppermute | solution.py:148
  15.9 1.2 %collective-permute-start.7 = (bf16[32,896]{1,0:T(8,128)(2,1)S(1)}, bf16[32,896]{1,0:T(8,128)(2,1)S(1)}, u32[]{:S(2)}, u32[]{:S(2)}) collective-permute-start(bf16[32,896]{1,0:T(8,128)(2,1)S(1)} %collective-permute-done.6.refs_2_), channel_id=1, source_target_pairs={{0,1},{1,0},{2,3},{3,2},{4,5},{5,4},{6,7},{7,6},{8,9},{9,8},{10,11... | collective-permute-start | bytes 172040 | tf_op jit(solution)/shard_map/ppermute | solution.py:148
  17.1 3.6 %collective-permute-start.10 = (bf16[64,896]{1,0:T(8,128)(2,1)S(1)}, bf16[64,896]{1,0:T(8,128)(2,1)S(1)}, u32[]{:S(2)}, u32[]{:S(2)}) collective-permute-start(bf16[64,896]{1,0:T(8,128)(2,1)S(1)} %constant_dynamic-update-slice_fusion.refs_6_), channel_id=1, source_target_pairs={{0,1},{1,0},{2,3},{3,2},{4,5},{5,4},{6,7},{7,6},{8,9},{9,8},{10,11... | collective-permute-start | bytes 344072 | tf_op jit(solution)/shard_map/ppermute | solution.py:148
  17.3 4.8 %collective-permute-start.5 = (bf16[128,896]{1,0:T(8,128)(2,1)S(1)}, bf16[128,896]{1,0:T(8,128)(2,1)S(1)}, u32[]{:S(2)}, u32[]{:S(2)}) collective-permute-start(bf16[128,896]{1,0:T(8,128)(2,1)S(1)} %pad_maximum_fusion.refs_0_), channel_id=1, source_target_pairs={{0,1},{1,0},{2,3},{3,2},{4,5},{5,4},{6,7},{7,6},{8,9},{9,8},{10,11... | collective-permute-start | bytes 688136 | tf_op jit(solution)/shard_map/ppermute | solution.py:148
  20.1 2.0 %collective-permute-start.9 = (bf16[96,896]{1,0:T(8,128)(2,1)S(1)}, bf16[96,896]{1,0:T(8,128)(2,1)S(1)}, u32[]{:S(2)}, u32[]{:S(2)}) collective-permute-start(bf16[96,896]{1,0:T(8,128)(2,1)S(1)} %collective-permute-done.8.refs_4_), channel_id=1, source_target_pairs={{0,1},{1,0},{2,3},{3,2},{4,5},{5,4},{6,7},{7,6},{8,9},{9,8},{10,11... | collective-permute-start | bytes 516104 | tf_op jit(solution)/shard_map/ppermute | solution.py:148
  20.1 1.6 %collective-permute-start.16 = (bf16[64,896]{1,0:T(8,128)(2,1)S(1)}, bf16[64,896]{1,0:T(8,128)(2,1)S(1)}, u32[]{:S(2)}, u32[]{:S(2)}) collective-permute-start(bf16[64,896]{1,0:T(8,128)(2,1)S(1)} %collective-permute-done.15.refs_12_), channel_id=1, source_target_pairs={{0,1},{1,0},{2,3},{3,2},{4,5},{5,4},{6,7},{7,6},{8,9},{9,8},{10,11... | collective-permute-start | bytes 344072 | tf_op jit(solution)/shard_map/ppermute | solution.py:148
  20.6 1.3 %collective-permute-start.14 = (bf16[64,896]{1,0:T(8,128)(2,1)S(1)}, bf16[64,896]{1,0:T(8,128)(2,1)S(1)}, u32[]{:S(2)}, u32[]{:S(2)}) collective-permute-start(bf16[64,896]{1,0:T(8,128)(2,1)S(1)} %collective-permute-done.13.refs_10_), channel_id=1, source_target_pairs={{0,1},{1,0},{2,3},{3,2},{4,5},{5,4},{6,7},{7,6},{8,9},{9,8},{10,11... | collective-permute-start | bytes 344072 | tf_op jit(solution)/shard_map/ppermute | solution.py:148
  20.7 1.4 %collective-permute-start.12 = (bf16[64,896]{1,0:T(8,128)(2,1)S(1)}, bf16[64,896]{1,0:T(8,128)(2,1)S(1)}, u32[]{:S(2)}, u32[]{:S(2)}) collective-permute-start(bf16[64,896]{1,0:T(8,128)(2,1)S(1)} %collective-permute-done.11.refs_8_), channel_id=1, source_target_pairs={{0,1},{1,0},{2,3},{3,2},{4,5},{5,4},{6,7},{7,6},{8,9},{9,8},{10,11... | collective-permute-start | bytes 344072 | tf_op jit(solution)/shard_map/ppermute | solution.py:148

commit v7 on v6

--- a/solution.py
+++ b/solution.py
@@ -90,23 +90,31 @@
         e_ref[at:to, :] = piece[:, :feat]
         x_ref[at:to, :] = piece[:, feat:].astype(jnp.float32)
         at = to
-    eye = lax.broadcasted_iota(jnp.int32, (per, per), 0) == lax.broadcasted_iota(jnp.int32, (per, per), 1)
     cols, rows = [], []
     for i in range(points // per):
-        e = e_ref[i * per : (i + 1) * per, :]
-        d = jnp.where(eye, dot(e, e, NT), 0.0)
-        cols.append(jnp.sum(d, axis=1, keepdims=True))
-        rows.append(jnp.sum(d, axis=0, keepdims=True))
+        e = e_ref[i * per : (i + 1) * per, :].astype(jnp.float32)
+        col = jnp.sum(e * e, axis=1, keepdims=True)
+        cols.append(col)
+        rows.append(jnp.broadcast_to(col, (per, per)).T[:1])
     row_sq = jnp.concatenate(rows, axis=1)
     rate = 1.0 / (TEMPER * feat)
-    degree = jnp.zeros((1, points), jnp.float32)
     step = 2 * per
-    for i in range(points // step):
-        g = dot(e_ref[i * step : (i + 1) * step, :], e_ref[...], NT)
+    blocks = points // step
+    sums = [jnp.zeros((1, step), jnp.float32) for _ in range(blocks)]
+    for i in range(blocks):
+        lo, hi = i * step, (i + 1) * step
+        g = dot(e_ref[lo:hi, :], e_ref[lo:, :], NT)
         col_sq = jnp.concatenate(cols[2 * i : 2 * i + 2], axis=0)
-        k = jnp.exp((2.0 * g - col_sq - row_sq) * rate)
-        degree = degree + jnp.sum(k, axis=0, keepdims=True)
-        k_ref[i * step : (i + 1) * step, :] = k.astype(jnp.bfloat16)
+        k = jnp.exp((2.0 * g - col_sq - row_sq[:, lo:]) * rate)
+        k_ref[lo:hi, lo:] = k.astype(jnp.bfloat16)
+        for j in range(i, blocks):
+            part = k[:, (j - i) * step : (j - i + 1) * step]
+            sums[j] = sums[j] + jnp.sum(part, axis=0, keepdims=True)
+            if j > i:
+                part = part.T
+                sums[i] = sums[i] + jnp.sum(part, axis=0, keepdims=True)
+                k_ref[j * step : (j + 1) * step, lo:hi] = part.astype(jnp.bfloat16)
+    degree = jnp.concatenate(sums, axis=1)
     scale = 1.0 / jnp.sqrt(degree)
     lane = lax.broadcasted_iota(jnp.int32, (vecs, 2 * vecs), 1)
     unit = (lane == lax.broadcasted_iota(jnp.int32, (vecs, 2 * vecs), 0) + vecs).astype(jnp.float32)

time: 32.5 us -> 31.7 us (0.975)
  Pallas kernels: 11.1 us -> 10.3 us
    pallas_call x1, Pallas kernels: 10.2 us -> 9.41 us  [replicated(): pl.pallas_call(functools.partial(embed_kernel, count, own, vecs, feat), o...]
where the time goes in v7:
time: 31.7 us; the launch traced here: 31.5 us
  starting transfers between devices  15.6 us (49%)
  Pallas kernels  10.3 us (32%)
  waiting for transfers between devices  5.51 us (17%)
    ppermute x17, starting transfers between devices, exchange(): return lax.ppermute(x, ('row', 'col'), pairs)  15.6 us
    pallas_call x1, Pallas kernels, replicated(): pl.pallas_call(functools.partial(embed_kernel, count, own, vecs, feat), o...  9.41 us
    ppermute x17, waiting for transfers between devices, exchange(): return lax.ppermute(x, ('row', 'col'), pairs)  5.51 us
    pallas_call x1, Pallas kernels, replicated(): pl.pallas_call(functools.partial(pack_kernel, vecs, feat), out_shape=pltp...  0.88 us
  transfers between devices with their start and end apart: 17, of which 6 were waited for; matrix products, arithmetic and copies ran while one was open for 0% of the time, Pallas kernels for 0%

profile of v7, /device:TPU:0, one launch (start us, length us, event | category | flops | bytes accessed | tf_op | source)
XLA Modules:
  0.0 31.5 jit_solution(7297444854402417993)
XLA Ops:
  0.0 0.9 %shard_map.28 = bf16[32,896]{1,0:T(8,128)(2,1)S(1)} custom-call(bf16[32,768]{1,0:T(8,128)(2,1)} %e_ref.1, f32[32,64]{1,0:T(8,128)} %bitcast.2), custom_call_target="tpu_custom_call" | custom-call | tf_op jit(solution)/shard_map/pallas_call | solution.py:163
  0.9 5.1 %collective-permute-start.3 = (bf16[32,896]{1,0:T(8,128)(2,1)S(1)}, bf16[32,896]{1,0:T(8,128)(2,1)S(1)}, u32[]{:S(2)}, u32[]{:S(2)}) collective-permute-start(bf16[32,896]{1,0:T(8,128)(2,1)S(1)} %shard_map.28), channel_id=1, source_target_pairs={{0,24},{1,25},{2,26},{3,27},{4,28},{5,29},{6,30},{7,31},{8,16},{9,... | collective-permute-start | bytes 172040 | tf_op jit(solution)/shard_map/ppermute | solution.py:156
  5.9 0.0 collective-permute-start.2
  5.9 1.5 %collective-permute-start.1 = (bf16[32,896]{1,0:T(8,128)(2,1)S(1)}, bf16[32,896]{1,0:T(8,128)(2,1)S(1)}, u32[]{:S(2)}, u32[]{:S(2)}) collective-permute-start(bf16[32,896]{1,0:T(8,128)(2,1)S(1)} %shard_map.28), channel_id=1, source_target_pairs={{0,4},{1,5},{2,6},{3,7},{4,0},{5,1},{6,2},{7,3},{8,12},{9,13},{10,... | collective-permute-start | bytes 172040 | tf_op jit(solution)/shard_map/ppermute | solution.py:156
  7.5 0.8 %collective-permute-start.6 = (bf16[32,896]{1,0:T(8,128)(2,1)S(1)}, bf16[32,896]{1,0:T(8,128)(2,1)S(1)}, u32[]{:S(2)}, u32[]{:S(2)}) collective-permute-start(bf16[32,896]{1,0:T(8,128)(2,1)S(1)} %shard_map.28), channel_id=1, source_target_pairs={{0,8},{1,9},{2,10},{3,11},{4,12},{5,13},{6,14},{7,15},{8,0},{9,1},... | collective-permute-start | bytes 172040 | tf_op jit(solution)/shard_map/ppermute | solution.py:156
  8.2 1.4 %collective-permute-start.4 = (bf16[32,896]{1,0:T(8,128)(2,1)S(1)}, bf16[32,896]{1,0:T(8,128)(2,1)S(1)}, u32[]{:S(2)}, u32[]{:S(2)}) collective-permute-start(bf16[32,896]{1,0:T(8,128)(2,1)S(1)} %shard_map.28), channel_id=1, source_target_pairs={{0,6},{1,7},{2,4},{3,5},{4,2},{5,3},{6,0},{7,1},{8,14},{9,15},{10,... | collective-permute-start | bytes 172040 | tf_op jit(solution)/shard_map/ppermute | solution.py:156
  9.7 0.0 collective-permute-done.3
  9.7 0.5 %collective-permute-start = (bf16[32,896]{1,0:T(8,128)(2,1)S(1)}, bf16[32,896]{1,0:T(8,128)(2,1)S(1)}, u32[]{:S(2)}, u32[]{:S(2)}) collective-permute-start(bf16[32,896]{1,0:T(8,128)(2,1)S(1)} %shard_map.28), channel_id=1, source_target_pairs={{0,2},{1,3},{2,0},{3,1},{4,6},{5,7},{6,4},{7,5},{8,10},{9,11},{10,... | collective-permute-start | bytes 172040 | tf_op jit(solution)/shard_map/ppermute | solution.py:156
  10.2 0.8 %collective-permute-done.2 = bf16[32,896]{1,0:T(8,128)(2,1)S(1)} collective-permute-done((bf16[32,896]{1,0:T(8,128)(2,1)S(1)}, bf16[32,896]{1,0:T(8,128)(2,1)S(1)}, u32[]{:S(2)}, u32[]{:S(2)}) %collective-permute-start.2) | collective-permute-done | bytes 57376 | tf_op jit(solution)/shard_map/ppermute | solution.py:156
  11.0 0.0 collective-permute-done.1
  11.0 1.6 %collective-permute-start.15 = (bf16[64,896]{1,0:T(8,128)(2,1)S(1)}, bf16[64,896]{1,0:T(8,128)(2,1)S(1)}, u32[]{:S(2)}, u32[]{:S(2)}) collective-permute-start(bf16[64,896]{1,0:T(8,128)(2,1)S(1)} %constant_dynamic-update-slice_fusion.refs_6_), channel_id=1, source_target_pairs={{0,2},{1,3},{2,0},{3,1},{4,6},{5,7},{6,4},{7,5},{8,10},{9,11},{10,... | collective-permute-start | bytes 344072 | tf_op jit(solution)/shard_map/ppermute | solution.py:156
  12.6 1.6 %collective-permute-start.13 = (bf16[64,896]{1,0:T(8,128)(2,1)S(1)}, bf16[64,896]{1,0:T(8,128)(2,1)S(1)}, u32[]{:S(2)}, u32[]{:S(2)}) collective-permute-start(bf16[64,896]{1,0:T(8,128)(2,1)S(1)} %constant_dynamic-update-slice_fusion.refs_6_), channel_id=1, source_target_pairs={{0,6},{1,7},{2,4},{3,5},{4,2},{5,3},{6,0},{7,1},{8,14},{9,15},{10,... | collective-permute-start | bytes 344072 | tf_op jit(solution)/shard_map/ppermute | solution.py:156
  14.1 0.0 collective-permute-done.4
  14.1 0.4 %collective-permute-start.11 = (bf16[64,896]{1,0:T(8,128)(2,1)S(1)}, bf16[64,896]{1,0:T(8,128)(2,1)S(1)}, u32[]{:S(2)}, u32[]{:S(2)}) collective-permute-start(bf16[64,896]{1,0:T(8,128)(2,1)S(1)} %constant_dynamic-update-slice_fusion.refs_6_), channel_id=1, source_target_pairs={{0,4},{1,5},{2,6},{3,7},{4,0},{5,1},{6,2},{7,3},{8,12},{9,13},{10,... | collective-permute-start | bytes 344072 | tf_op jit(solution)/shard_map/ppermute | solution.py:156
  14.6 0.0 collective-permute-done
  14.6 1.2 %collective-permute-start.8 = (bf16[96,896]{1,0:T(8,128)(2,1)S(1)}, bf16[96,896]{1,0:T(8,128)(2,1)S(1)}, u32[]{:S(2)}, u32[]{:S(2)}) collective-permute-start(bf16[96,896]{1,0:T(8,128)(2,1)S(1)} %pad_maximum_fusion.1), channel_id=1, source_target_pairs={{0,8},{1,9},{2,10},{3,11},{4,12},{5,13},{6,14},{7,15},{8,0},{9,1},... | collective-permute-start | bytes 516104 | tf_op jit(solution)/shard_map/ppermute | solution.py:156
  15.9 0.0 collective-permute-done.6.refs_2_
  15.9 0.0 collective-permute-start.7
  15.9 1.2 %collective-permute-done.7.refs_3_ = bf16[32,896]{1,0:T(8,128)(2,1)S(1)} collective-permute-done((bf16[32,896]{1,0:T(8,128)(2,1)S(1)}, bf16[32,896]{1,0:T(8,128)(2,1)S(1)}, u32[]{:S(2)}, u32[]{:S(2)}) %collective-permute-start.7) | collective-permute-done | bytes 57376 | tf_op jit(solution)/shard_map/ppermute | solution.py:156
  17.1 0.2 collective-permute-start.10
  17.3 0.0 collective-permute-done.15.refs_12_
  17.3 0.4 %collective-permute-start.5 = (bf16[128,896]{1,0:T(8,128)(2,1)S(1)}, bf16[128,896]{1,0:T(8,128)(2,1)S(1)}, u32[]{:S(2)}, u32[]{:S(2)}) collective-permute-start(bf16[128,896]{1,0:T(8,128)(2,1)S(1)} %pad_maximum_fusion.refs_0_), channel_id=1, source_target_pairs={{0,1},{1,0},{2,3},{3,2},{4,5},{5,4},{6,7},{7,6},{8,9},{9,8},{10,11... | collective-permute-start | bytes 688136 | tf_op jit(solution)/shard_map/ppermute | solution.py:156
  17.6 2.5 %collective-permute-done.8.refs_4_ = bf16[96,896]{1,0:T(8,128)(2,1)S(1)} collective-permute-done((bf16[96,896]{1,0:T(8,128)(2,1)S(1)}, bf16[96,896]{1,0:T(8,128)(2,1)S(1)}, u32[]{:S(2)}, u32[]{:S(2)}) %collective-permute-start.8) | collective-permute-done | bytes 172064 | tf_op jit(solution)/shard_map/ppermute | solution.py:156
  20.1 0.0 collective-permute-start.9
  20.1 0.0 collective-permute-done.13.refs_10_
  20.1 0.5 %collective-permute-start.16 = (bf16[64,896]{1,0:T(8,128)(2,1)S(1)}, bf16[64,896]{1,0:T(8,128)(2,1)S(1)}, u32[]{:S(2)}, u32[]{:S(2)}) collective-permute-start(bf16[64,896]{1,0:T(8,128)(2,1)S(1)} %collective-permute-done.15.refs_12_), channel_id=1, source_target_pairs={{0,1},{1,0},{2,3},{3,2},{4,5},{5,4},{6,7},{7,6},{8,9},{9,8},{10,11... | collective-permute-start | bytes 344072 | tf_op jit(solution)/shard_map/ppermute | solution.py:156
  20.6 0.0 collective-permute-done.11.refs_8_
  20.6 0.1 collective-permute-start.14
  20.7 0.0 collective-permute-done.10.refs_7_
  20.7 0.4 %collective-permute-start.12 = (bf16[64,896]{1,0:T(8,128)(2,1)S(1)}, bf16[64,896]{1,0:T(8,128)(2,1)S(1)}, u32[]{:S(2)}, u32[]{:S(2)}) collective-permute-start(bf16[64,896]{1,0:T(8,128)(2,1)S(1)} %collective-permute-done.11.refs_8_), channel_id=1, source_target_pairs={{0,1},{1,0},{2,3},{3,2},{4,5},{5,4},{6,7},{7,6},{8,9},{9,8},{10,11... | collective-permute-start | bytes 344072 | tf_op jit(solution)/shard_map/ppermute | solution.py:156
  21.1 0.5 %collective-permute-done.16.refs_13_ = bf16[64,896]{1,0:T(8,128)(2,1)S(1)} collective-permute-done((bf16[64,896]{1,0:T(8,128)(2,1)S(1)}, bf16[64,896]{1,0:T(8,128)(2,1)S(1)}, u32[]{:S(2)}, u32[]{:S(2)}) %collective-permute-start.16) | collective-permute-done | bytes 114720 | tf_op jit(solution)/shard_map/ppermute | solution.py:156
  21.7 0.3 collective-permute-done.14.refs_11_
  21.9 0.2 collective-permute-done.12.refs_9_
  22.1 0.0 collective-permute-done.5.refs_1_
  22.1 0.0 collective-permute-done.9.refs_5_
  22.1 9.4 %shard_map.29 = f32[32,64]{1,0:T(8,128)} custom-call(bf16[128,896]{1,0:T(8,128)(2,1)S(1)} %pad_maximum_fusion.refs_0_, bf16[128,896]{1,0:T(8,128)(2,1)S(1)} %collective-permute-done.5.refs_1_, bf16[32,896]{1,0:T(8,128)(2,1)S(1)} %collective-permute-done.6.refs_2_, bf16[32,896]{1,0:T(8,128)(2,1)S(1)} %collective-permute-done.7.refs_3_, ...), custom_call_target="tpu_custom_call" | custom-call | tf_op jit(solution)/shard_map/pallas_call | solution.py:190
  (4 shorter events, 0.1 us)
Async XLA Ops:
  0.9 8.8 %collective-permute-start.3 = (bf16[32,896]{1,0:T(8,128)(2,1)S(1)}, bf16[32,896]{1,0:T(8,128)(2,1)S(1)}, u32[]{:S(2)}, u32[]{:S(2)}) collective-permute-start(bf16[32,896]{1,0:T(8,128)(2,1)S(1)} %shard_map.28), channel_id=1, source_target_pairs={{0,24},{1,25},{2,26},{3,27},{4,28},{5,29},{6,30},{7,31},{8,16},{9,... | collective-permute-start | bytes 172040 | tf_op jit(solution)/shard_map/ppermute | solution.py:156
  5.9 5.1 %collective-permute-start.2 = (bf16[32,896]{1,0:T(8,128)(2,1)S(1)}, bf16[32,896]{1,0:T(8,128)(2,1)S(1)}, u32[]{:S(2)}, u32[]{:S(2)}) collective-permute-start(bf16[32,896]{1,0:T(8,128)(2,1)S(1)} %shard_map.28), channel_id=1, source_target_pairs={{0,16},{1,17},{2,18},{3,19},{4,20},{5,21},{6,22},{7,23},{8,24},{9,... | collective-permute-start | bytes 172040 | tf_op jit(solution)/shard_map/ppermute | solution.py:156
  5.9 5.1 %collective-permute-start.1 = (bf16[32,896]{1,0:T(8,128)(2,1)S(1)}, bf16[32,896]{1,0:T(8,128)(2,1)S(1)}, u32[]{:S(2)}, u32[]{:S(2)}) collective-permute-start(bf16[32,896]{1,0:T(8,128)(2,1)S(1)} %shard_map.28), channel_id=1, source_target_pairs={{0,4},{1,5},{2,6},{3,7},{4,0},{5,1},{6,2},{7,3},{8,12},{9,13},{10,... | collective-permute-start | bytes 172040 | tf_op jit(solution)/shard_map/ppermute | solution.py:156
  7.5 8.4 %collective-permute-start.6 = (bf16[32,896]{1,0:T(8,128)(2,1)S(1)}, bf16[32,896]{1,0:T(8,128)(2,1)S(1)}, u32[]{:S(2)}, u32[]{:S(2)}) collective-permute-start(bf16[32,896]{1,0:T(8,128)(2,1)S(1)} %shard_map.28), channel_id=1, source_target_pairs={{0,8},{1,9},{2,10},{3,11},{4,12},{5,13},{6,14},{7,15},{8,0},{9,1},... | collective-permute-start | bytes 172040 | tf_op jit(solution)/shard_map/ppermute | solution.py:156
  8.2 5.9 %collective-permute-start.4 = (bf16[32,896]{1,0:T(8,128)(2,1)S(1)}, bf16[32,896]{1,0:T(8,128)(2,1)S(1)}, u32[]{:S(2)}, u32[]{:S(2)}) collective-permute-start(bf16[32,896]{1,0:T(8,128)(2,1)S(1)} %shard_map.28), channel_id=1, source_target_pairs={{0,6},{1,7},{2,4},{3,5},{4,2},{5,3},{6,0},{7,1},{8,14},{9,15},{10,... | collective-permute-start | bytes 172040 | tf_op jit(solution)/shard_map/ppermute | solution.py:156
  9.7 4.9 %collective-permute-start = (bf16[32,896]{1,0:T(8,128)(2,1)S(1)}, bf16[32,896]{1,0:T(8,128)(2,1)S(1)}, u32[]{:S(2)}, u32[]{:S(2)}) collective-permute-start(bf16[32,896]{1,0:T(8,128)(2,1)S(1)} %shard_map.28), channel_id=1, source_target_pairs={{0,2},{1,3},{2,0},{3,1},{4,6},{5,7},{6,4},{7,5},{8,10},{9,11},{10,... | collective-permute-start | bytes 172040 | tf_op jit(solution)/shard_map/ppermute | solution.py:156
  11.0 6.2 %collective-permute-start.15 = (bf16[64,896]{1,0:T(8,128)(2,1)S(1)}, bf16[64,896]{1,0:T(8,128)(2,1)S(1)}, u32[]{:S(2)}, u32[]{:S(2)}) collective-permute-start(bf16[64,896]{1,0:T(8,128)(2,1)S(1)} %constant_dynamic-update-slice_fusion.refs_6_), channel_id=1, source_target_pairs={{0,2},{1,3},{2,0},{3,1},{4,6},{5,7},{6,4},{7,5},{8,10},{9,11},{10,... | collective-permute-start | bytes 344072 | tf_op jit(solution)/shard_map/ppermute | solution.py:156
  12.6 7.5 %collective-permute-start.13 = (bf16[64,896]{1,0:T(8,128)(2,1)S(1)}, bf16[64,896]{1,0:T(8,128)(2,1)S(1)}, u32[]{:S(2)}, u32[]{:S(2)}) collective-permute-start(bf16[64,896]{1,0:T(8,128)(2,1)S(1)} %constant_dynamic-update-slice_fusion.refs_6_), channel_id=1, source_target_pairs={{0,6},{1,7},{2,4},{3,5},{4,2},{5,3},{6,0},{7,1},{8,14},{9,15},{10,... | collective-permute-start | bytes 344072 | tf_op jit(solution)/shard_map/ppermute | solution.py:156
  14.1 6.5 %collective-permute-start.11 = (bf16[64,896]{1,0:T(8,128)(2,1)S(1)}, bf16[64,896]{1,0:T(8,128)(2,1)S(1)}, u32[]{:S(2)}, u32[]{:S(2)}) collective-permute-start(bf16[64,896]{1,0:T(8,128)(2,1)S(1)} %constant_dynamic-update-slice_fusion.refs_6_), channel_id=1, source_target_pairs={{0,4},{1,5},{2,6},{3,7},{4,0},{5,1},{6,2},{7,3},{8,12},{9,13},{10,... | collective-permute-start | bytes 344072 | tf_op jit(solution)/shard_map/ppermute | solution.py:156
  14.6 5.5 %collective-permute-start.8 = (bf16[96,896]{1,0:T(8,128)(2,1)S(1)}, bf16[96,896]{1,0:T(8,128)(2,1)S(1)}, u32[]{:S(2)}, u32[]{:S(2)}) collective-permute-start(bf16[96,896]{1,0:T(8,128)(2,1)S(1)} %pad_maximum_fusion.1), channel_id=1, source_target_pairs={{0,8},{1,9},{2,10},{3,11},{4,12},{5,13},{6,14},{7,15},{8,0},{9,1},... | collective-permute-start | bytes 516104 | tf_op jit(solution)/shard_map/ppermute | solution.py:156
  15.9 1.2 %collective-permute-start.7 = (bf16[32,896]{1,0:T(8,128)(2,1)S(1)}, bf16[32,896]{1,0:T(8,128)(2,1)S(1)}, u32[]{:S(2)}, u32[]{:S(2)}) collective-permute-start(bf16[32,896]{1,0:T(8,128)(2,1)S(1)} %collective-permute-done.6.refs_2_), channel_id=1, source_target_pairs={{0,1},{1,0},{2,3},{3,2},{4,5},{5,4},{6,7},{7,6},{8,9},{9,8},{10,11... | collective-permute-start | bytes 172040 | tf_op jit(solution)/shard_map/ppermute | solution.py:156
  17.1 3.6 %collective-permute-start.10 = (bf16[64,896]{1,0:T(8,128)(2,1)S(1)}, bf16[64,896]{1,0:T(8,128)(2,1)S(1)}, u32[]{:S(2)}, u32[]{:S(2)}) collective-permute-start(bf16[64,896]{1,0:T(8,128)(2,1)S(1)} %constant_dynamic-update-slice_fusion.refs_6_), channel_id=1, source_target_pairs={{0,1},{1,0},{2,3},{3,2},{4,5},{5,4},{6,7},{7,6},{8,9},{9,8},{10,11... | collective-permute-start | bytes 344072 | tf_op jit(solution)/shard_map/ppermute | solution.py:156
  17.3 4.8 %collective-permute-start.5 = (bf16[128,896]{1,0:T(8,128)(2,1)S(1)}, bf16[128,896]{1,0:T(8,128)(2,1)S(1)}, u32[]{:S(2)}, u32[]{:S(2)}) collective-permute-start(bf16[128,896]{1,0:T(8,128)(2,1)S(1)} %pad_maximum_fusion.refs_0_), channel_id=1, source_target_pairs={{0,1},{1,0},{2,3},{3,2},{4,5},{5,4},{6,7},{7,6},{8,9},{9,8},{10,11... | collective-permute-start | bytes 688136 | tf_op jit(solution)/shard_map/ppermute | solution.py:156
  20.1 2.0 %collective-permute-start.9 = (bf16[96,896]{1,0:T(8,128)(2,1)S(1)}, bf16[96,896]{1,0:T(8,128)(2,1)S(1)}, u32[]{:S(2)}, u32[]{:S(2)}) collective-permute-start(bf16[96,896]{1,0:T(8,128)(2,1)S(1)} %collective-permute-done.8.refs_4_), channel_id=1, source_target_pairs={{0,1},{1,0},{2,3},{3,2},{4,5},{5,4},{6,7},{7,6},{8,9},{9,8},{10,11... | collective-permute-start | bytes 516104 | tf_op jit(solution)/shard_map/ppermute | solution.py:156
  20.1 1.6 %collective-permute-start.16 = (bf16[64,896]{1,0:T(8,128)(2,1)S(1)}, bf16[64,896]{1,0:T(8,128)(2,1)S(1)}, u32[]{:S(2)}, u32[]{:S(2)}) collective-permute-start(bf16[64,896]{1,0:T(8,128)(2,1)S(1)} %collective-permute-done.15.refs_12_), channel_id=1, source_target_pairs={{0,1},{1,0},{2,3},{3,2},{4,5},{5,4},{6,7},{7,6},{8,9},{9,8},{10,11... | collective-permute-start | bytes 344072 | tf_op jit(solution)/shard_map/ppermute | solution.py:156
  20.6 1.3 %collective-permute-start.14 = (bf16[64,896]{1,0:T(8,128)(2,1)S(1)}, bf16[64,896]{1,0:T(8,128)(2,1)S(1)}, u32[]{:S(2)}, u32[]{:S(2)}) collective-permute-start(bf16[64,896]{1,0:T(8,128)(2,1)S(1)} %collective-permute-done.13.refs_10_), channel_id=1, source_target_pairs={{0,1},{1,0},{2,3},{3,2},{4,5},{5,4},{6,7},{7,6},{8,9},{9,8},{10,11... | collective-permute-start | bytes 344072 | tf_op jit(solution)/shard_map/ppermute | solution.py:156
  20.7 1.4 %collective-permute-start.12 = (bf16[64,896]{1,0:T(8,128)(2,1)S(1)}, bf16[64,896]{1,0:T(8,128)(2,1)S(1)}, u32[]{:S(2)}, u32[]{:S(2)}) collective-permute-start(bf16[64,896]{1,0:T(8,128)(2,1)S(1)} %collective-permute-done.11.refs_8_), channel_id=1, source_target_pairs={{0,1},{1,0},{2,3},{3,2},{4,5},{5,4},{6,7},{7,6},{8,9},{9,8},{10,11... | collective-permute-start | bytes 344072 | tf_op jit(solution)/shard_map/ppermute | solution.py:156

commit v8 on v7

--- a/solution.py
+++ b/solution.py
@@ -93,11 +93,13 @@
     cols, rows = [], []
     for i in range(points // per):
         e = e_ref[i * per : (i + 1) * per, :].astype(jnp.float32)
-        col = jnp.sum(e * e, axis=1, keepdims=True)
+        col = jnp.sum(e * e, axis=1, keepdims=True) * (1.0 / (TEMPER * feat))
         cols.append(col)
         rows.append(jnp.broadcast_to(col, (per, per)).T[:1])
     row_sq = jnp.concatenate(rows, axis=1)
     rate = 1.0 / (TEMPER * feat)
+    start = jnp.concatenate([x_ref[i * per : (i + 1) * per, :].T for i in range(points // per)], axis=1)
+    start = start[:vecs] + start[vecs:]
     step = 2 * per
     blocks = points // step
     sums = [jnp.zeros((1, step), jnp.float32) for _ in range(blocks)]
@@ -105,7 +107,7 @@
         lo, hi = i * step, (i + 1) * step
         g = dot(e_ref[lo:hi, :], e_ref[lo:, :], NT)
         col_sq = jnp.concatenate(cols[2 * i : 2 * i + 2], axis=0)
-        k = jnp.exp((2.0 * g - col_sq - row_sq[:, lo:]) * rate)
+        k = jnp.exp(g * (2.0 * rate) - col_sq - row_sq[:, lo:])
         k_ref[lo:hi, lo:] = k.astype(jnp.bfloat16)
         for j in range(i, blocks):
             part = k[:, (j - i) * step : (j - i + 1) * step]
@@ -118,8 +120,7 @@
     scale = 1.0 / jnp.sqrt(degree)
     lane = lax.broadcasted_iota(jnp.int32, (vecs, 2 * vecs), 1)
     unit = (lane == lax.broadcasted_iota(jnp.int32, (vecs, 2 * vecs), 0) + vecs).astype(jnp.float32)
-    start = jnp.concatenate([x_ref[i * per : (i + 1) * per, :].T for i in range(points // per)], axis=1)
-    scaled = ((start[:vecs] + start[vecs:]) * scale).astype(jnp.bfloat16)
+    scaled = (start * scale).astype(jnp.bfloat16)
     mixed = dot(scaled, k_ref[...]) * scale
     for sweep in range(ITERS):
         last = sweep == ITERS - 1
@@ -234,7 +235,8 @@
     rows, cols = mesh.shape["row"], mesh.shape["col"]
 
     def body(embeddings, start_block):
-        if (rows, cols) == (8, 4) and embeddings.shape[0] * 4 == 128 and start_block.shape[0] == 64:
+        own, vecs = embeddings.shape[0], start_block.shape[0]
+        if (rows, cols) == (8, 4) and own * cols == 2 * vecs == 128:
             return replicated(embeddings, start_block, rows, cols)
         return distributed(embeddings, start_block)
 

time: 31.7 us -> 31.6 us (level)
  no operation moved by 1% of the time
where the time goes in v8:
time: 31.6 us; the launch traced here: 31.5 us
  starting transfers between devices  15.6 us (49%)
  Pallas kernels  10.2 us (32%)
  waiting for transfers between devices  5.51 us (17%)
    ppermute x17, starting transfers between devices, exchange(): return lax.ppermute(x, ('row', 'col'), pairs)  15.6 us
    pallas_call x1, Pallas kernels, replicated(): pl.pallas_call(functools.partial(embed_kernel, count, own, vecs, feat), o...  9.36 us
    ppermute x17, waiting for transfers between devices, exchange(): return lax.ppermute(x, ('row', 'col'), pairs)  5.51 us
    pallas_call x1, Pallas kernels, replicated(): pl.pallas_call(functools.partial(pack_kernel, vecs, feat), out_shape=pltp...  0.88 us
  transfers between devices with their start and end apart: 17, of which 6 were waited for; matrix products, arithmetic and copies ran while one was open for 0% of the time, Pallas kernels for 0%

profile of v8, /device:TPU:0, one launch (start us, length us, event | category | flops | bytes accessed | tf_op | source)
XLA Modules:
  0.0 31.5 jit_solution(8808215374916437056)
XLA Ops:
  0.0 0.9 %shard_map.28 = bf16[32,896]{1,0:T(8,128)(2,1)S(1)} custom-call(bf16[32,768]{1,0:T(8,128)(2,1)} %e_ref.1, f32[32,64]{1,0:T(8,128)} %bitcast.2), custom_call_target="tpu_custom_call" | custom-call | tf_op jit(solution)/shard_map/pallas_call | solution.py:164
  0.9 5.1 %collective-permute-start.3 = (bf16[32,896]{1,0:T(8,128)(2,1)S(1)}, bf16[32,896]{1,0:T(8,128)(2,1)S(1)}, u32[]{:S(2)}, u32[]{:S(2)}) collective-permute-start(bf16[32,896]{1,0:T(8,128)(2,1)S(1)} %shard_map.28), channel_id=1, source_target_pairs={{0,24},{1,25},{2,26},{3,27},{4,28},{5,29},{6,30},{7,31},{8,16},{9,... | collective-permute-start | bytes 172040 | tf_op jit(solution)/shard_map/ppermute | solution.py:157
  5.9 0.0 collective-permute-start.2
  5.9 1.5 %collective-permute-start.1 = (bf16[32,896]{1,0:T(8,128)(2,1)S(1)}, bf16[32,896]{1,0:T(8,128)(2,1)S(1)}, u32[]{:S(2)}, u32[]{:S(2)}) collective-permute-start(bf16[32,896]{1,0:T(8,128)(2,1)S(1)} %shard_map.28), channel_id=1, source_target_pairs={{0,4},{1,5},{2,6},{3,7},{4,0},{5,1},{6,2},{7,3},{8,12},{9,13},{10,... | collective-permute-start | bytes 172040 | tf_op jit(solution)/shard_map/ppermute | solution.py:157
  7.5 0.8 %collective-permute-start.6 = (bf16[32,896]{1,0:T(8,128)(2,1)S(1)}, bf16[32,896]{1,0:T(8,128)(2,1)S(1)}, u32[]{:S(2)}, u32[]{:S(2)}) collective-permute-start(bf16[32,896]{1,0:T(8,128)(2,1)S(1)} %shard_map.28), channel_id=1, source_target_pairs={{0,8},{1,9},{2,10},{3,11},{4,12},{5,13},{6,14},{7,15},{8,0},{9,1},... | collective-permute-start | bytes 172040 | tf_op jit(solution)/shard_map/ppermute | solution.py:157
  8.2 1.4 %collective-permute-start.4 = (bf16[32,896]{1,0:T(8,128)(2,1)S(1)}, bf16[32,896]{1,0:T(8,128)(2,1)S(1)}, u32[]{:S(2)}, u32[]{:S(2)}) collective-permute-start(bf16[32,896]{1,0:T(8,128)(2,1)S(1)} %shard_map.28), channel_id=1, source_target_pairs={{0,6},{1,7},{2,4},{3,5},{4,2},{5,3},{6,0},{7,1},{8,14},{9,15},{10,... | collective-permute-start | bytes 172040 | tf_op jit(solution)/shard_map/ppermute | solution.py:157
  9.7 0.0 collective-permute-done.3
  9.7 0.5 %collective-permute-start = (bf16[32,896]{1,0:T(8,128)(2,1)S(1)}, bf16[32,896]{1,0:T(8,128)(2,1)S(1)}, u32[]{:S(2)}, u32[]{:S(2)}) collective-permute-start(bf16[32,896]{1,0:T(8,128)(2,1)S(1)} %shard_map.28), channel_id=1, source_target_pairs={{0,2},{1,3},{2,0},{3,1},{4,6},{5,7},{6,4},{7,5},{8,10},{9,11},{10,... | collective-permute-start | bytes 172040 | tf_op jit(solution)/shard_map/ppermute | solution.py:157
  10.2 0.8 %collective-permute-done.2 = bf16[32,896]{1,0:T(8,128)(2,1)S(1)} collective-permute-done((bf16[32,896]{1,0:T(8,128)(2,1)S(1)}, bf16[32,896]{1,0:T(8,128)(2,1)S(1)}, u32[]{:S(2)}, u32[]{:S(2)}) %collective-permute-start.2) | collective-permute-done | bytes 57376 | tf_op jit(solution)/shard_map/ppermute | solution.py:157
  11.0 0.0 collective-permute-done.1
  11.0 1.6 %collective-permute-start.15 = (bf16[64,896]{1,0:T(8,128)(2,1)S(1)}, bf16[64,896]{1,0:T(8,128)(2,1)S(1)}, u32[]{:S(2)}, u32[]{:S(2)}) collective-permute-start(bf16[64,896]{1,0:T(8,128)(2,1)S(1)} %constant_dynamic-update-slice_fusion.refs_6_), channel_id=1, source_target_pairs={{0,2},{1,3},{2,0},{3,1},{4,6},{5,7},{6,4},{7,5},{8,10},{9,11},{10,... | collective-permute-start | bytes 344072 | tf_op jit(solution)/shard_map/ppermute | solution.py:157
  12.6 1.6 %collective-permute-start.13 = (bf16[64,896]{1,0:T(8,128)(2,1)S(1)}, bf16[64,896]{1,0:T(8,128)(2,1)S(1)}, u32[]{:S(2)}, u32[]{:S(2)}) collective-permute-start(bf16[64,896]{1,0:T(8,128)(2,1)S(1)} %constant_dynamic-update-slice_fusion.refs_6_), channel_id=1, source_target_pairs={{0,6},{1,7},{2,4},{3,5},{4,2},{5,3},{6,0},{7,1},{8,14},{9,15},{10,... | collective-permute-start | bytes 344072 | tf_op jit(solution)/shard_map/ppermute | solution.py:157
  14.1 0.0 collective-permute-done.4
  14.1 0.4 %collective-permute-start.11 = (bf16[64,896]{1,0:T(8,128)(2,1)S(1)}, bf16[64,896]{1,0:T(8,128)(2,1)S(1)}, u32[]{:S(2)}, u32[]{:S(2)}) collective-permute-start(bf16[64,896]{1,0:T(8,128)(2,1)S(1)} %constant_dynamic-update-slice_fusion.refs_6_), channel_id=1, source_target_pairs={{0,4},{1,5},{2,6},{3,7},{4,0},{5,1},{6,2},{7,3},{8,12},{9,13},{10,... | collective-permute-start | bytes 344072 | tf_op jit(solution)/shard_map/ppermute | solution.py:157
  14.6 0.0 collective-permute-done
  14.6 1.2 %collective-permute-start.8 = (bf16[96,896]{1,0:T(8,128)(2,1)S(1)}, bf16[96,896]{1,0:T(8,128)(2,1)S(1)}, u32[]{:S(2)}, u32[]{:S(2)}) collective-permute-start(bf16[96,896]{1,0:T(8,128)(2,1)S(1)} %pad_maximum_fusion.1), channel_id=1, source_target_pairs={{0,8},{1,9},{2,10},{3,11},{4,12},{5,13},{6,14},{7,15},{8,0},{9,1},... | collective-permute-start | bytes 516104 | tf_op jit(solution)/shard_map/ppermute | solution.py:157
  15.9 0.0 collective-permute-done.6.refs_2_
  15.9 0.0 collective-permute-start.7
  15.9 1.2 %collective-permute-done.7.refs_3_ = bf16[32,896]{1,0:T(8,128)(2,1)S(1)} collective-permute-done((bf16[32,896]{1,0:T(8,128)(2,1)S(1)}, bf16[32,896]{1,0:T(8,128)(2,1)S(1)}, u32[]{:S(2)}, u32[]{:S(2)}) %collective-permute-start.7) | collective-permute-done | bytes 57376 | tf_op jit(solution)/shard_map/ppermute | solution.py:157
  17.1 0.2 collective-permute-start.10
  17.3 0.0 collective-permute-done.15.refs_12_
  17.3 0.4 %collective-permute-start.5 = (bf16[128,896]{1,0:T(8,128)(2,1)S(1)}, bf16[128,896]{1,0:T(8,128)(2,1)S(1)}, u32[]{:S(2)}, u32[]{:S(2)}) collective-permute-start(bf16[128,896]{1,0:T(8,128)(2,1)S(1)} %pad_maximum_fusion.refs_0_), channel_id=1, source_target_pairs={{0,1},{1,0},{2,3},{3,2},{4,5},{5,4},{6,7},{7,6},{8,9},{9,8},{10,11... | collective-permute-start | bytes 688136 | tf_op jit(solution)/shard_map/ppermute | solution.py:157
  17.6 2.5 %collective-permute-done.8.refs_4_ = bf16[96,896]{1,0:T(8,128)(2,1)S(1)} collective-permute-done((bf16[96,896]{1,0:T(8,128)(2,1)S(1)}, bf16[96,896]{1,0:T(8,128)(2,1)S(1)}, u32[]{:S(2)}, u32[]{:S(2)}) %collective-permute-start.8) | collective-permute-done | bytes 172064 | tf_op jit(solution)/shard_map/ppermute | solution.py:157
  20.1 0.0 collective-permute-start.9
  20.1 0.0 collective-permute-done.13.refs_10_
  20.1 0.5 %collective-permute-start.16 = (bf16[64,896]{1,0:T(8,128)(2,1)S(1)}, bf16[64,896]{1,0:T(8,128)(2,1)S(1)}, u32[]{:S(2)}, u32[]{:S(2)}) collective-permute-start(bf16[64,896]{1,0:T(8,128)(2,1)S(1)} %collective-permute-done.15.refs_12_), channel_id=1, source_target_pairs={{0,1},{1,0},{2,3},{3,2},{4,5},{5,4},{6,7},{7,6},{8,9},{9,8},{10,11... | collective-permute-start | bytes 344072 | tf_op jit(solution)/shard_map/ppermute | solution.py:157
  20.6 0.0 collective-permute-done.11.refs_8_
  20.6 0.1 collective-permute-start.14
  20.7 0.0 collective-permute-done.10.refs_7_
  20.7 0.4 %collective-permute-start.12 = (bf16[64,896]{1,0:T(8,128)(2,1)S(1)}, bf16[64,896]{1,0:T(8,128)(2,1)S(1)}, u32[]{:S(2)}, u32[]{:S(2)}) collective-permute-start(bf16[64,896]{1,0:T(8,128)(2,1)S(1)} %collective-permute-done.11.refs_8_), channel_id=1, source_target_pairs={{0,1},{1,0},{2,3},{3,2},{4,5},{5,4},{6,7},{7,6},{8,9},{9,8},{10,11... | collective-permute-start | bytes 344072 | tf_op jit(solution)/shard_map/ppermute | solution.py:157
  21.1 0.5 %collective-permute-done.16.refs_13_ = bf16[64,896]{1,0:T(8,128)(2,1)S(1)} collective-permute-done((bf16[64,896]{1,0:T(8,128)(2,1)S(1)}, bf16[64,896]{1,0:T(8,128)(2,1)S(1)}, u32[]{:S(2)}, u32[]{:S(2)}) %collective-permute-start.16) | collective-permute-done | bytes 114720 | tf_op jit(solution)/shard_map/ppermute | solution.py:157
  21.7 0.3 collective-permute-done.14.refs_11_
  21.9 0.2 collective-permute-done.12.refs_9_
  22.1 0.0 collective-permute-done.5.refs_1_
  22.1 0.0 collective-permute-done.9.refs_5_
  22.1 9.4 %shard_map.29 = f32[32,64]{1,0:T(8,128)} custom-call(bf16[128,896]{1,0:T(8,128)(2,1)S(1)} %pad_maximum_fusion.refs_0_, bf16[128,896]{1,0:T(8,128)(2,1)S(1)} %collective-permute-done.5.refs_1_, bf16[32,896]{1,0:T(8,128)(2,1)S(1)} %collective-permute-done.6.refs_2_, bf16[32,896]{1,0:T(8,128)(2,1)S(1)} %collective-permute-done.7.refs_3_, ...), custom_call_target="tpu_custom_call" | custom-call | tf_op jit(solution)/shard_map/pallas_call | solution.py:191
  (4 shorter events, 0.1 us)
Async XLA Ops:
  0.9 8.8 %collective-permute-start.3 = (bf16[32,896]{1,0:T(8,128)(2,1)S(1)}, bf16[32,896]{1,0:T(8,128)(2,1)S(1)}, u32[]{:S(2)}, u32[]{:S(2)}) collective-permute-start(bf16[32,896]{1,0:T(8,128)(2,1)S(1)} %shard_map.28), channel_id=1, source_target_pairs={{0,24},{1,25},{2,26},{3,27},{4,28},{5,29},{6,30},{7,31},{8,16},{9,... | collective-permute-start | bytes 172040 | tf_op jit(solution)/shard_map/ppermute | solution.py:157
  5.9 5.1 %collective-permute-start.2 = (bf16[32,896]{1,0:T(8,128)(2,1)S(1)}, bf16[32,896]{1,0:T(8,128)(2,1)S(1)}, u32[]{:S(2)}, u32[]{:S(2)}) collective-permute-start(bf16[32,896]{1,0:T(8,128)(2,1)S(1)} %shard_map.28), channel_id=1, source_target_pairs={{0,16},{1,17},{2,18},{3,19},{4,20},{5,21},{6,22},{7,23},{8,24},{9,... | collective-permute-start | bytes 172040 | tf_op jit(solution)/shard_map/ppermute | solution.py:157
  5.9 5.1 %collective-permute-start.1 = (bf16[32,896]{1,0:T(8,128)(2,1)S(1)}, bf16[32,896]{1,0:T(8,128)(2,1)S(1)}, u32[]{:S(2)}, u32[]{:S(2)}) collective-permute-start(bf16[32,896]{1,0:T(8,128)(2,1)S(1)} %shard_map.28), channel_id=1, source_target_pairs={{0,4},{1,5},{2,6},{3,7},{4,0},{5,1},{6,2},{7,3},{8,12},{9,13},{10,... | collective-permute-start | bytes 172040 | tf_op jit(solution)/shard_map/ppermute | solution.py:157
  7.5 8.4 %collective-permute-start.6 = (bf16[32,896]{1,0:T(8,128)(2,1)S(1)}, bf16[32,896]{1,0:T(8,128)(2,1)S(1)}, u32[]{:S(2)}, u32[]{:S(2)}) collective-permute-start(bf16[32,896]{1,0:T(8,128)(2,1)S(1)} %shard_map.28), channel_id=1, source_target_pairs={{0,8},{1,9},{2,10},{3,11},{4,12},{5,13},{6,14},{7,15},{8,0},{9,1},... | collective-permute-start | bytes 172040 | tf_op jit(solution)/shard_map/ppermute | solution.py:157
  8.2 5.9 %collective-permute-start.4 = (bf16[32,896]{1,0:T(8,128)(2,1)S(1)}, bf16[32,896]{1,0:T(8,128)(2,1)S(1)}, u32[]{:S(2)}, u32[]{:S(2)}) collective-permute-start(bf16[32,896]{1,0:T(8,128)(2,1)S(1)} %shard_map.28), channel_id=1, source_target_pairs={{0,6},{1,7},{2,4},{3,5},{4,2},{5,3},{6,0},{7,1},{8,14},{9,15},{10,... | collective-permute-start | bytes 172040 | tf_op jit(solution)/shard_map/ppermute | solution.py:157
  9.7 4.9 %collective-permute-start = (bf16[32,896]{1,0:T(8,128)(2,1)S(1)}, bf16[32,896]{1,0:T(8,128)(2,1)S(1)}, u32[]{:S(2)}, u32[]{:S(2)}) collective-permute-start(bf16[32,896]{1,0:T(8,128)(2,1)S(1)} %shard_map.28), channel_id=1, source_target_pairs={{0,2},{1,3},{2,0},{3,1},{4,6},{5,7},{6,4},{7,5},{8,10},{9,11},{10,... | collective-permute-start | bytes 172040 | tf_op jit(solution)/shard_map/ppermute | solution.py:157
  11.0 6.2 %collective-permute-start.15 = (bf16[64,896]{1,0:T(8,128)(2,1)S(1)}, bf16[64,896]{1,0:T(8,128)(2,1)S(1)}, u32[]{:S(2)}, u32[]{:S(2)}) collective-permute-start(bf16[64,896]{1,0:T(8,128)(2,1)S(1)} %constant_dynamic-update-slice_fusion.refs_6_), channel_id=1, source_target_pairs={{0,2},{1,3},{2,0},{3,1},{4,6},{5,7},{6,4},{7,5},{8,10},{9,11},{10,... | collective-permute-start | bytes 344072 | tf_op jit(solution)/shard_map/ppermute | solution.py:157
  12.6 7.5 %collective-permute-start.13 = (bf16[64,896]{1,0:T(8,128)(2,1)S(1)}, bf16[64,896]{1,0:T(8,128)(2,1)S(1)}, u32[]{:S(2)}, u32[]{:S(2)}) collective-permute-start(bf16[64,896]{1,0:T(8,128)(2,1)S(1)} %constant_dynamic-update-slice_fusion.refs_6_), channel_id=1, source_target_pairs={{0,6},{1,7},{2,4},{3,5},{4,2},{5,3},{6,0},{7,1},{8,14},{9,15},{10,... | collective-permute-start | bytes 344072 | tf_op jit(solution)/shard_map/ppermute | solution.py:157
  14.1 6.5 %collective-permute-start.11 = (bf16[64,896]{1,0:T(8,128)(2,1)S(1)}, bf16[64,896]{1,0:T(8,128)(2,1)S(1)}, u32[]{:S(2)}, u32[]{:S(2)}) collective-permute-start(bf16[64,896]{1,0:T(8,128)(2,1)S(1)} %constant_dynamic-update-slice_fusion.refs_6_), channel_id=1, source_target_pairs={{0,4},{1,5},{2,6},{3,7},{4,0},{5,1},{6,2},{7,3},{8,12},{9,13},{10,... | collective-permute-start | bytes 344072 | tf_op jit(solution)/shard_map/ppermute | solution.py:157
  14.6 5.5 %collective-permute-start.8 = (bf16[96,896]{1,0:T(8,128)(2,1)S(1)}, bf16[96,896]{1,0:T(8,128)(2,1)S(1)}, u32[]{:S(2)}, u32[]{:S(2)}) collective-permute-start(bf16[96,896]{1,0:T(8,128)(2,1)S(1)} %pad_maximum_fusion.1), channel_id=1, source_target_pairs={{0,8},{1,9},{2,10},{3,11},{4,12},{5,13},{6,14},{7,15},{8,0},{9,1},... | collective-permute-start | bytes 516104 | tf_op jit(solution)/shard_map/ppermute | solution.py:157
  15.9 1.2 %collective-permute-start.7 = (bf16[32,896]{1,0:T(8,128)(2,1)S(1)}, bf16[32,896]{1,0:T(8,128)(2,1)S(1)}, u32[]{:S(2)}, u32[]{:S(2)}) collective-permute-start(bf16[32,896]{1,0:T(8,128)(2,1)S(1)} %collective-permute-done.6.refs_2_), channel_id=1, source_target_pairs={{0,1},{1,0},{2,3},{3,2},{4,5},{5,4},{6,7},{7,6},{8,9},{9,8},{10,11... | collective-permute-start | bytes 172040 | tf_op jit(solution)/shard_map/ppermute | solution.py:157
  17.1 3.6 %collective-permute-start.10 = (bf16[64,896]{1,0:T(8,128)(2,1)S(1)}, bf16[64,896]{1,0:T(8,128)(2,1)S(1)}, u32[]{:S(2)}, u32[]{:S(2)}) collective-permute-start(bf16[64,896]{1,0:T(8,128)(2,1)S(1)} %constant_dynamic-update-slice_fusion.refs_6_), channel_id=1, source_target_pairs={{0,1},{1,0},{2,3},{3,2},{4,5},{5,4},{6,7},{7,6},{8,9},{9,8},{10,11... | collective-permute-start | bytes 344072 | tf_op jit(solution)/shard_map/ppermute | solution.py:157
  17.3 4.8 %collective-permute-start.5 = (bf16[128,896]{1,0:T(8,128)(2,1)S(1)}, bf16[128,896]{1,0:T(8,128)(2,1)S(1)}, u32[]{:S(2)}, u32[]{:S(2)}) collective-permute-start(bf16[128,896]{1,0:T(8,128)(2,1)S(1)} %pad_maximum_fusion.refs_0_), channel_id=1, source_target_pairs={{0,1},{1,0},{2,3},{3,2},{4,5},{5,4},{6,7},{7,6},{8,9},{9,8},{10,11... | collective-permute-start | bytes 688136 | tf_op jit(solution)/shard_map/ppermute | solution.py:157
  20.1 2.0 %collective-permute-start.9 = (bf16[96,896]{1,0:T(8,128)(2,1)S(1)}, bf16[96,896]{1,0:T(8,128)(2,1)S(1)}, u32[]{:S(2)}, u32[]{:S(2)}) collective-permute-start(bf16[96,896]{1,0:T(8,128)(2,1)S(1)} %collective-permute-done.8.refs_4_), channel_id=1, source_target_pairs={{0,1},{1,0},{2,3},{3,2},{4,5},{5,4},{6,7},{7,6},{8,9},{9,8},{10,11... | collective-permute-start | bytes 516104 | tf_op jit(solution)/shard_map/ppermute | solution.py:157
  20.1 1.6 %collective-permute-start.16 = (bf16[64,896]{1,0:T(8,128)(2,1)S(1)}, bf16[64,896]{1,0:T(8,128)(2,1)S(1)}, u32[]{:S(2)}, u32[]{:S(2)}) collective-permute-start(bf16[64,896]{1,0:T(8,128)(2,1)S(1)} %collective-permute-done.15.refs_12_), channel_id=1, source_target_pairs={{0,1},{1,0},{2,3},{3,2},{4,5},{5,4},{6,7},{7,6},{8,9},{9,8},{10,11... | collective-permute-start | bytes 344072 | tf_op jit(solution)/shard_map/ppermute | solution.py:157
  20.6 1.3 %collective-permute-start.14 = (bf16[64,896]{1,0:T(8,128)(2,1)S(1)}, bf16[64,896]{1,0:T(8,128)(2,1)S(1)}, u32[]{:S(2)}, u32[]{:S(2)}) collective-permute-start(bf16[64,896]{1,0:T(8,128)(2,1)S(1)} %collective-permute-done.13.refs_10_), channel_id=1, source_target_pairs={{0,1},{1,0},{2,3},{3,2},{4,5},{5,4},{6,7},{7,6},{8,9},{9,8},{10,11... | collective-permute-start | bytes 344072 | tf_op jit(solution)/shard_map/ppermute | solution.py:157
  20.7 1.4 %collective-permute-start.12 = (bf16[64,896]{1,0:T(8,128)(2,1)S(1)}, bf16[64,896]{1,0:T(8,128)(2,1)S(1)}, u32[]{:S(2)}, u32[]{:S(2)}) collective-permute-start(bf16[64,896]{1,0:T(8,128)(2,1)S(1)} %collective-permute-done.11.refs_8_), channel_id=1, source_target_pairs={{0,1},{1,0},{2,3},{3,2},{4,5},{5,4},{6,7},{7,6},{8,9},{9,8},{10,11... | collective-permute-start | bytes 344072 | tf_op jit(solution)/shard_map/ppermute | solution.py:157

commit v9 on v8

--- a/solution.py
+++ b/solution.py
@@ -82,7 +82,7 @@
 
 def embed_kernel(pieces, own, vecs, feat, *refs):
     piece_refs, out_ref = refs[:pieces], refs[pieces]
-    e_ref, k_ref, x_ref, m_ref = refs[pieces + 1 :]
+    e_ref, k_ref, x_ref = refs[pieces + 1 :]
     points, per = e_ref.shape[0], 2 * vecs
     at = 0
     for piece in piece_refs:
@@ -124,9 +124,8 @@
     mixed = dot(scaled, k_ref[...]) * scale
     for sweep in range(ITERS):
         last = sweep == ITERS - 1
-        for i, part in enumerate(split(mixed, 3)):
-            m_ref[i * vecs : (i + 1) * vecs, :] = part
-        p = dot(m_ref[...], m_ref[...], NT)
+        stack = jnp.concatenate(split(mixed, 3), axis=0)
+        p = dot(stack, stack, NT)
         p = p[:vecs] + p[vecs : 2 * vecs] + p[2 * vecs :]
         p = p[:, : 2 * vecs] + jnp.concatenate([p[:, 2 * vecs :], jnp.zeros((vecs, vecs), jnp.float32)], axis=1)
         p = p + pltpu.roll(p, vecs, 1)
@@ -197,7 +196,6 @@
             pltpu.VMEM((points, feat), jnp.bfloat16),
             pltpu.VMEM((points, points), jnp.bfloat16),
             pltpu.VMEM((points, 2 * vecs), jnp.float32),
-            pltpu.VMEM((3 * vecs, points), jnp.bfloat16),
         ],
         compiler_params=pltpu.CompilerParams(vmem_limit_bytes=40 * 1024 * 1024),
     )(*pieces).T

time: 31.6 us -> 31.6 us (level)
  no operation moved by 1% of the time
where the time goes in v9:
time: 31.6 us; the launch traced here: 31.5 us
  starting transfers between devices  15.6 us (49%)
  Pallas kernels  10.2 us (32%)
  waiting for transfers between devices  5.51 us (17%)
    ppermute x17, starting transfers between devices, exchange(): return lax.ppermute(x, ('row', 'col'), pairs)  15.6 us
    pallas_call x1, Pallas kernels, replicated(): pl.pallas_call(functools.partial(embed_kernel, count, own, vecs, feat), o...  9.36 us
    ppermute x17, waiting for transfers between devices, exchange(): return lax.ppermute(x, ('row', 'col'), pairs)  5.51 us
    pallas_call x1, Pallas kernels, replicated(): pl.pallas_call(functools.partial(pack_kernel, vecs, feat), out_shape=pltp...  0.88 us
  transfers between devices with their start and end apart: 17, of which 6 were waited for; matrix products, arithmetic and copies ran while one was open for 0% of the time, Pallas kernels for 0%

profile of v9, /device:TPU:0, one launch (start us, length us, event | category | flops | bytes accessed | tf_op | source)
XLA Modules:
  0.0 31.5 jit_solution(8808215374916437056)
XLA Ops:
  0.0 0.9 %shard_map.28 = bf16[32,896]{1,0:T(8,128)(2,1)S(1)} custom-call(bf16[32,768]{1,0:T(8,128)(2,1)} %e_ref.1, f32[32,64]{1,0:T(8,128)} %bitcast.2), custom_call_target="tpu_custom_call" | custom-call | tf_op jit(solution)/shard_map/pallas_call | solution.py:163
  0.9 5.1 %collective-permute-start.3 = (bf16[32,896]{1,0:T(8,128)(2,1)S(1)}, bf16[32,896]{1,0:T(8,128)(2,1)S(1)}, u32[]{:S(2)}, u32[]{:S(2)}) collective-permute-start(bf16[32,896]{1,0:T(8,128)(2,1)S(1)} %shard_map.28), channel_id=1, source_target_pairs={{0,24},{1,25},{2,26},{3,27},{4,28},{5,29},{6,30},{7,31},{8,16},{9,... | collective-permute-start | bytes 172040 | tf_op jit(solution)/shard_map/ppermute | solution.py:156
  5.9 0.0 collective-permute-start.2
  5.9 1.5 %collective-permute-start.1 = (bf16[32,896]{1,0:T(8,128)(2,1)S(1)}, bf16[32,896]{1,0:T(8,128)(2,1)S(1)}, u32[]{:S(2)}, u32[]{:S(2)}) collective-permute-start(bf16[32,896]{1,0:T(8,128)(2,1)S(1)} %shard_map.28), channel_id=1, source_target_pairs={{0,4},{1,5},{2,6},{3,7},{4,0},{5,1},{6,2},{7,3},{8,12},{9,13},{10,... | collective-permute-start | bytes 172040 | tf_op jit(solution)/shard_map/ppermute | solution.py:156
  7.5 0.8 %collective-permute-start.6 = (bf16[32,896]{1,0:T(8,128)(2,1)S(1)}, bf16[32,896]{1,0:T(8,128)(2,1)S(1)}, u32[]{:S(2)}, u32[]{:S(2)}) collective-permute-start(bf16[32,896]{1,0:T(8,128)(2,1)S(1)} %shard_map.28), channel_id=1, source_target_pairs={{0,8},{1,9},{2,10},{3,11},{4,12},{5,13},{6,14},{7,15},{8,0},{9,1},... | collective-permute-start | bytes 172040 | tf_op jit(solution)/shard_map/ppermute | solution.py:156
  8.2 1.4 %collective-permute-start.4 = (bf16[32,896]{1,0:T(8,128)(2,1)S(1)}, bf16[32,896]{1,0:T(8,128)(2,1)S(1)}, u32[]{:S(2)}, u32[]{:S(2)}) collective-permute-start(bf16[32,896]{1,0:T(8,128)(2,1)S(1)} %shard_map.28), channel_id=1, source_target_pairs={{0,6},{1,7},{2,4},{3,5},{4,2},{5,3},{6,0},{7,1},{8,14},{9,15},{10,... | collective-permute-start | bytes 172040 | tf_op jit(solution)/shard_map/ppermute | solution.py:156
  9.7 0.0 collective-permute-done.3
  9.7 0.5 %collective-permute-start = (bf16[32,896]{1,0:T(8,128)(2,1)S(1)}, bf16[32,896]{1,0:T(8,128)(2,1)S(1)}, u32[]{:S(2)}, u32[]{:S(2)}) collective-permute-start(bf16[32,896]{1,0:T(8,128)(2,1)S(1)} %shard_map.28), channel_id=1, source_target_pairs={{0,2},{1,3},{2,0},{3,1},{4,6},{5,7},{6,4},{7,5},{8,10},{9,11},{10,... | collective-permute-start | bytes 172040 | tf_op jit(solution)/shard_map/ppermute | solution.py:156
  10.2 0.8 %collective-permute-done.2 = bf16[32,896]{1,0:T(8,128)(2,1)S(1)} collective-permute-done((bf16[32,896]{1,0:T(8,128)(2,1)S(1)}, bf16[32,896]{1,0:T(8,128)(2,1)S(1)}, u32[]{:S(2)}, u32[]{:S(2)}) %collective-permute-start.2) | collective-permute-done | bytes 57376 | tf_op jit(solution)/shard_map/ppermute | solution.py:156
  11.0 0.0 collective-permute-done.1
  11.0 1.6 %collective-permute-start.15 = (bf16[64,896]{1,0:T(8,128)(2,1)S(1)}, bf16[64,896]{1,0:T(8,128)(2,1)S(1)}, u32[]{:S(2)}, u32[]{:S(2)}) collective-permute-start(bf16[64,896]{1,0:T(8,128)(2,1)S(1)} %constant_dynamic-update-slice_fusion.refs_6_), channel_id=1, source_target_pairs={{0,2},{1,3},{2,0},{3,1},{4,6},{5,7},{6,4},{7,5},{8,10},{9,11},{10,... | collective-permute-start | bytes 344072 | tf_op jit(solution)/shard_map/ppermute | solution.py:156
  12.6 1.6 %collective-permute-start.13 = (bf16[64,896]{1,0:T(8,128)(2,1)S(1)}, bf16[64,896]{1,0:T(8,128)(2,1)S(1)}, u32[]{:S(2)}, u32[]{:S(2)}) collective-permute-start(bf16[64,896]{1,0:T(8,128)(2,1)S(1)} %constant_dynamic-update-slice_fusion.refs_6_), channel_id=1, source_target_pairs={{0,6},{1,7},{2,4},{3,5},{4,2},{5,3},{6,0},{7,1},{8,14},{9,15},{10,... | collective-permute-start | bytes 344072 | tf_op jit(solution)/shard_map/ppermute | solution.py:156
  14.1 0.0 collective-permute-done.4
  14.1 0.4 %collective-permute-start.11 = (bf16[64,896]{1,0:T(8,128)(2,1)S(1)}, bf16[64,896]{1,0:T(8,128)(2,1)S(1)}, u32[]{:S(2)}, u32[]{:S(2)}) collective-permute-start(bf16[64,896]{1,0:T(8,128)(2,1)S(1)} %constant_dynamic-update-slice_fusion.refs_6_), channel_id=1, source_target_pairs={{0,4},{1,5},{2,6},{3,7},{4,0},{5,1},{6,2},{7,3},{8,12},{9,13},{10,... | collective-permute-start | bytes 344072 | tf_op jit(solution)/shard_map/ppermute | solution.py:156
  14.6 0.0 collective-permute-done
  14.6 1.2 %collective-permute-start.8 = (bf16[96,896]{1,0:T(8,128)(2,1)S(1)}, bf16[96,896]{1,0:T(8,128)(2,1)S(1)}, u32[]{:S(2)}, u32[]{:S(2)}) collective-permute-start(bf16[96,896]{1,0:T(8,128)(2,1)S(1)} %pad_maximum_fusion.1), channel_id=1, source_target_pairs={{0,8},{1,9},{2,10},{3,11},{4,12},{5,13},{6,14},{7,15},{8,0},{9,1},... | collective-permute-start | bytes 516104 | tf_op jit(solution)/shard_map/ppermute | solution.py:156
  15.9 0.0 collective-permute-done.6.refs_2_
  15.9 0.0 collective-permute-start.7
  15.9 1.2 %collective-permute-done.7.refs_3_ = bf16[32,896]{1,0:T(8,128)(2,1)S(1)} collective-permute-done((bf16[32,896]{1,0:T(8,128)(2,1)S(1)}, bf16[32,896]{1,0:T(8,128)(2,1)S(1)}, u32[]{:S(2)}, u32[]{:S(2)}) %collective-permute-start.7) | collective-permute-done | bytes 57376 | tf_op jit(solution)/shard_map/ppermute | solution.py:156
  17.1 0.2 collective-permute-start.10
  17.3 0.0 collective-permute-done.15.refs_12_
  17.3 0.4 %collective-permute-start.5 = (bf16[128,896]{1,0:T(8,128)(2,1)S(1)}, bf16[128,896]{1,0:T(8,128)(2,1)S(1)}, u32[]{:S(2)}, u32[]{:S(2)}) collective-permute-start(bf16[128,896]{1,0:T(8,128)(2,1)S(1)} %pad_maximum_fusion.refs_0_), channel_id=1, source_target_pairs={{0,1},{1,0},{2,3},{3,2},{4,5},{5,4},{6,7},{7,6},{8,9},{9,8},{10,11... | collective-permute-start | bytes 688136 | tf_op jit(solution)/shard_map/ppermute | solution.py:156
  17.6 2.5 %collective-permute-done.8.refs_4_ = bf16[96,896]{1,0:T(8,128)(2,1)S(1)} collective-permute-done((bf16[96,896]{1,0:T(8,128)(2,1)S(1)}, bf16[96,896]{1,0:T(8,128)(2,1)S(1)}, u32[]{:S(2)}, u32[]{:S(2)}) %collective-permute-start.8) | collective-permute-done | bytes 172064 | tf_op jit(solution)/shard_map/ppermute | solution.py:156
  20.1 0.0 collective-permute-start.9
  20.1 0.0 collective-permute-done.13.refs_10_
  20.1 0.5 %collective-permute-start.16 = (bf16[64,896]{1,0:T(8,128)(2,1)S(1)}, bf16[64,896]{1,0:T(8,128)(2,1)S(1)}, u32[]{:S(2)}, u32[]{:S(2)}) collective-permute-start(bf16[64,896]{1,0:T(8,128)(2,1)S(1)} %collective-permute-done.15.refs_12_), channel_id=1, source_target_pairs={{0,1},{1,0},{2,3},{3,2},{4,5},{5,4},{6,7},{7,6},{8,9},{9,8},{10,11... | collective-permute-start | bytes 344072 | tf_op jit(solution)/shard_map/ppermute | solution.py:156
  20.6 0.0 collective-permute-done.11.refs_8_
  20.6 0.1 collective-permute-start.14
  20.7 0.0 collective-permute-done.10.refs_7_
  20.7 0.4 %collective-permute-start.12 = (bf16[64,896]{1,0:T(8,128)(2,1)S(1)}, bf16[64,896]{1,0:T(8,128)(2,1)S(1)}, u32[]{:S(2)}, u32[]{:S(2)}) collective-permute-start(bf16[64,896]{1,0:T(8,128)(2,1)S(1)} %collective-permute-done.11.refs_8_), channel_id=1, source_target_pairs={{0,1},{1,0},{2,3},{3,2},{4,5},{5,4},{6,7},{7,6},{8,9},{9,8},{10,11... | collective-permute-start | bytes 344072 | tf_op jit(solution)/shard_map/ppermute | solution.py:156
  21.1 0.5 %collective-permute-done.16.refs_13_ = bf16[64,896]{1,0:T(8,128)(2,1)S(1)} collective-permute-done((bf16[64,896]{1,0:T(8,128)(2,1)S(1)}, bf16[64,896]{1,0:T(8,128)(2,1)S(1)}, u32[]{:S(2)}, u32[]{:S(2)}) %collective-permute-start.16) | collective-permute-done | bytes 114720 | tf_op jit(solution)/shard_map/ppermute | solution.py:156
  21.7 0.3 collective-permute-done.14.refs_11_
  21.9 0.2 collective-permute-done.12.refs_9_
  22.1 0.0 collective-permute-done.5.refs_1_
  22.1 0.0 collective-permute-done.9.refs_5_
  22.1 9.4 %shard_map.29 = f32[32,64]{1,0:T(8,128)} custom-call(bf16[128,896]{1,0:T(8,128)(2,1)S(1)} %pad_maximum_fusion.refs_0_, bf16[128,896]{1,0:T(8,128)(2,1)S(1)} %collective-permute-done.5.refs_1_, bf16[32,896]{1,0:T(8,128)(2,1)S(1)} %collective-permute-done.6.refs_2_, bf16[32,896]{1,0:T(8,128)(2,1)S(1)} %collective-permute-done.7.refs_3_, ...), custom_call_target="tpu_custom_call" | custom-call | tf_op jit(solution)/shard_map/pallas_call | solution.py:190
  (4 shorter events, 0.1 us)
Async XLA Ops:
  0.9 8.8 %collective-permute-start.3 = (bf16[32,896]{1,0:T(8,128)(2,1)S(1)}, bf16[32,896]{1,0:T(8,128)(2,1)S(1)}, u32[]{:S(2)}, u32[]{:S(2)}) collective-permute-start(bf16[32,896]{1,0:T(8,128)(2,1)S(1)} %shard_map.28), channel_id=1, source_target_pairs={{0,24},{1,25},{2,26},{3,27},{4,28},{5,29},{6,30},{7,31},{8,16},{9,... | collective-permute-start | bytes 172040 | tf_op jit(solution)/shard_map/ppermute | solution.py:156
  5.9 5.1 %collective-permute-start.2 = (bf16[32,896]{1,0:T(8,128)(2,1)S(1)}, bf16[32,896]{1,0:T(8,128)(2,1)S(1)}, u32[]{:S(2)}, u32[]{:S(2)}) collective-permute-start(bf16[32,896]{1,0:T(8,128)(2,1)S(1)} %shard_map.28), channel_id=1, source_target_pairs={{0,16},{1,17},{2,18},{3,19},{4,20},{5,21},{6,22},{7,23},{8,24},{9,... | collective-permute-start | bytes 172040 | tf_op jit(solution)/shard_map/ppermute | solution.py:156
  5.9 5.1 %collective-permute-start.1 = (bf16[32,896]{1,0:T(8,128)(2,1)S(1)}, bf16[32,896]{1,0:T(8,128)(2,1)S(1)}, u32[]{:S(2)}, u32[]{:S(2)}) collective-permute-start(bf16[32,896]{1,0:T(8,128)(2,1)S(1)} %shard_map.28), channel_id=1, source_target_pairs={{0,4},{1,5},{2,6},{3,7},{4,0},{5,1},{6,2},{7,3},{8,12},{9,13},{10,... | collective-permute-start | bytes 172040 | tf_op jit(solution)/shard_map/ppermute | solution.py:156
  7.5 8.4 %collective-permute-start.6 = (bf16[32,896]{1,0:T(8,128)(2,1)S(1)}, bf16[32,896]{1,0:T(8,128)(2,1)S(1)}, u32[]{:S(2)}, u32[]{:S(2)}) collective-permute-start(bf16[32,896]{1,0:T(8,128)(2,1)S(1)} %shard_map.28), channel_id=1, source_target_pairs={{0,8},{1,9},{2,10},{3,11},{4,12},{5,13},{6,14},{7,15},{8,0},{9,1},... | collective-permute-start | bytes 172040 | tf_op jit(solution)/shard_map/ppermute | solution.py:156
  8.2 5.9 %collective-permute-start.4 = (bf16[32,896]{1,0:T(8,128)(2,1)S(1)}, bf16[32,896]{1,0:T(8,128)(2,1)S(1)}, u32[]{:S(2)}, u32[]{:S(2)}) collective-permute-start(bf16[32,896]{1,0:T(8,128)(2,1)S(1)} %shard_map.28), channel_id=1, source_target_pairs={{0,6},{1,7},{2,4},{3,5},{4,2},{5,3},{6,0},{7,1},{8,14},{9,15},{10,... | collective-permute-start | bytes 172040 | tf_op jit(solution)/shard_map/ppermute | solution.py:156
  9.7 4.9 %collective-permute-start = (bf16[32,896]{1,0:T(8,128)(2,1)S(1)}, bf16[32,896]{1,0:T(8,128)(2,1)S(1)}, u32[]{:S(2)}, u32[]{:S(2)}) collective-permute-start(bf16[32,896]{1,0:T(8,128)(2,1)S(1)} %shard_map.28), channel_id=1, source_target_pairs={{0,2},{1,3},{2,0},{3,1},{4,6},{5,7},{6,4},{7,5},{8,10},{9,11},{10,... | collective-permute-start | bytes 172040 | tf_op jit(solution)/shard_map/ppermute | solution.py:156
  11.0 6.2 %collective-permute-start.15 = (bf16[64,896]{1,0:T(8,128)(2,1)S(1)}, bf16[64,896]{1,0:T(8,128)(2,1)S(1)}, u32[]{:S(2)}, u32[]{:S(2)}) collective-permute-start(bf16[64,896]{1,0:T(8,128)(2,1)S(1)} %constant_dynamic-update-slice_fusion.refs_6_), channel_id=1, source_target_pairs={{0,2},{1,3},{2,0},{3,1},{4,6},{5,7},{6,4},{7,5},{8,10},{9,11},{10,... | collective-permute-start | bytes 344072 | tf_op jit(solution)/shard_map/ppermute | solution.py:156
  12.6 7.5 %collective-permute-start.13 = (bf16[64,896]{1,0:T(8,128)(2,1)S(1)}, bf16[64,896]{1,0:T(8,128)(2,1)S(1)}, u32[]{:S(2)}, u32[]{:S(2)}) collective-permute-start(bf16[64,896]{1,0:T(8,128)(2,1)S(1)} %constant_dynamic-update-slice_fusion.refs_6_), channel_id=1, source_target_pairs={{0,6},{1,7},{2,4},{3,5},{4,2},{5,3},{6,0},{7,1},{8,14},{9,15},{10,... | collective-permute-start | bytes 344072 | tf_op jit(solution)/shard_map/ppermute | solution.py:156
  14.1 6.5 %collective-permute-start.11 = (bf16[64,896]{1,0:T(8,128)(2,1)S(1)}, bf16[64,896]{1,0:T(8,128)(2,1)S(1)}, u32[]{:S(2)}, u32[]{:S(2)}) collective-permute-start(bf16[64,896]{1,0:T(8,128)(2,1)S(1)} %constant_dynamic-update-slice_fusion.refs_6_), channel_id=1, source_target_pairs={{0,4},{1,5},{2,6},{3,7},{4,0},{5,1},{6,2},{7,3},{8,12},{9,13},{10,... | collective-permute-start | bytes 344072 | tf_op jit(solution)/shard_map/ppermute | solution.py:156
  14.6 5.5 %collective-permute-start.8 = (bf16[96,896]{1,0:T(8,128)(2,1)S(1)}, bf16[96,896]{1,0:T(8,128)(2,1)S(1)}, u32[]{:S(2)}, u32[]{:S(2)}) collective-permute-start(bf16[96,896]{1,0:T(8,128)(2,1)S(1)} %pad_maximum_fusion.1), channel_id=1, source_target_pairs={{0,8},{1,9},{2,10},{3,11},{4,12},{5,13},{6,14},{7,15},{8,0},{9,1},... | collective-permute-start | bytes 516104 | tf_op jit(solution)/shard_map/ppermute | solution.py:156
  15.9 1.2 %collective-permute-start.7 = (bf16[32,896]{1,0:T(8,128)(2,1)S(1)}, bf16[32,896]{1,0:T(8,128)(2,1)S(1)}, u32[]{:S(2)}, u32[]{:S(2)}) collective-permute-start(bf16[32,896]{1,0:T(8,128)(2,1)S(1)} %collective-permute-done.6.refs_2_), channel_id=1, source_target_pairs={{0,1},{1,0},{2,3},{3,2},{4,5},{5,4},{6,7},{7,6},{8,9},{9,8},{10,11... | collective-permute-start | bytes 172040 | tf_op jit(solution)/shard_map/ppermute | solution.py:156
  17.1 3.6 %collective-permute-start.10 = (bf16[64,896]{1,0:T(8,128)(2,1)S(1)}, bf16[64,896]{1,0:T(8,128)(2,1)S(1)}, u32[]{:S(2)}, u32[]{:S(2)}) collective-permute-start(bf16[64,896]{1,0:T(8,128)(2,1)S(1)} %constant_dynamic-update-slice_fusion.refs_6_), channel_id=1, source_target_pairs={{0,1},{1,0},{2,3},{3,2},{4,5},{5,4},{6,7},{7,6},{8,9},{9,8},{10,11... | collective-permute-start | bytes 344072 | tf_op jit(solution)/shard_map/ppermute | solution.py:156
  17.3 4.8 %collective-permute-start.5 = (bf16[128,896]{1,0:T(8,128)(2,1)S(1)}, bf16[128,896]{1,0:T(8,128)(2,1)S(1)}, u32[]{:S(2)}, u32[]{:S(2)}) collective-permute-start(bf16[128,896]{1,0:T(8,128)(2,1)S(1)} %pad_maximum_fusion.refs_0_), channel_id=1, source_target_pairs={{0,1},{1,0},{2,3},{3,2},{4,5},{5,4},{6,7},{7,6},{8,9},{9,8},{10,11... | collective-permute-start | bytes 688136 | tf_op jit(solution)/shard_map/ppermute | solution.py:156
  20.1 2.0 %collective-permute-start.9 = (bf16[96,896]{1,0:T(8,128)(2,1)S(1)}, bf16[96,896]{1,0:T(8,128)(2,1)S(1)}, u32[]{:S(2)}, u32[]{:S(2)}) collective-permute-start(bf16[96,896]{1,0:T(8,128)(2,1)S(1)} %collective-permute-done.8.refs_4_), channel_id=1, source_target_pairs={{0,1},{1,0},{2,3},{3,2},{4,5},{5,4},{6,7},{7,6},{8,9},{9,8},{10,11... | collective-permute-start | bytes 516104 | tf_op jit(solution)/shard_map/ppermute | solution.py:156
  20.1 1.6 %collective-permute-start.16 = (bf16[64,896]{1,0:T(8,128)(2,1)S(1)}, bf16[64,896]{1,0:T(8,128)(2,1)S(1)}, u32[]{:S(2)}, u32[]{:S(2)}) collective-permute-start(bf16[64,896]{1,0:T(8,128)(2,1)S(1)} %collective-permute-done.15.refs_12_), channel_id=1, source_target_pairs={{0,1},{1,0},{2,3},{3,2},{4,5},{5,4},{6,7},{7,6},{8,9},{9,8},{10,11... | collective-permute-start | bytes 344072 | tf_op jit(solution)/shard_map/ppermute | solution.py:156
  20.6 1.3 %collective-permute-start.14 = (bf16[64,896]{1,0:T(8,128)(2,1)S(1)}, bf16[64,896]{1,0:T(8,128)(2,1)S(1)}, u32[]{:S(2)}, u32[]{:S(2)}) collective-permute-start(bf16[64,896]{1,0:T(8,128)(2,1)S(1)} %collective-permute-done.13.refs_10_), channel_id=1, source_target_pairs={{0,1},{1,0},{2,3},{3,2},{4,5},{5,4},{6,7},{7,6},{8,9},{9,8},{10,11... | collective-permute-start | bytes 344072 | tf_op jit(solution)/shard_map/ppermute | solution.py:156
  20.7 1.4 %collective-permute-start.12 = (bf16[64,896]{1,0:T(8,128)(2,1)S(1)}, bf16[64,896]{1,0:T(8,128)(2,1)S(1)}, u32[]{:S(2)}, u32[]{:S(2)}) collective-permute-start(bf16[64,896]{1,0:T(8,128)(2,1)S(1)} %collective-permute-done.11.refs_8_), channel_id=1, source_target_pairs={{0,1},{1,0},{2,3},{3,2},{4,5},{5,4},{6,7},{7,6},{8,9},{9,8},{10,11... | collective-permute-start | bytes 344072 | tf_op jit(solution)/shard_map/ppermute | solution.py:156
